TPU v7x, 32 devices: a whole 2x2x4 slice. The times are simulated.
32 devices in a mesh: groups: 2 (over y), seq: 4 (over z), head: 2 (over x), rep: 2 (over core).
Axes of the slice: x: 2, y: 2, z: 4, core: 2. Of those that a mesh axis runs over, the one named last changes fastest.
Arguments:
- queries: bfloat16 [8192, 8, 128], P(('groups', 'seq', 'rep'), 'head'), parts along dimension 0, may hold values from -1.796875 to 1.796875
- keys: bfloat16 [8192, 8, 128], P(('groups', 'seq', 'rep'), 'head'), parts along dimension 0, may hold values from -1.796875 to 1.796875
- values: bfloat16 [8192, 8, 128], P(('groups', 'seq', 'rep'), 'head'), parts along dimension 0, may hold values from -6 to 6
- out_grad: bfloat16 [8192, 8, 128], P(('groups', 'seq', 'rep'), 'head'), parts along dimension 0, may hold values from -1.796875 to 1.796875
- level_table: float32 [7, 8], P(None, 'head'), may hold values from 0.25 to 2
Outputs:
- attended: bfloat16 [8192, 8, 128], P(('groups', 'seq', 'rep'), 'head'), parts along dimension 0
- query_grad: bfloat16 [8192, 8, 128], P(('groups', 'seq', 'rep'), 'head'), parts along dimension 0
- key_grad: bfloat16 [8192, 8, 128], P(('groups', 'seq', 'rep'), 'head'), parts along dimension 0
- value_grad: bfloat16 [8192, 8, 128], P(('groups', 'seq', 'rep'), 'head'), parts along dimension 0
There are 2 independent parts, one for each index of `groups`. A program takes and returns all parts, laid end to end along the dimension named above; an argument that names none is the same for every part. Nothing has to cross between parts.
All inputs are finite; a program needn't handle non-finite values.
Results may differ from a plain program's by a relative error of at most 0.001.
Values sent between devices are 32-bit elements; how exact they have to be, the bound alone decides.
No kernel may reach another device: no remote copies, remote signals or barrier semaphores. Data moves between devices by JAX's collectives and lax.ppermute only.
A program may use at most 64 MiB of HBM per device.

v0:
```python
import jax
import jax.numpy as jnp
from jax import lax
from jax.sharding import PartitionSpec as P

BLOCK = 64


def partner_2(block, axis, apart):
    count = lax.axis_size(axis)
    route = []
    for low in range(count):
        high = low | 1 << apart
        if high != low and high < count:
            route += [(low, high), (high, low)]
    return lax.ppermute(block, axis, route)


def product(form, left, right):
    return jnp.einsum(form, left, right, precision=lax.Precision.HIGHEST)


def bit_length(numbers, top):
    total = jnp.zeros(numbers.shape, jnp.int32)
    for shift in range(top):
        total = total + (jnp.right_shift(numbers, shift) > 0).astype(jnp.int32)
    return total


def scaled_weights(level_table):
    count = level_table.shape[0]
    power = jnp.maximum(jnp.arange(count, dtype=jnp.int32) - 1, 0).astype(jnp.float32)
    scale = 1.0 / jnp.sqrt(jnp.float32(BLOCK) * jnp.exp2(power))
    return level_table * scale[:, None]


def level_weights(level_index, weights):
    onehot = (level_index[..., None] == jnp.arange(weights.shape[0], dtype=jnp.int32)).astype(
        jnp.float32
    )
    return product("...l,lh->...h", onehot, weights)


def per_device(queries, keys, values, out_grad, level_table):
    rows, heads, width = queries.shape
    levels = level_table.shape[0]
    blocks_here = rows // BLOCK
    local_levels = blocks_here.bit_length() - 1
    devices = lax.axis_size(("seq", "rep"))
    position = lax.axis_index(("seq", "rep"))
    weights = scaled_weights(level_table)
    shape4 = (blocks_here, BLOCK, heads, width)
    qb = queries.astype(jnp.float32).reshape(shape4)
    kb = keys.astype(jnp.float32).reshape(shape4)
    vb = values.astype(jnp.float32).reshape(shape4)
    gb = out_grad.astype(jnp.float32).reshape(shape4)
    order = jnp.arange(BLOCK, dtype=jnp.int32)
    causal = (order[:, None] >= order[None, :]).astype(jnp.float32)
    masking = weights[0][None, :, None, None] * causal[None, None, :, :]
    scores = product("nchd,nshd->nhcs", qb, kb) * masking
    grads = product("nchd,nshd->nhcs", gb, vb) * masking
    key_state = product("nchd,nche->nhde", kb, vb)
    query_state = product("nchd,nche->nhde", qb, gb)
    blocks = jnp.arange(blocks_here, dtype=jnp.int32)
    earlier = (blocks[None, :] < blocks[:, None]).astype(jnp.float32)
    local_coef = (
        level_weights(
            bit_length(jnp.bitwise_xor(blocks[:, None], blocks[None, :]), levels), weights
        )
        * earlier[:, :, None]
    )
    read_state = product("nmh,mhde->nhde", local_coef, key_state)
    back_state = product("nmh,nhde->mhde", local_coef, query_state)
    own_keys = jnp.sum(key_state, axis=0)
    own_queries = jnp.sum(query_state, axis=0)
    blank = jnp.zeros((heads, width, width), jnp.float32)
    group = jnp.stack([own_keys, own_queries])
    far_keys = blank
    far_queries = blank
    for bit_index in range(devices.bit_length() - 1):
        partner = partner_2(group, ("seq", "rep"), bit_index)
        upper = (jnp.right_shift(position, bit_index) % 2).astype(jnp.float32)
        level_row = weights[local_levels + 1 + bit_index][:, None, None]
        far_keys = far_keys + upper * level_row * partner[0]
        far_queries = far_queries + (1.0 - upper) * level_row * partner[1]
        group = group + partner
    total_read = read_state + far_keys[None]
    total_back = back_state + far_queries[None]
    attended = product("nhcs,nshe->nche", scores, vb) + product("nchd,nhde->nche", qb, total_read)
    query_grad = product("nhcs,nshd->nchd", grads, kb) + product("nche,nhde->nchd", gb, total_read)
    key_grad = product("nhcs,nchd->nshd", grads, qb) + product("nche,nhde->nchd", vb, total_back)
    value_grad = product("nhcs,nche->nshe", scores, gb) + product("nchd,nhde->nche", kb, total_back)
    flat = (rows, heads, width)
    return (
        attended.reshape(flat).astype(jnp.bfloat16),
        query_grad.reshape(flat).astype(jnp.bfloat16),
        key_grad.reshape(flat).astype(jnp.bfloat16),
        value_grad.reshape(flat).astype(jnp.bfloat16),
    )


def solution(mesh):
    return jax.shard_map(
        per_device,
        mesh=mesh,
        in_specs=(
            P(("groups", "seq", "rep"), "head", None),
            P(("groups", "seq", "rep"), "head", None),
            P(("groups", "seq", "rep"), "head", None),
            P(("groups", "seq", "rep"), "head", None),
            P(None, "head"),
        ),
        out_specs=(
            P(("groups", "seq", "rep"), "head", None),
            P(("groups", "seq", "rep"), "head", None),
            P(("groups", "seq", "rep"), "head", None),
            P(("groups", "seq", "rep"), "head", None),
        ),
        check_vma=False,
    )
```

profile of v0, /device:TPU:0, one launch (start us, length us, event | category | flops | bytes accessed | tf_op | source)
XLA Modules:
  0.0 73.2 jit_solution(1686333156762153502)
XLA Ops:
  0.6 0.0 copy-start
  0.6 0.0 copy-start.2
  0.7 3.1 %fusion.62 = (f32[4,128,128]{2,1,0:T(8,128)S(1)}, f32[8,4,128,128]{3,2,1,0:T(8,128)}) fusion(bf16[8,64,4,128]{3,2,1,0:T(4,128)(2,1)} %bitcast.74, bf16[8,64,4,128]{3,2,1,0:T(4,128)(2,1)} %bitcast.70), kind=kOutput, calls=%fused_computation.92 | convolution fusion | flops 67567616 | bytes 3407872 | tf_op jit(solution)/shard_map/nchd,nche->nhde/dot_general | solution.py:20
  3.8 0.0 copy-done
  3.8 0.0 copy-done.2
  3.8 0.0 copy-start.7
  3.8 0.5 fusion.63
  4.3 0.0 copy-start.5
  4.3 0.7 copy-done.5
  5.0 0.8 %pad_maximum_fusion = f32[2,4,128,128]{3,2,1,0:T(8,128)} fusion(f32[1,4,128,128]{3,2,1,0:T(8,128)S(1)} %bitcast.78, f32[1,4,128,128]{3,2,1,0:T(8,128)S(1)} %bitcast.81), kind=kLoop, calls=%fused_computation.34 | loop fusion | flops 131072 | bytes 1048576 | tf_op jit(solution)/shard_map/stack | solution.py:77
  5.8 0.5 collective-permute-start
  6.4 0.0 copy-done.7
  6.4 0.4 fusion.32
  6.8 1.4 %collective-permute-done = f32[2,4,128,128]{3,2,1,0:T(8,128)} collective-permute-done((f32[2,4,128,128]{3,2,1,0:T(8,128)}, f32[2,4,128,128]{3,2,1,0:T(8,128)}, u32[]{:S(2)}, u32[]{:S(2)}) %collective-permute-start) | collective-permute-done | bytes 524320 | tf_op jit(solution)/shard_map/ppermute | solution.py:16
  8.2 2.0 %fusion.61 = f32[2,4,128,128]{3,2,1,0:T(8,128)} fusion(f32[2,4,128,128]{3,2,1,0:T(8,128)} %collective-permute-done, f32[1,4,128,128]{3,2,1,0:T(8,128)S(1)} %bitcast.79, f32[1,4,128,128]{3,2,1,0:T(8,128)} %bitcast.82), kind=kLoop, calls=%fused_computation.91 | loop fusion | flops 262144 | bytes 1572864 | tf_op jit(solution)/shard_map/add | solution.py:86
  10.1 2.9 %collective-permute-start.1 = (f32[2,4,128,128]{3,2,1,0:T(8,128)}, f32[2,4,128,128]{3,2,1,0:T(8,128)}, u32[]{:S(2)}, u32[]{:S(2)}) collective-permute-start(f32[2,4,128,128]{3,2,1,0:T(8,128)} %fusion.61), channel_id=1, source_target_pairs={{0,4},{4,0},{1,5},{5,1},{8,12},{12,8},{9,13},{13,9},{2,6},{6,2},{3... | collective-permute-start | bytes 1572872 | tf_op jit(solution)/shard_map/ppermute | solution.py:16
  13.1 0.3 multiply_reduce_fusion.2
  13.4 0.1 copy.71
  13.4 0.0 copy-start.6
  13.4 0.1 broadcast_multiply_fusion
  13.5 0.0 copy-start.4
  13.5 1.5 %convolution_multiply_fusion.1 = f32[8,4,64,64]{3,2,1,0:T(8,128)S(1)} fusion(f32[4,64,64]{2,1,0:T(8,128)S(1)} %broadcast_multiply_fusion, bf16[8,64,4,128]{3,2,1,0:T(4,128)(2,1)S(1)} %bitcast.67, bf16[8,64,4,128]{3,2,1,0:T(4,128)(2,1)} %bitcast.71), kind=kOutput, calls=%fused_computation.19 | convolution fusion | flops 33685504 | bytes 1638400 | tf_op jit(solution)/shard_map/nchd,nshd->nhcs/dot_general | solution.py:20
  15.0 0.0 copy-start.1
  15.1 10.6 %collective-permute-done.1 = f32[2,4,128,128]{3,2,1,0:T(8,128)} collective-permute-done((f32[2,4,128,128]{3,2,1,0:T(8,128)}, f32[2,4,128,128]{3,2,1,0:T(8,128)}, u32[]{:S(2)}, u32[]{:S(2)}) %collective-permute-start.1) | collective-permute-done | bytes 524320 | tf_op jit(solution)/shard_map/ppermute | solution.py:16
  25.6 0.0 copy-done.6
  25.6 1.3 %fusion.72 = f32[2,4,128,128]{3,2,1,0:T(8,128)S(1)} fusion(f32[2,4,128,128]{3,2,1,0:T(8,128)} %collective-permute-done.1, f32[2,4,128,128]{3,2,1,0:T(8,128)} %collective-permute-done, f32[1,4,128,128]{3,2,1,0:T(8,128)S(1)} %bitcast.80, f32[1,4,128,128]{3,2,1,0:T(8,128)S(1)} %bitcast.83), kind=kLoop, calls=%fused_computation.94 | loop fusion | flops 393216 | bytes 2097152 | tf_op jit(solution)/shard_map/add | solution.py:86
  26.9 2.8 %collective-permute-start.2 = (f32[2,4,128,128]{3,2,1,0:T(8,128)S(1)}, f32[2,4,128,128]{3,2,1,0:T(8,128)S(1)}, u32[]{:S(2)}, u32[]{:S(2)}) collective-permute-start(f32[2,4,128,128]{3,2,1,0:T(8,128)S(1)} %fusion.72), channel_id=1, source_target_pairs={{0,8},{8,0},{1,9},{9,1},{4,12},{12,4},{5,13},{13,5},{2,10},{10,2},... | collective-permute-start | bytes 1572872 | tf_op jit(solution)/shard_map/ppermute | solution.py:16
  29.7 0.0 copy-done.4
  29.7 0.4 convolution_multiply_fusion
  30.1 0.0 copy-done.1
  30.1 3.1 %fusion = f32[4,128,128,8]{2,3,1,0:T(8,128)S(1)} fusion(f32[8,8,4,1]{0,1,3,2:T(8,128)S(1)} %copy.71, f32[8,4,128,128]{3,2,1,0:T(8,128)S(1)} %copy-done.1), kind=kOutput, calls=%fused_computation | convolution fusion | flops 50331648 | bytes 4195328 | tf_op jit(solution)/shard_map/nmh,nhde->mhde/dot_general | solution.py:20
  33.2 19.3 %collective-permute-done.2 = f32[2,4,128,128]{3,2,1,0:T(8,128)S(1)} collective-permute-done((f32[2,4,128,128]{3,2,1,0:T(8,128)S(1)}, f32[2,4,128,128]{3,2,1,0:T(8,128)S(1)}, u32[]{:S(2)}, u32[]{:S(2)}) %collective-permute-start.2) | collective-permute-done | bytes 524320 | tf_op jit(solution)/shard_map/ppermute | solution.py:16
  52.6 1.4 %fusion.52 = (f32[4,128,128]{2,1,0:T(8,128)S(1)}, f32[4,128,128]{2,1,0:T(8,128)S(1)}) fusion(f32[2,4,128,128]{3,2,1,0:T(8,128)S(1)} %collective-permute-done.2, f32[2,4,128,128]{3,2,1,0:T(8,128)} %collective-permute-done.1, f32[2,4,128,128]{3,2,1,0:T(8,128)} %collective-permute-done, f32[4]{0:T(128)S(1)} %get-tuple-element.10, f32[4]{0:T(128)S(1)} %get-tuple-element.9, ...), kind=kLoop, calls=%fused_computation.55 | loop fusion | flops 655360 | bytes 2097248 | tf_op jit(solution)/shard_map/add | solution.py:88
  53.9 0.0 copy-start.3
  53.9 3.4 %add_bitcast_fusion = (f32[8,4,128,128]{3,0,2,1:T(8,128)S(1)}, f32[8,4,128,128]{3,0,2,1:T(8,128)S(1)}) fusion(f32[4,128,128,8]{2,3,1,0:T(8,128)S(1)} %fusion, f32[4,128,128]{2,1,0:T(8,128)S(1)} %get-tuple-element.15, f32[4,128,128]{2,1,0:T(8,128)S(1)} %get-tuple-element.16, f32[8,8,4,1]{0,1,3,2:T(8,128)S(1)} %copy.71, ...), kind=kOutput, calls=%fused_computation.4 | convolution fusion | flops 51380224 | bytes 8913920 | tf_op jit(solution)/shard_map/nmh,mhde->nhde/dot_general | solution.py:20
  57.3 0.0 copy-done.3
  57.3 1.4 %fusion.12 = f32[8,64,4,128]{3,1,2,0:T(8,128)S(1)} fusion(f32[8,4,128,128]{3,0,2,1:T(8,128)S(1)} %get-tuple-element.22, bf16[8,64,4,128]{3,2,1,0:T(4,128)(2,1)S(1)} %bitcast.72), kind=kOutput, calls=%fused_computation.14 | convolution fusion | flops 402653184 | bytes 3670016 | tf_op jit(solution)/shard_map/nchd,nhde->nche/dot_general | solution.py:20
  58.7 2.4 %fusion.15 = f32[8,64,4,128]{3,1,2,0:T(8,128)S(1)} fusion(f32[8,4,128,128]{3,0,2,1:T(8,128)S(1)} %get-tuple-element.22, bf16[8,64,4,128]{3,2,1,0:T(4,128)(2,1)S(1)} %bitcast.76), kind=kOutput, calls=%fused_computation.15 | convolution fusion | flops 402653184 | bytes 3670016 | tf_op jit(solution)/shard_map/nche,nhde->nchd/dot_general | solution.py:20
  61.1 2.3 %fusion.18 = f32[8,64,4,128]{3,1,2,0:T(8,128)S(1)} fusion(f32[8,4,128,128]{3,0,2,1:T(8,128)S(1)} %get-tuple-element.21, bf16[8,64,4,128]{3,2,1,0:T(4,128)(2,1)S(1)} %bitcast.63), kind=kOutput, calls=%fused_computation.16 | convolution fusion | flops 402653184 | bytes 3670016 | tf_op jit(solution)/shard_map/nche,nhde->nchd/dot_general | solution.py:20
  63.4 1.4 %fusion.21 = f32[8,64,4,128]{3,1,2,0:T(8,128)S(1)} fusion(f32[8,4,128,128]{3,0,2,1:T(8,128)S(1)} %get-tuple-element.21, bf16[8,64,4,128]{3,2,1,0:T(4,128)(2,1)S(1)} %bitcast.68), kind=kOutput, calls=%fused_computation.17 | convolution fusion | flops 402653184 | bytes 3670016 | tf_op jit(solution)/shard_map/nchd,nhde->nche/dot_general | solution.py:20
  64.8 0.7 fusion.28
  65.5 1.2 %copy.65 = bf16[512,4,128]{2,1,0:T(4,128)(2,1)} copy(bf16[512,4,128]{2,0,1:T(8,128)(2,1)S(1)} %bitcast.84) | data formatting | bytes 1048576
  66.7 0.7 fusion.29
  67.5 1.2 %copy.66 = bf16[512,4,128]{2,1,0:T(4,128)(2,1)} copy(bf16[512,4,128]{2,0,1:T(8,128)(2,1)S(1)} %bitcast.85) | data formatting | bytes 1048576
  68.7 1.0 %fusion.30 = bf16[8,64,4,128]{3,1,2,0:T(8,128)(2,1)S(1)} fusion(f32[8,64,4,128]{3,1,2,0:T(8,128)S(1)} %fusion.18, f32[8,4,64,64]{3,2,1,0:T(8,128)S(1)} %convolution_multiply_fusion, bf16[8,64,4,128]{3,2,1,0:T(4,128)(2,1)S(1)} %bitcast.73), kind=kOutput, calls=%fused_computation.30 | convolution fusion | flops 201850880 | bytes 2621440 | tf_op jit(solution)/shard_map/nhcs,nchd->nshd/dot_general | solution.py:20
  69.8 1.2 %copy.67 = bf16[512,4,128]{2,1,0:T(4,128)(2,1)} copy(bf16[512,4,128]{2,0,1:T(8,128)(2,1)S(1)} %bitcast.86) | data formatting | bytes 1048576
  71.0 1.0 %fusion.31 = bf16[8,64,4,128]{3,1,2,0:T(8,128)(2,1)S(1)} fusion(f32[8,64,4,128]{3,1,2,0:T(8,128)S(1)} %fusion.21, f32[8,4,64,64]{3,2,1,0:T(8,128)S(1)} %convolution_multiply_fusion.1, bf16[8,64,4,128]{3,2,1,0:T(4,128)(2,1)S(1)} %bitcast.77), kind=kOutput, calls=%fused_computation.31 | convolution fusion | flops 201850880 | bytes 2621440 | tf_op jit(solution)/shard_map/nhcs,nche->nshe/dot_general | solution.py:20
  72.0 1.2 %copy.68 = bf16[512,4,128]{2,1,0:T(4,128)(2,1)} copy(bf16[512,4,128]{2,0,1:T(8,128)(2,1)S(1)} %bitcast.87) | data formatting | bytes 1048576
  (9 shorter events, 0.2 us)
Async XLA Ops:
  0.6 3.2 %copy-start = (bf16[512,4,128]{2,1,0:T(4,128)(2,1)S(1)}, bf16[512,4,128]{2,1,0:T(4,128)(2,1)}, u32[]{:S(2)}) copy-start(bf16[512,4,128]{2,1,0:T(4,128)(2,1)} %param.7) | copy-start | bytes 1572868
  0.6 3.2 %copy-start.2 = (bf16[512,4,128]{2,1,0:T(4,128)(2,1)S(1)}, bf16[512,4,128]{2,1,0:T(4,128)(2,1)}, u32[]{:S(2)}) copy-start(bf16[512,4,128]{2,1,0:T(4,128)(2,1)} %param.6) | copy-start | bytes 1572868
  3.8 2.6 %copy-start.7 = (f32[7,4]{0,1:T(4,128)S(1)}, f32[7,4]{0,1:T(4,128)}, u32[]{:S(2)}) copy-start(f32[7,4]{0,1:T(4,128)} %param.9) | copy-start | bytes 340
  4.3 0.7 copy-start.5
  5.8 2.3 %collective-permute-start = (f32[2,4,128,128]{3,2,1,0:T(8,128)}, f32[2,4,128,128]{3,2,1,0:T(8,128)}, u32[]{:S(2)}, u32[]{:S(2)}) collective-permute-start(f32[2,4,128,128]{3,2,1,0:T(8,128)} %pad_maximum_fusion), channel_id=1, source_target_pairs={{0,1},{1,0},{4,5},{5,4},{8,9},{9,8},{12,13},{13,12},{2,3},{3,2},{6... | collective-permute-start | bytes 1572872 | tf_op jit(solution)/shard_map/ppermute | solution.py:16
  10.1 15.5 %collective-permute-start.1 = (f32[2,4,128,128]{3,2,1,0:T(8,128)}, f32[2,4,128,128]{3,2,1,0:T(8,128)}, u32[]{:S(2)}, u32[]{:S(2)}) collective-permute-start(f32[2,4,128,128]{3,2,1,0:T(8,128)} %fusion.61), channel_id=1, source_target_pairs={{0,4},{4,0},{1,5},{5,1},{8,12},{12,8},{9,13},{13,9},{2,6},{6,2},{3... | collective-permute-start | bytes 1572872 | tf_op jit(solution)/shard_map/ppermute | solution.py:16
  13.4 12.2 %copy-start.6 = (f32[4,128,128]{2,1,0:T(8,128)S(1)}, f32[4,128,128]{2,1,0:T(8,128)}, u32[]{:S(2)}) copy-start(f32[4,128,128]{2,1,0:T(8,128)} %copy-done.5) | copy-start | bytes 786436
  13.5 16.2 %copy-start.4 = (bf16[512,4,128]{2,1,0:T(4,128)(2,1)S(1)}, bf16[512,4,128]{2,1,0:T(4,128)(2,1)}, u32[]{:S(2)}) copy-start(bf16[512,4,128]{2,1,0:T(4,128)(2,1)} %param.8) | copy-start | bytes 1572868
  15.0 15.1 %copy-start.1 = (f32[8,4,128,128]{3,2,1,0:T(8,128)S(1)}, f32[8,4,128,128]{3,2,1,0:T(8,128)}, u32[]{:S(2)}) copy-start(f32[8,4,128,128]{3,2,1,0:T(8,128)} %get-tuple-element.18) | copy-start | bytes 6291460
  26.9 25.7 %collective-permute-start.2 = (f32[2,4,128,128]{3,2,1,0:T(8,128)S(1)}, f32[2,4,128,128]{3,2,1,0:T(8,128)S(1)}, u32[]{:S(2)}, u32[]{:S(2)}) collective-permute-start(f32[2,4,128,128]{3,2,1,0:T(8,128)S(1)} %fusion.72), channel_id=1, source_target_pairs={{0,8},{8,0},{1,9},{9,1},{4,12},{12,4},{5,13},{13,5},{2,10},{10,2},... | collective-permute-start | bytes 1572872 | tf_op jit(solution)/shard_map/ppermute | solution.py:16
  53.9 3.4 %copy-start.3 = (bf16[512,4,128]{2,1,0:T(4,128)(2,1)S(1)}, bf16[512,4,128]{2,1,0:T(4,128)(2,1)}, u32[]{:S(2)}) copy-start(bf16[512,4,128]{2,1,0:T(4,128)(2,1)} %param.5) | copy-start | bytes 1572868
where the time goes:
time: 73.5 us; the launch traced here: 73.2 us
  waiting for transfers between devices  31.2 us (42%)
  matrix products  23.3 us (32%)
  starting transfers between devices  6.22 us (8%)
  other arithmetic  5.83 us (8%)
  local copies, waits for them, and re-layouts  5.75 us (8%)
  between operations  0.91 us (1%)
    ppermute x3, waiting for transfers between devices, partner_2(): return lax.ppermute(block, axis, route)  31.2 us
    dot_general x15, matrix products, product(): return jnp.einsum(form, left, right, precision=lax.Precision.HIGHEST)  23.3 us
    ppermute x3, starting transfers between devices, partner_2(): return lax.ppermute(block, axis, route)  6.22 us
    unnamed x20, local copies, waits for them, and re-layouts  5.54 us
    add x2, other arithmetic, per_device(): group = group + partner  3.24 us
  transfers between devices with their start and end apart: 3, of which 3 were waited for; matrix products, arithmetic and copies ran while one was open for 8% of the time, Pallas kernels for 0%

commit v1 on v0

v1 whole, which is shorter than its diff:
```python
import functools
import math

import jax
import jax.numpy as jnp
import numpy as np
from jax import lax
from jax.experimental import pallas as pl
from jax.experimental.pallas import tpu as pltpu
from jax.sharding import PartitionSpec as P

BLOCK = 64
TILE = 256
F32 = jnp.float32
BF16 = jnp.bfloat16


def swap_cores(block):
    return lax.ppermute(block, "rep", [(0, 1), (1, 0)])


def swap_chips(block, mask):
    count = lax.axis_size("seq")
    return lax.ppermute(block, "seq", [(chip, chip ^ mask) for chip in range(count)])


def level_scale(level):
    return float(np.float32(1.0) / np.sqrt(np.float32(BLOCK * 2 ** max(level - 1, 0))))


def dot_tn(left, right):
    return lax.dot_general(left, right, (((0,), (0,)), ((), ())), preferred_element_type=F32)


def dot_nt(left, right):
    return lax.dot_general(left, right, (((1,), (1,)), ((), ())), preferred_element_type=F32)


def dot_nn(left, right):
    return lax.dot_general(left, right, (((1,), (0,)), ((), ())), preferred_element_type=F32)


def split(value):
    high = value.astype(BF16)
    return high, (value - high.astype(F32)).astype(BF16)


def state_kernel(heads, q_ref, k_ref, v_ref, g_ref, send_ref, keep_ref, per_head_ref, wide):
    rows = q_ref.shape[0] // heads
    half = heads // 2
    core = lax.axis_index("rep")
    for which, ref in enumerate((q_ref, k_ref, v_ref, g_ref)):
        wide[which] = ref[...].astype(F32)
    for which in range(4):
        for head in range(heads):
            per_head_ref[which, head] = wide[which, pl.ds(head, rows, stride=heads), :].astype(BF16)
    for place in range(half):
        for owner, out_ref in ((1 - core, send_ref), (core, keep_ref)):
            head = owner * half + place
            out_ref[0, place] = dot_tn(per_head_ref[1, head], per_head_ref[2, head])
            out_ref[1, place] = dot_tn(per_head_ref[0, head], per_head_ref[3, head])


def states(queries, keys, values, out_grad):
    rows, heads, width = queries.shape
    flat = [array.reshape(rows * heads, width) for array in (queries, keys, values, out_grad)]
    half = (2, heads // 2, width, width)
    return pl.pallas_call(
        functools.partial(state_kernel, heads),
        out_shape=(
            jax.ShapeDtypeStruct(half, F32),
            jax.ShapeDtypeStruct(half, F32),
            jax.ShapeDtypeStruct((4, heads, rows, width), BF16),
        ),
        in_specs=[pl.BlockSpec(memory_space=pltpu.VMEM)] * 4,
        out_specs=[pl.BlockSpec(memory_space=pltpu.VMEM)] * 3,
        scratch_shapes=[pltpu.VMEM((4, rows * heads, width), F32)],
        compiler_params=pltpu.CompilerParams(vmem_limit_bytes=24 * 2**20),
        name="states",
    )(*flat)


def local_kernel(table_ref, per_head_ref, out_ref):
    head = pl.program_id(0)
    rows = per_head_ref.shape[1]
    tiles = rows // TILE
    weight = [table_ref[level, head] * level_scale(level) for level in range((rows // BLOCK).bit_length())]
    row = lax.broadcasted_iota(jnp.int32, (TILE, TILE), 0)
    column = lax.broadcasted_iota(jnp.int32, (TILE, TILE), 1)
    apart = jnp.bitwise_xor(row // BLOCK, column // BLOCK)
    mask = jnp.where(apart == 0, weight[0], weight[1])
    for level in range(2, (TILE // BLOCK).bit_length()):
        mask = jnp.where(apart >= 1 << (level - 1), weight[level], mask)
    mask = jnp.where(row >= column, mask, 0.0)
    part = [[per_head_ref[which, pl.ds(tile * TILE, TILE), :] for tile in range(tiles)] for which in range(4)]
    queries, keys, values, out_grad = part
    results = [[None] * tiles for _ in range(4)]

    def add(which, tile, value):
        held = results[which][tile]
        results[which][tile] = value if held is None else held + value

    for later in range(tiles):
        for earlier in range(later + 1):
            scale = mask if later == earlier else weight[(TILE // BLOCK).bit_length() - 1 + (later ^ earlier).bit_length()]
            scores = split(dot_nt(queries[later], keys[earlier]) * scale)
            grads = split(dot_nt(out_grad[later], values[earlier]) * scale)
            for piece in scores:
                add(0, later, dot_nn(piece, values[earlier]))
                add(3, earlier, dot_tn(piece, out_grad[later]))
            for piece in grads:
                add(1, later, dot_nn(piece, keys[earlier]))
                add(2, earlier, dot_tn(piece, queries[later]))
    for which in range(4):
        for tile in range(tiles):
            out_ref[which, pl.ds(tile * TILE, TILE), :] = results[which][tile]


def local_part(level_table, per_head):
    _, heads, rows, width = per_head.shape
    return pl.pallas_call(
        local_kernel,
        grid=(heads,),
        out_shape=jax.ShapeDtypeStruct((4, heads, rows, width), F32),
        in_specs=[
            pl.BlockSpec(memory_space=pltpu.SMEM),
            pl.BlockSpec((4, None, rows, width), lambda head: (0, head, 0, 0)),
        ],
        out_specs=pl.BlockSpec((4, None, rows, width), lambda head: (0, head, 0, 0)),
        compiler_params=pltpu.CompilerParams(vmem_limit_bytes=24 * 2**20),
        cost_estimate=pl.CostEstimate(flops=3 * 10**9, bytes_accessed=6 * 2**20, transcendentals=0),
        name="local",
    )(level_table, per_head)


def final_kernel(per_head_ref, local_ref, far_ref, *refs):
    out_refs, wide = refs[:4], refs[4]
    heads, rows = per_head_ref.shape[1:3]
    for head in range(heads):
        keys_far = split(far_ref[0, head])
        queries_far = split(far_ref[1, head])
        q, k, v, g = (per_head_ref[which, head] for which in range(4))
        results = [local_ref[which, head] for which in range(4)]
        for piece in keys_far:
            results[0] += dot_nn(q, piece)
            results[1] += dot_nt(g, piece)
        for piece in queries_far:
            results[2] += dot_nt(v, piece)
            results[3] += dot_nn(k, piece)
        for which in range(4):
            wide[which, pl.ds(head, rows, stride=heads), :] = results[which]
    for which in range(4):
        out_refs[which][...] = wide[which].astype(BF16)


def final_part(per_head, local, far):
    _, heads, rows, width = per_head.shape
    outs = pl.pallas_call(
        final_kernel,
        out_shape=[jax.ShapeDtypeStruct((rows * heads, width), BF16)] * 4,
        in_specs=[pl.BlockSpec(memory_space=pltpu.VMEM)] * 3,
        out_specs=[pl.BlockSpec(memory_space=pltpu.VMEM)] * 4,
        scratch_shapes=[pltpu.VMEM((4, rows * heads, width), F32)],
        compiler_params=pltpu.CompilerParams(vmem_limit_bytes=24 * 2**20),
        name="final",
    )(per_head, local, far)
    return tuple(out.reshape(rows, heads, width) for out in outs)


def per_device(queries, keys, values, out_grad, level_table):
    rows, heads, width = queries.shape
    half = heads // 2
    chips = lax.axis_size("seq")
    core = lax.axis_index("rep")
    chip = lax.axis_index("seq")
    local_levels = (rows // BLOCK).bit_length()
    scale = jnp.array([level_scale(level) for level in range(level_table.shape[0])], F32)
    weights = level_table * scale[:, None]

    send, keep, per_head = states(queries, keys, values, out_grad)
    received = swap_cores(send)
    total = keep + received
    mine = []
    for mask in range(chips - 1, 0, -1):
        later = (chip ^ mask) < chip
        mine.append((mask, later, swap_chips(jnp.where(later, total[1], total[0]), mask)))
    near_other = swap_cores(jnp.where(core == 0, keep[0], keep[1]))
    near_mine = jnp.where(core == 0, received[1], received[0])
    local = local_part(level_table, per_head)

    own = lax.dynamic_slice_in_dim(weights, core * half, half, 1)[:, :, None, None]
    others = lax.dynamic_slice_in_dim(weights, (1 - core) * half, half, 1)[:, :, None, None]
    upper = (core == 1).astype(F32)
    far = []
    for table, near, pieces in (
        (own, near_mine, [piece for _, _, piece in mine]),
        (others, near_other, [swap_cores(piece) for _, _, piece in mine]),
    ):
        keys_far = upper * table[local_levels] * near
        queries_far = (1.0 - upper) * table[local_levels] * near
        for (mask, later, _), piece in zip(mine, pieces):
            term = table[local_levels + mask.bit_length()] * piece
            keys_far += jnp.where(later, term, 0.0)
            queries_far += jnp.where(later, 0.0, term)
        far.append(jnp.stack([keys_far, queries_far]))
    first = jnp.where(core == 0, far[0], far[1])
    second = jnp.where(core == 0, far[1], far[0])
    return final_part(per_head, local, jnp.concatenate([first, second], axis=1))


def solution(mesh):
    part = P(("groups", "seq", "rep"), "head", None)
    return jax.shard_map(
        per_device,
        mesh=mesh,
        in_specs=(part, part, part, part, P(None, "head")),
        out_specs=(part, part, part, part),
        check_vma=False,
    )
```

time: 73.5 us -> 36.9 us (0.50)
  matrix products: 23.3 us -> 0 us
  waiting for transfers between devices: 31.2 us -> 11.4 us
  Pallas kernels: 0 us -> 11.5 us
  other arithmetic: 5.83 us -> 1.58 us
  local copies, waits for them, and re-layouts: 5.75 us -> 4.93 us
    dot_general x15 -> x0, matrix products: 23.3 us -> none  [product(): return jnp.einsum(form, left, right, precision=lax.Precision.HIGHEST)]
    ppermute x3 -> x8, waiting for transfers between devices: 31.2 us -> 11.4 us  [the longest x3 10.2 us: swap_chips(): lax.ppermute(block, 'seq', [(chip, chip ^ mask) for chip in range(count)])]
    pallas_call x0 -> x3, Pallas kernels: none -> 11.5 us  [the longest x1 7.53 us: local_part(): pl.pallas_call(local_kernel, grid=(heads,), out_shape=jax.ShapeDtypeStruc...]
    add x4 -> x1, other arithmetic: 4.6 us -> 0.05 us  [per_device(): total = keep + received]
    mul x3, other arithmetic: 0.38 us -> 1.12 us  [the longest x1 0.69 us: per_device(): weights = level_table * scale[:, None]]
    unnamed x20 -> x9, local copies, waits for them, and re-layouts: 5.54 us -> 4.92 us
    ppermute x3 -> x8, starting transfers between devices: 6.22 us -> 6.34 us  [the longest x3 5.75 us: swap_chips(): lax.ppermute(block, 'seq', [(chip, chip ^ mask) for chip in range(count)])]
  transfers between devices with their start and end apart: 3 -> 8, of which waited for: 3 -> 4; matrix products, arithmetic and copies ran while one was open for 8% -> 6% of each run, Pallas kernels for 0% -> 21%
where the time goes in v1:
time: 36.9 us; the launch traced here: 36.5 us
  Pallas kernels  11.5 us (31%)
  waiting for transfers between devices  11.4 us (31%)
  starting transfers between devices  6.34 us (17%)
  local copies, waits for them, and re-layouts  4.93 us (13%)
  other arithmetic  1.58 us (4%)
  between operations  0.75 us (2%)
    ppermute x3, waiting for transfers between devices, swap_chips(): lax.ppermute(block, 'seq', [(chip, chip ^ mask) for chip in range(count)])  10.2 us
    pallas_call x1, Pallas kernels, local_part(): pl.pallas_call(local_kernel, grid=(heads,), out_shape=jax.ShapeDtypeStruc...  7.53 us
    ppermute x3, starting transfers between devices, swap_chips(): lax.ppermute(block, 'seq', [(chip, chip ^ mask) for chip in range(count)])  5.75 us
    unnamed x9, local copies, waits for them, and re-layouts  4.92 us
    pallas_call x1, Pallas kernels, final_part(): pl.pallas_call(final_kernel, out_shape=[jax.ShapeDtypeStruct((rows * head...  2.6 us
    pallas_call x1, Pallas kernels, states(): pl.pallas_call(functools.partial(state_kernel, heads), out_shape=(jax.Sha...  1.4 us
    ppermute x5, waiting for transfers between devices, swap_cores(): return lax.ppermute(block, 'rep', [(0, 1), (1, 0)])  1.17 us
  transfers between devices with their start and end apart: 8, of which 4 were waited for; matrix products, arithmetic and copies ran while one was open for 6% of the time, Pallas kernels for 21%

profile of v1, /device:TPU:0, one launch (start us, length us, event | category | flops | bytes accessed | tf_op | source)
XLA Modules:
  0.0 36.5 jit_solution(10633247557348224386)
XLA Ops:
  0.6 0.0 copy-start
  0.6 1.0 %copy-done = bf16[512,4,128]{2,1,0:T(4,128)(2,1)S(1)} copy-done((bf16[512,4,128]{2,1,0:T(4,128)(2,1)S(1)}, bf16[512,4,128]{2,1,0:T(4,128)(2,1)}, u32[]{:S(2)}) %copy-start) | copy-done | bytes 524312
  1.7 0.0 copy-start.1
  1.7 1.0 %copy-done.1 = bf16[512,4,128]{2,1,0:T(4,128)(2,1)S(1)} copy-done((bf16[512,4,128]{2,1,0:T(4,128)(2,1)S(1)}, bf16[512,4,128]{2,1,0:T(4,128)(2,1)}, u32[]{:S(2)}) %copy-start.1) | copy-done | bytes 524312
  2.7 0.0 copy-start.2
  2.7 1.0 %copy-done.2 = bf16[512,4,128]{2,1,0:T(4,128)(2,1)S(1)} copy-done((bf16[512,4,128]{2,1,0:T(4,128)(2,1)S(1)}, bf16[512,4,128]{2,1,0:T(4,128)(2,1)}, u32[]{:S(2)}) %copy-start.2) | copy-done | bytes 524312
  3.8 0.0 copy-start.3
  3.8 1.0 %copy-done.3 = bf16[512,4,128]{2,1,0:T(4,128)(2,1)S(1)} copy-done((bf16[512,4,128]{2,1,0:T(4,128)(2,1)S(1)}, bf16[512,4,128]{2,1,0:T(4,128)(2,1)}, u32[]{:S(2)}) %copy-start.3) | copy-done | bytes 524312
  4.8 1.4 %states.1 = (f32[2,2,128,128]{3,2,1,0:T(8,128)S(1)}, f32[2,2,128,128]{3,2,1,0:T(8,128)S(1)}, bf16[4,4,512,128]{3,2,1,0:T(8,128)(2,1)S(1)}) custom-call(bf16[2048,128]{1,0:T(8,128)(2,1)S(1)} %bitcast.30, bf16[2048,128]{1,0:T(8,128)(2,1)S(1)} %bitcast.31, bf16[2048,128]{1,0:T(8,128)(2,1)S(1)} %bitcast.32, bf16[2048,128]{1,0:T(8,128)(2,1)S(1)} %bitcast.33), custom_call_target="tpu_custom_call" | custom-call | tf_op jit(solution)/shard_map/states/pallas_call | solution.py:68
  6.2 0.5 %collective-permute-start.4 = (f32[2,128,128]{2,1,0:T(8,128)S(1)}, f32[2,128,128]{2,1,0:T(8,128)S(1)}, u32[]{:S(2)}, u32[]{:S(2)}) collective-permute-start(f32[2,128,128]{2,1,0:T(8,128)S(1)} %select_bitcast_fusion), channel_id=1, source_target_pairs={{0,1},{1,0},{2,3},{3,2},{4,5},{5,4},{6,7},{7,6},{8,9},{9,8},{10,11... | collective-permute-start | bytes 393224 | tf_op jit(solution)/shard_map/ppermute | solution.py:19
  6.7 0.1 collective-permute-start
  6.8 0.8 %copy.10.table_ref = f32[7,4]{1,0:T(8,128)S(1)} copy(f32[7,4]{0,1:T(4,128)} %param.10) | data formatting | bytes 224 | tf_op args[4]
  7.6 0.7 %broadcast_multiply_fusion = f32[7,4]{0,1:T(4,128)S(1)} fusion(f32[7,4]{0,1:T(4,128)} %param.10, f32[7]{0:T(128)} %constant.25.clone), kind=kLoop, calls=%fused_computation.23 | loop fusion | flops 28 | bytes 252 | tf_op jit(solution)/shard_map/mul | solution.py:178
  8.3 7.5 %local.1.local_ref = f32[4,4,512,128]{3,2,1,0:T(8,128)S(1)} custom-call(f32[7,4]{1,0:T(8,128)S(1)} %copy.10.table_ref, bf16[4,4,512,128]{3,2,1,0:T(8,128)(2,1)S(1)} %get-tuple-element.11.per_head_ref), custom_call_target="tpu_custom_call" | custom-call | flops 3000000000 | bytes 6291456 | tf_op jit(solution)/shard_map/local/pallas_call | solution.py:121
  15.8 0.0 collective-permute-done
  15.9 5.1 %collective-permute-start.1 = (f32[2,128,128]{2,1,0:T(8,128)S(1)}, f32[2,128,128]{2,1,0:T(8,128)S(1)}, u32[]{:S(2)}, u32[]{:S(2)}) collective-permute-start(f32[2,128,128]{2,1,0:T(8,128)S(1)} %get-tuple-element.32), channel_id=1, source_target_pairs={{0,12},{4,8},{8,4},{12,0},{1,13},{5,9},{9,5},{13,1},{2,14},{6,10},... | collective-permute-start | bytes 393224 | tf_op jit(solution)/shard_map/ppermute | solution.py:24
  21.0 0.0 collective-permute-start.3
  21.0 0.6 %collective-permute-start.2 = (f32[2,128,128]{2,1,0:T(8,128)S(1)}, f32[2,128,128]{2,1,0:T(8,128)S(1)}, u32[]{:S(2)}, u32[]{:S(2)}) collective-permute-start(f32[2,128,128]{2,1,0:T(8,128)S(1)} %get-tuple-element.34), channel_id=1, source_target_pairs={{0,8},{4,12},{8,0},{12,4},{1,9},{5,13},{9,1},{13,5},{2,10},{6,14},... | collective-permute-start | bytes 393224 | tf_op jit(solution)/shard_map/ppermute | solution.py:24
  21.7 0.2 multiply_reduce_fusion.3
  21.9 0.2 multiply_reduce_fusion.1
  22.1 3.3 %collective-permute-done.1 = f32[2,128,128]{2,1,0:T(8,128)S(1)} collective-permute-done((f32[2,128,128]{2,1,0:T(8,128)S(1)}, f32[2,128,128]{2,1,0:T(8,128)S(1)}, u32[]{:S(2)}, u32[]{:S(2)}) %collective-permute-start.1) | collective-permute-done | bytes 131104 | tf_op jit(solution)/shard_map/ppermute | solution.py:24
  25.4 0.0 collective-permute-start.5
  25.4 3.3 %collective-permute-done.3 = f32[2,128,128]{2,1,0:T(8,128)S(1)} collective-permute-done((f32[2,128,128]{2,1,0:T(8,128)S(1)}, f32[2,128,128]{2,1,0:T(8,128)S(1)}, u32[]{:S(2)}, u32[]{:S(2)}) %collective-permute-start.3) | collective-permute-done | bytes 131104 | tf_op jit(solution)/shard_map/ppermute | solution.py:24
  28.7 0.0 collective-permute-start.7
  28.7 3.6 %collective-permute-done.2 = f32[2,128,128]{2,1,0:T(8,128)S(1)} collective-permute-done((f32[2,128,128]{2,1,0:T(8,128)S(1)}, f32[2,128,128]{2,1,0:T(8,128)S(1)}, u32[]{:S(2)}, u32[]{:S(2)}) %collective-permute-start.2) | collective-permute-done | bytes 131104 | tf_op jit(solution)/shard_map/ppermute | solution.py:24
  32.3 0.0 collective-permute-start.6
  32.3 0.1 add_bitcast_fusion.3
  32.5 0.0 collective-permute-done.4
  32.5 0.0 collective-permute-done.5
  32.5 0.0 collective-permute-done.7
  32.5 1.2 %collective-permute-done.6 = f32[2,128,128]{2,1,0:T(8,128)S(1)} collective-permute-done((f32[2,128,128]{2,1,0:T(8,128)S(1)}, f32[2,128,128]{2,1,0:T(8,128)S(1)}, u32[]{:S(2)}, u32[]{:S(2)}) %collective-permute-start.6) | collective-permute-done | bytes 131104 | tf_op jit(solution)/shard_map/ppermute | solution.py:19
  33.7 0.1 add_bitcast_fusion.1
  33.9 2.6 %final.1 = (bf16[2048,128]{1,0:T(8,128)(2,1)}, bf16[2048,128]{1,0:T(8,128)(2,1)}, bf16[2048,128]{1,0:T(8,128)(2,1)}, bf16[2048,128]{1,0:T(8,128)(2,1)}) custom-call(bf16[4,4,512,128]{3,2,1,0:T(8,128)(2,1)S(1)} %get-tuple-element.11.per_head_ref, f32[4,4,512,128]{3,2,1,0:T(8,128)S(1)} %local.1.local_ref, f32[2,4,128,128]{3,2,1,0:T(8,128)S(1)} %pad_maximum_fusion.far_ref), custom_call_target="tpu_custom_call" | custom-call | tf_op jit(solution)/shard_map/final/pallas_call | solution.py:158
  (6 shorter events, 0.2 us)
Async XLA Ops:
  0.6 1.0 %copy-start = (bf16[512,4,128]{2,1,0:T(4,128)(2,1)S(1)}, bf16[512,4,128]{2,1,0:T(4,128)(2,1)}, u32[]{:S(2)}) copy-start(bf16[512,4,128]{2,1,0:T(4,128)(2,1)} %param.6) | copy-start | bytes 1572868
  1.7 1.0 %copy-start.1 = (bf16[512,4,128]{2,1,0:T(4,128)(2,1)S(1)}, bf16[512,4,128]{2,1,0:T(4,128)(2,1)}, u32[]{:S(2)}) copy-start(bf16[512,4,128]{2,1,0:T(4,128)(2,1)} %param.7) | copy-start | bytes 1572868
  2.7 1.0 %copy-start.2 = (bf16[512,4,128]{2,1,0:T(4,128)(2,1)S(1)}, bf16[512,4,128]{2,1,0:T(4,128)(2,1)}, u32[]{:S(2)}) copy-start(bf16[512,4,128]{2,1,0:T(4,128)(2,1)} %param.8) | copy-start | bytes 1572868
  3.8 1.0 %copy-start.3 = (bf16[512,4,128]{2,1,0:T(4,128)(2,1)S(1)}, bf16[512,4,128]{2,1,0:T(4,128)(2,1)}, u32[]{:S(2)}) copy-start(bf16[512,4,128]{2,1,0:T(4,128)(2,1)} %param.9) | copy-start | bytes 1572868
  6.2 26.2 %collective-permute-start.4 = (f32[2,128,128]{2,1,0:T(8,128)S(1)}, f32[2,128,128]{2,1,0:T(8,128)S(1)}, u32[]{:S(2)}, u32[]{:S(2)}) collective-permute-start(f32[2,128,128]{2,1,0:T(8,128)S(1)} %select_bitcast_fusion), channel_id=1, source_target_pairs={{0,1},{1,0},{2,3},{3,2},{4,5},{5,4},{6,7},{7,6},{8,9},{9,8},{10,11... | collective-permute-start | bytes 393224 | tf_op jit(solution)/shard_map/ppermute | solution.py:19
  6.7 9.1 %collective-permute-start = (f32[2,2,128,128]{3,2,1,0:T(8,128)S(1)}, f32[2,2,128,128]{3,2,1,0:T(8,128)S(1)}, u32[]{:S(2)}, u32[]{:S(2)}) collective-permute-start(f32[2,2,128,128]{3,2,1,0:T(8,128)S(1)} %get-tuple-element.12), channel_id=1, source_target_pairs={{0,1},{1,0},{2,3},{3,2},{4,5},{5,4},{6,7},{7,6},{8,9},{9,8},{10,11... | collective-permute-start | bytes 786440 | tf_op jit(solution)/shard_map/ppermute | solution.py:19
  15.9 9.5 %collective-permute-start.1 = (f32[2,128,128]{2,1,0:T(8,128)S(1)}, f32[2,128,128]{2,1,0:T(8,128)S(1)}, u32[]{:S(2)}, u32[]{:S(2)}) collective-permute-start(f32[2,128,128]{2,1,0:T(8,128)S(1)} %get-tuple-element.32), channel_id=1, source_target_pairs={{0,12},{4,8},{8,4},{12,0},{1,13},{5,9},{9,5},{13,1},{2,14},{6,10},... | collective-permute-start | bytes 393224 | tf_op jit(solution)/shard_map/ppermute | solution.py:24
  21.0 7.7 %collective-permute-start.3 = (f32[2,128,128]{2,1,0:T(8,128)S(1)}, f32[2,128,128]{2,1,0:T(8,128)S(1)}, u32[]{:S(2)}, u32[]{:S(2)}) collective-permute-start(f32[2,128,128]{2,1,0:T(8,128)S(1)} %get-tuple-element.33), channel_id=1, source_target_pairs={{0,4},{4,0},{8,12},{12,8},{1,5},{5,1},{9,13},{13,9},{2,6},{6,2},{1... | collective-permute-start | bytes 393224 | tf_op jit(solution)/shard_map/ppermute | solution.py:24
  21.0 11.3 %collective-permute-start.2 = (f32[2,128,128]{2,1,0:T(8,128)S(1)}, f32[2,128,128]{2,1,0:T(8,128)S(1)}, u32[]{:S(2)}, u32[]{:S(2)}) collective-permute-start(f32[2,128,128]{2,1,0:T(8,128)S(1)} %get-tuple-element.34), channel_id=1, source_target_pairs={{0,8},{4,12},{8,0},{12,4},{1,9},{5,13},{9,1},{13,5},{2,10},{6,14},... | collective-permute-start | bytes 393224 | tf_op jit(solution)/shard_map/ppermute | solution.py:24
  25.4 7.1 %collective-permute-start.5 = (f32[2,128,128]{2,1,0:T(8,128)S(1)}, f32[2,128,128]{2,1,0:T(8,128)S(1)}, u32[]{:S(2)}, u32[]{:S(2)}) collective-permute-start(f32[2,128,128]{2,1,0:T(8,128)S(1)} %collective-permute-done.1), channel_id=1, source_target_pairs={{0,1},{1,0},{2,3},{3,2},{4,5},{5,4},{6,7},{7,6},{8,9},{9,8},{10,11... | collective-permute-start | bytes 393224 | tf_op jit(solution)/shard_map/ppermute | solution.py:19
  28.7 3.8 %collective-permute-start.7 = (f32[2,128,128]{2,1,0:T(8,128)S(1)}, f32[2,128,128]{2,1,0:T(8,128)S(1)}, u32[]{:S(2)}, u32[]{:S(2)}) collective-permute-start(f32[2,128,128]{2,1,0:T(8,128)S(1)} %collective-permute-done.3), channel_id=1, source_target_pairs={{0,1},{1,0},{2,3},{3,2},{4,5},{5,4},{6,7},{7,6},{8,9},{9,8},{10,11... | collective-permute-start | bytes 393224 | tf_op jit(solution)/shard_map/ppermute | solution.py:19
  32.3 1.3 %collective-permute-start.6 = (f32[2,128,128]{2,1,0:T(8,128)S(1)}, f32[2,128,128]{2,1,0:T(8,128)S(1)}, u32[]{:S(2)}, u32[]{:S(2)}) collective-permute-start(f32[2,128,128]{2,1,0:T(8,128)S(1)} %collective-permute-done.2), channel_id=1, source_target_pairs={{0,1},{1,0},{2,3},{3,2},{4,5},{5,4},{6,7},{7,6},{8,9},{9,8},{10,11... | collective-permute-start | bytes 393224 | tf_op jit(solution)/shard_map/ppermute | solution.py:19

commit v2 on v1

v2 whole, which is shorter than its diff:
```python
import functools
import math

import jax
import jax.numpy as jnp
import numpy as np
from jax import lax
from jax.experimental import pallas as pl
from jax.experimental.pallas import tpu as pltpu
from jax.sharding import PartitionSpec as P

BLOCK = 64
TILE = 128
CHUNKS = 2
F32 = jnp.float32
BF16 = jnp.bfloat16


def swap_cores(block):
    return lax.ppermute(block, "rep", [(0, 1), (1, 0)])


def swap_chips(block, mask):
    count = lax.axis_size("seq")
    return lax.ppermute(block, "seq", [(chip, chip ^ mask) for chip in range(count)])


def level_scale(level):
    return float(np.float32(1.0) / np.sqrt(np.float32(BLOCK * 2 ** max(level - 1, 0))))


def dot_tn(left, right):
    return lax.dot_general(left, right, (((0,), (0,)), ((), ())), preferred_element_type=F32)


def dot_nt(left, right):
    return lax.dot_general(left, right, (((1,), (1,)), ((), ())), preferred_element_type=F32)


def dot_nn(left, right):
    return lax.dot_general(left, right, (((1,), (0,)), ((), ())), preferred_element_type=F32)


def split(value):
    high = value.astype(BF16)
    return high, (value - high.astype(F32)).astype(BF16)


def state_kernel(heads, q_ref, k_ref, v_ref, g_ref, send_ref, keep_ref, per_head_ref, narrow, wide, arrived):
    rows = q_ref.shape[0] // heads
    half = heads // 2
    core = lax.axis_index("rep")
    sources = (q_ref, k_ref, v_ref, g_ref)
    length = rows * heads // CHUNKS

    def fetch(which, chunk):
        span = pl.ds(chunk * length, length)
        return pltpu.make_async_copy(sources[which].at[span], narrow.at[which, span], arrived.at[which, chunk])

    pairs = ((1, 2), (0, 3))
    for pair in pairs:
        for which in pair:
            for chunk in range(CHUNKS):
                fetch(which, chunk).start()
    for kind, pair in enumerate(pairs):
        for which in pair:
            for chunk in range(CHUNKS):
                fetch(which, chunk).wait()
            wide[which] = narrow[which].astype(F32)
            for head in range(heads):
                per_head_ref[which, head] = wide[which, pl.ds(head, rows, stride=heads), :].astype(BF16)
        for place in range(half):
            for owner, out_ref in ((1 - core, send_ref), (core, keep_ref)):
                head = owner * half + place
                out_ref[kind, place] = dot_tn(per_head_ref[pair[0], head], per_head_ref[pair[1], head])


def states(heads, flat):
    rows, width = flat[0].shape[0] // heads, flat[0].shape[1]
    half = (2, heads // 2, width, width)
    return pl.pallas_call(
        functools.partial(state_kernel, heads),
        out_shape=(
            jax.ShapeDtypeStruct(half, F32),
            jax.ShapeDtypeStruct(half, F32),
            jax.ShapeDtypeStruct((4, heads, rows, width), BF16),
        ),
        in_specs=[pl.BlockSpec(memory_space=pltpu.HBM)] * 4,
        out_specs=[pl.BlockSpec(memory_space=pltpu.VMEM)] * 3,
        scratch_shapes=[
            pltpu.VMEM((4, rows * heads, width), BF16),
            pltpu.VMEM((4, rows * heads, width), F32),
            pltpu.SemaphoreType.DMA((4, CHUNKS)),
        ],
        compiler_params=pltpu.CompilerParams(vmem_limit_bytes=24 * 2**20),
        name="states",
    )(*[pltpu.with_memory_space_constraint(array, pltpu.HBM) for array in flat])


def local_kernel(table_ref, per_head_ref, out_ref):
    head = pl.program_id(0)
    rows = per_head_ref.shape[1]
    tiles = rows // TILE
    inner = (TILE // BLOCK).bit_length()
    weight = [table_ref[level, head] * level_scale(level) for level in range(inner + tiles.bit_length() - 1)]
    row = lax.broadcasted_iota(jnp.int32, (TILE, TILE), 0)
    column = lax.broadcasted_iota(jnp.int32, (TILE, TILE), 1)
    apart = jnp.bitwise_xor(row // BLOCK, column // BLOCK)
    level_mask = jnp.where(apart == 0, weight[0], weight[1])
    for level in range(2, inner):
        level_mask = jnp.where(apart >= 1 << (level - 1), weight[level], level_mask)
    lower = jnp.where(row >= column, level_mask, 0.0)
    upper = jnp.where(row <= column, level_mask, 0.0)
    part = [[per_head_ref[which, pl.ds(tile * TILE, TILE), :] for tile in range(tiles)] for which in range(4)]
    queries, keys, values, out_grad = part

    def sums(states):
        table = {(0, tile): states[tile] for tile in range(tiles)}
        for bit in range(1, tiles.bit_length() - 1):
            for group in range(tiles >> bit):
                table[bit, group] = table[bit - 1, 2 * group] + table[bit - 1, 2 * group + 1]
        return table

    def gather(table, tile, side):
        total = None
        for bit in range(tiles.bit_length() - 1):
            if (tile >> bit) % 2 == side:
                term = weight[inner + bit] * table[bit, (tile >> bit) ^ 1]
                total = term if total is None else total + term
        return [] if total is None else split(total)

    key_sums = sums([dot_tn(keys[tile], values[tile]) for tile in range(tiles)])
    query_sums = sums([dot_tn(queries[tile], out_grad[tile]) for tile in range(tiles)])
    for tile in range(tiles):
        q, k, v, g = (array[tile] for array in part)
        read, back = gather(key_sums, tile, 1), gather(query_sums, tile, 0)
        terms = (
            (dot_nt(q, k) * lower, v, q, read, dot_nn),
            (dot_nt(g, v) * lower, k, g, read, dot_nt),
            (dot_nt(v, g) * upper, q, v, back, dot_nt),
            (dot_nt(k, q) * upper, g, k, back, dot_nn),
        )
        for which, (inside, other, mine, pieces, multiply) in enumerate(terms):
            result = dot_nn(jnp.concatenate(split(inside), 1), jnp.concatenate([other, other], 0))
            for piece in pieces:
                result += multiply(mine, piece)
            out_ref[which, pl.ds(tile * TILE, TILE), :] = result


def local_part(level_table, per_head):
    _, heads, rows, width = per_head.shape
    block = pl.BlockSpec((4, None, rows, width), lambda head: (0, head, 0, 0))
    return pl.pallas_call(
        local_kernel,
        grid=(heads,),
        out_shape=jax.ShapeDtypeStruct((4, heads, rows, width), F32),
        in_specs=[pl.BlockSpec(memory_space=pltpu.SMEM), block],
        out_specs=block,
        compiler_params=pltpu.CompilerParams(vmem_limit_bytes=24 * 2**20),
        cost_estimate=pl.CostEstimate(flops=3 * 10**9, bytes_accessed=6 * 2**20, transcendentals=0),
        name="local",
    )(level_table, per_head)


def final_kernel(per_head_ref, local_ref, far_ref, *refs):
    out_refs, (wide, narrow, left) = refs[:4], refs[4:]
    heads, rows = per_head_ref.shape[1:3]
    far = [[split(far_ref[kind, head]) for head in range(heads)] for kind in range(2)]
    plan = ((0, 0, 0, dot_nn), (1, 3, 0, dot_nt), (2, 2, 1, dot_nt), (3, 1, 1, dot_nn))
    copies = []
    for which, source, kind, multiply in plan:
        for head in range(heads):
            result = local_ref[which, head]
            for piece in far[kind][head]:
                result += multiply(per_head_ref[source, head], piece)
            wide[which, pl.ds(head, rows, stride=heads), :] = result
        narrow[which] = wide[which].astype(BF16)
        copy = pltpu.make_async_copy(narrow.at[which], out_refs[which], left.at[which])
        copy.start()
        copies.append(copy)
    for copy in copies:
        copy.wait()


def final_part(per_head, local, far):
    _, heads, rows, width = per_head.shape
    outs = pl.pallas_call(
        final_kernel,
        out_shape=[jax.ShapeDtypeStruct((rows * heads, width), BF16)] * 4,
        in_specs=[pl.BlockSpec(memory_space=pltpu.VMEM)] * 3,
        out_specs=[pl.BlockSpec(memory_space=pltpu.HBM)] * 4,
        scratch_shapes=[
            pltpu.VMEM((4, rows * heads, width), F32),
            pltpu.VMEM((4, rows * heads, width), BF16),
            pltpu.SemaphoreType.DMA((4,)),
        ],
        compiler_params=pltpu.CompilerParams(vmem_limit_bytes=24 * 2**20),
        name="final",
    )(per_head, local, far)
    return tuple(out.reshape(rows, heads, width) for out in outs)


def per_device(queries, keys, values, out_grad, level_table):
    rows, heads, width = queries.shape
    half = heads // 2
    chips = lax.axis_size("seq")
    core = lax.axis_index("rep")
    chip = lax.axis_index("seq")
    local_levels = (rows // BLOCK).bit_length()
    scale = jnp.array([level_scale(level) for level in range(level_table.shape[0])], F32)
    weights = level_table * scale[:, None]

    flat = [array.reshape(rows * heads, width) for array in (queries, keys, values, out_grad)]
    send, keep, per_head = states(heads, flat)
    received = swap_cores(send)
    total = keep + received
    masks = range(chips - 1, 0, -1)
    payloads = [jnp.where((chip ^ mask) < chip, total[1], total[0]) for mask in masks]
    payloads, held = lax.optimization_barrier((payloads, per_head))
    mine = [(mask, (chip ^ mask) < chip, swap_chips(payload, mask)) for mask, payload in zip(masks, payloads)]
    near_other = swap_cores(jnp.where(core == 0, keep[0], keep[1]))
    near_mine = jnp.where(core == 0, received[1], received[0])
    local = local_part(level_table, held)

    own = lax.dynamic_slice_in_dim(weights, core * half, half, 1)[:, :, None, None]
    others = lax.dynamic_slice_in_dim(weights, (1 - core) * half, half, 1)[:, :, None, None]
    upper = (core == 1).astype(F32)
    far = []
    for table, near, pieces in (
        (own, near_mine, [piece for _, _, piece in mine]),
        (others, near_other, [swap_cores(piece) for _, _, piece in mine]),
    ):
        keys_far = upper * table[local_levels] * near
        queries_far = (1.0 - upper) * table[local_levels] * near
        for (mask, later, _), piece in zip(mine, pieces):
            term = table[local_levels + mask.bit_length()] * piece
            keys_far += jnp.where(later, term, 0.0)
            queries_far += jnp.where(later, 0.0, term)
        far.append(jnp.stack([keys_far, queries_far]))
    first = jnp.where(core == 0, far[0], far[1])
    second = jnp.where(core == 0, far[1], far[0])
    return final_part(per_head, local, jnp.concatenate([first, second], axis=1))


def solution(mesh):
    part = P(("groups", "seq", "rep"), "head", None)
    return jax.shard_map(
        per_device,
        mesh=mesh,
        in_specs=(part, part, part, part, P(None, "head")),
        out_specs=(part, part, part, part),
        check_vma=False,
    )
```

time: 36.9 us -> 26.5 us (0.72)
  waiting for transfers between devices: 11.4 us -> 5.14 us
  local copies, waits for them, and re-layouts: 4.93 us -> 0.78 us
  starting transfers between devices: 6.34 us -> 6.91 us
  Pallas kernels: 11.5 us -> 11.1 us
    ppermute x3, waiting for transfers between devices: 10.2 us -> 4.28 us  [swap_chips(): lax.ppermute(block, 'seq', [(chip, chip ^ mask) for chip in range(count)])]
    unnamed x9 -> x1, local copies, waits for them, and re-layouts: 4.92 us -> 0.77 us
    pallas_call x1, Pallas kernels: 7.53 us -> 6.3 us  [local_part(): pl.pallas_call(local_kernel, grid=(heads,), out_shape=jax.ShapeDtypeStruc...]
    pallas_call x1, Pallas kernels: 1.4 us -> 2.57 us  [states(): pl.pallas_call(functools.partial(state_kernel, heads), out_shape=(jax.Sha...]
    ppermute x5, starting transfers between devices: 0.59 us -> 1.16 us  [swap_cores(): return lax.ppermute(block, 'rep', [(0, 1), (1, 0)])]
  transfers between devices with their start and end apart: 8 -> 8, of which waited for: 4 -> 3; matrix products, arithmetic and copies ran while one was open for 6% -> 8% of each run, Pallas kernels for 21% -> 24%
where the time goes in v2:
time: 26.5 us; the launch traced here: 26.3 us
  Pallas kernels  11.1 us (42%)
  starting transfers between devices  6.91 us (26%)
  waiting for transfers between devices  5.14 us (19%)
  other arithmetic  1.58 us (6%)
  local copies, waits for them, and re-layouts  0.78 us (3%)
  between operations  0.75 us (3%)
    pallas_call x1, Pallas kernels, local_part(): pl.pallas_call(local_kernel, grid=(heads,), out_shape=jax.ShapeDtypeStruc...  6.3 us
    ppermute x3, starting transfers between devices, swap_chips(): lax.ppermute(block, 'seq', [(chip, chip ^ mask) for chip in range(count)])  5.76 us
    ppermute x3, waiting for transfers between devices, swap_chips(): lax.ppermute(block, 'seq', [(chip, chip ^ mask) for chip in range(count)])  4.28 us
    pallas_call x1, Pallas kernels, states(): pl.pallas_call(functools.partial(state_kernel, heads), out_shape=(jax.Sha...  2.57 us
    pallas_call x1, Pallas kernels, final_part(): pl.pallas_call(final_kernel, out_shape=[jax.ShapeDtypeStruct((rows * head...  2.26 us
    ppermute x5, starting transfers between devices, swap_cores(): return lax.ppermute(block, 'rep', [(0, 1), (1, 0)])  1.16 us
    ppermute x5, waiting for transfers between devices, swap_cores(): return lax.ppermute(block, 'rep', [(0, 1), (1, 0)])  0.86 us
    unnamed x1, local copies, waits for them, and re-layouts  0.77 us
  transfers between devices with their start and end apart: 8, of which 3 were waited for; matrix products, arithmetic and copies ran while one was open for 8% of the time, Pallas kernels for 24%

profile of v2, /device:TPU:0, one launch (start us, length us, event | category | flops | bytes accessed | tf_op | source)
XLA Modules:
  0.0 26.3 jit_solution(11109868532842180524)
XLA Ops:
  0.6 2.6 %states.1 = (f32[2,2,128,128]{3,2,1,0:T(8,128)S(1)}, f32[2,2,128,128]{3,2,1,0:T(8,128)S(1)}, bf16[4,4,512,128]{3,2,1,0:T(8,128)(2,1)S(1)}) custom-call(bf16[2048,128]{1,0:T(8,128)(2,1)} %bitcast.30, bf16[2048,128]{1,0:T(8,128)(2,1)} %bitcast.31, bf16[2048,128]{1,0:T(8,128)(2,1)} %bitcast.32, bf16[2048,128]{1,0:T(8,128)(2,1)} %bitcast.33), custom_call_target="tpu_custom_call" | custom-call | tf_op jit(solution)/shard_map/states/pallas_call | solution.py:81
  3.2 0.5 %collective-permute-start.4 = (f32[2,128,128]{2,1,0:T(8,128)S(1)}, f32[2,128,128]{2,1,0:T(8,128)S(1)}, u32[]{:S(2)}, u32[]{:S(2)}) collective-permute-start(f32[2,128,128]{2,1,0:T(8,128)S(1)} %select_bitcast_fusion), channel_id=1, source_target_pairs={{0,1},{1,0},{2,3},{3,2},{4,5},{5,4},{6,7},{7,6},{8,9},{9,8},{10,11... | collective-permute-start | bytes 393224 | tf_op jit(solution)/shard_map/ppermute | solution.py:20
  3.7 0.1 collective-permute-start
  3.8 0.7 %broadcast_multiply_fusion = f32[7,4]{0,1:T(4,128)S(1)} fusion(f32[7,4]{0,1:T(4,128)} %param.10, f32[7]{0:T(128)} %constant.25.clone), kind=kLoop, calls=%fused_computation.23 | loop fusion | flops 28 | bytes 252 | tf_op jit(solution)/shard_map/mul | solution.py:211
  4.5 0.8 %copy.10.table_ref = f32[7,4]{1,0:T(8,128)S(1)} copy(f32[7,4]{0,1:T(4,128)} %param.10) | data formatting | bytes 224 | tf_op args[4]
  5.3 0.2 multiply_reduce_fusion.3
  5.5 0.2 multiply_reduce_fusion.1
  5.7 0.0 collective-permute-done
  5.8 5.1 %collective-permute-start.1 = (f32[2,128,128]{2,1,0:T(8,128)S(1)}, f32[2,128,128]{2,1,0:T(8,128)S(1)}, u32[]{:S(2)}, u32[]{:S(2)}) collective-permute-start(f32[2,128,128]{2,1,0:T(8,128)S(1)} %get-tuple-element.19), channel_id=1, source_target_pairs={{0,12},{4,8},{8,4},{12,0},{1,13},{5,9},{9,5},{13,1},{2,14},{6,10},... | collective-permute-start | bytes 393224 | tf_op jit(solution)/shard_map/ppermute | solution.py:25
  10.9 0.0 collective-permute-start.2
  10.9 0.6 %collective-permute-start.3 = (f32[2,128,128]{2,1,0:T(8,128)S(1)}, f32[2,128,128]{2,1,0:T(8,128)S(1)}, u32[]{:S(2)}, u32[]{:S(2)}) collective-permute-start(f32[2,128,128]{2,1,0:T(8,128)S(1)} %get-tuple-element.21), channel_id=1, source_target_pairs={{0,4},{4,0},{8,12},{12,8},{1,5},{5,1},{9,13},{13,9},{2,6},{6,2},{1... | collective-permute-start | bytes 393224 | tf_op jit(solution)/shard_map/ppermute | solution.py:25
  11.6 6.3 %local.1.local_ref = f32[4,4,512,128]{3,2,1,0:T(8,128)S(1)} custom-call(f32[7,4]{1,0:T(8,128)S(1)} %copy.10.table_ref, bf16[4,4,512,128]{3,2,1,0:T(8,128)(2,1)S(1)} %get-tuple-element.18.per_head_ref), custom_call_target="tpu_custom_call" | custom-call | flops 3000000000 | bytes 6291456 | tf_op jit(solution)/shard_map/local/pallas_call | solution.py:153
  17.9 0.0 collective-permute-done.1
  17.9 0.1 collective-permute-start.5
  18.0 4.3 %collective-permute-done.2 = f32[2,128,128]{2,1,0:T(8,128)S(1)} collective-permute-done((f32[2,128,128]{2,1,0:T(8,128)S(1)}, f32[2,128,128]{2,1,0:T(8,128)S(1)}, u32[]{:S(2)}, u32[]{:S(2)}) %collective-permute-start.2) | collective-permute-done | bytes 131104 | tf_op jit(solution)/shard_map/ppermute | solution.py:25
  22.3 0.0 collective-permute-start.6
  22.3 0.0 collective-permute-done.3
  22.3 0.5 %collective-permute-start.7 = (f32[2,128,128]{2,1,0:T(8,128)S(1)}, f32[2,128,128]{2,1,0:T(8,128)S(1)}, u32[]{:S(2)}, u32[]{:S(2)}) collective-permute-start(f32[2,128,128]{2,1,0:T(8,128)S(1)} %collective-permute-done.3), channel_id=1, source_target_pairs={{0,1},{1,0},{2,3},{3,2},{4,5},{5,4},{6,7},{7,6},{8,9},{9,8},{10,11... | collective-permute-start | bytes 393224 | tf_op jit(solution)/shard_map/ppermute | solution.py:20
  22.8 0.1 add_bitcast_fusion.3
  22.9 0.0 collective-permute-done.4
  22.9 0.0 collective-permute-done.5
  22.9 0.7 %collective-permute-done.6 = f32[2,128,128]{2,1,0:T(8,128)S(1)} collective-permute-done((f32[2,128,128]{2,1,0:T(8,128)S(1)}, f32[2,128,128]{2,1,0:T(8,128)S(1)}, u32[]{:S(2)}, u32[]{:S(2)}) %collective-permute-start.6) | collective-permute-done | bytes 131104 | tf_op jit(solution)/shard_map/ppermute | solution.py:20
  23.6 0.2 collective-permute-done.7
  23.8 0.1 add_bitcast_fusion.1
  24.0 2.3 %final.1 = (bf16[2048,128]{1,0:T(8,128)(2,1)}, bf16[2048,128]{1,0:T(8,128)(2,1)}, bf16[2048,128]{1,0:T(8,128)(2,1)}, bf16[2048,128]{1,0:T(8,128)(2,1)}) custom-call(bf16[4,4,512,128]{3,2,1,0:T(8,128)(2,1)S(1)} %get-tuple-element.18.per_head_ref, f32[4,4,512,128]{3,2,1,0:T(8,128)S(1)} %local.1.local_ref, f32[2,4,128,128]{3,2,1,0:T(8,128)S(1)} %pad_maximum_fusion.far_ref), custom_call_target="tpu_custom_call" | custom-call | tf_op jit(solution)/shard_map/final/pallas_call | solution.py:187
  (6 shorter events, 0.2 us)
Async XLA Ops:
  3.2 19.7 %collective-permute-start.4 = (f32[2,128,128]{2,1,0:T(8,128)S(1)}, f32[2,128,128]{2,1,0:T(8,128)S(1)}, u32[]{:S(2)}, u32[]{:S(2)}) collective-permute-start(f32[2,128,128]{2,1,0:T(8,128)S(1)} %select_bitcast_fusion), channel_id=1, source_target_pairs={{0,1},{1,0},{2,3},{3,2},{4,5},{5,4},{6,7},{7,6},{8,9},{9,8},{10,11... | collective-permute-start | bytes 393224 | tf_op jit(solution)/shard_map/ppermute | solution.py:20
  3.7 2.0 %collective-permute-start = (f32[2,2,128,128]{3,2,1,0:T(8,128)S(1)}, f32[2,2,128,128]{3,2,1,0:T(8,128)S(1)}, u32[]{:S(2)}, u32[]{:S(2)}) collective-permute-start(f32[2,2,128,128]{3,2,1,0:T(8,128)S(1)} %get-tuple-element.17), channel_id=1, source_target_pairs={{0,1},{1,0},{2,3},{3,2},{4,5},{5,4},{6,7},{7,6},{8,9},{9,8},{10,11... | collective-permute-start | bytes 786440 | tf_op jit(solution)/shard_map/ppermute | solution.py:20
  5.8 12.1 %collective-permute-start.1 = (f32[2,128,128]{2,1,0:T(8,128)S(1)}, f32[2,128,128]{2,1,0:T(8,128)S(1)}, u32[]{:S(2)}, u32[]{:S(2)}) collective-permute-start(f32[2,128,128]{2,1,0:T(8,128)S(1)} %get-tuple-element.19), channel_id=1, source_target_pairs={{0,12},{4,8},{8,4},{12,0},{1,13},{5,9},{9,5},{13,1},{2,14},{6,10},... | collective-permute-start | bytes 393224 | tf_op jit(solution)/shard_map/ppermute | solution.py:25
  10.9 11.3 %collective-permute-start.2 = (f32[2,128,128]{2,1,0:T(8,128)S(1)}, f32[2,128,128]{2,1,0:T(8,128)S(1)}, u32[]{:S(2)}, u32[]{:S(2)}) collective-permute-start(f32[2,128,128]{2,1,0:T(8,128)S(1)} %get-tuple-element.20), channel_id=1, source_target_pairs={{0,8},{4,12},{8,0},{12,4},{1,9},{5,13},{9,1},{13,5},{2,10},{6,14},... | collective-permute-start | bytes 393224 | tf_op jit(solution)/shard_map/ppermute | solution.py:25
  10.9 11.3 %collective-permute-start.3 = (f32[2,128,128]{2,1,0:T(8,128)S(1)}, f32[2,128,128]{2,1,0:T(8,128)S(1)}, u32[]{:S(2)}, u32[]{:S(2)}) collective-permute-start(f32[2,128,128]{2,1,0:T(8,128)S(1)} %get-tuple-element.21), channel_id=1, source_target_pairs={{0,4},{4,0},{8,12},{12,8},{1,5},{5,1},{9,13},{13,9},{2,6},{6,2},{1... | collective-permute-start | bytes 393224 | tf_op jit(solution)/shard_map/ppermute | solution.py:25
  17.9 5.0 %collective-permute-start.5 = (f32[2,128,128]{2,1,0:T(8,128)S(1)}, f32[2,128,128]{2,1,0:T(8,128)S(1)}, u32[]{:S(2)}, u32[]{:S(2)}) collective-permute-start(f32[2,128,128]{2,1,0:T(8,128)S(1)} %collective-permute-done.1), channel_id=1, source_target_pairs={{0,1},{1,0},{2,3},{3,2},{4,5},{5,4},{6,7},{7,6},{8,9},{9,8},{10,11... | collective-permute-start | bytes 393224 | tf_op jit(solution)/shard_map/ppermute | solution.py:20
  22.3 1.3 %collective-permute-start.6 = (f32[2,128,128]{2,1,0:T(8,128)S(1)}, f32[2,128,128]{2,1,0:T(8,128)S(1)}, u32[]{:S(2)}, u32[]{:S(2)}) collective-permute-start(f32[2,128,128]{2,1,0:T(8,128)S(1)} %collective-permute-done.2), channel_id=1, source_target_pairs={{0,1},{1,0},{2,3},{3,2},{4,5},{5,4},{6,7},{7,6},{8,9},{9,8},{10,11... | collective-permute-start | bytes 393224 | tf_op jit(solution)/shard_map/ppermute | solution.py:20
  22.3 1.5 %collective-permute-start.7 = (f32[2,128,128]{2,1,0:T(8,128)S(1)}, f32[2,128,128]{2,1,0:T(8,128)S(1)}, u32[]{:S(2)}, u32[]{:S(2)}) collective-permute-start(f32[2,128,128]{2,1,0:T(8,128)S(1)} %collective-permute-done.3), channel_id=1, source_target_pairs={{0,1},{1,0},{2,3},{3,2},{4,5},{5,4},{6,7},{7,6},{8,9},{9,8},{10,11... | collective-permute-start | bytes 393224 | tf_op jit(solution)/shard_map/ppermute | solution.py:20

commit v3 on v2

v3 whole, which is shorter than its diff:
```python
import functools
import math

import jax
import jax.numpy as jnp
import numpy as np
from jax import lax
from jax.experimental import pallas as pl
from jax.experimental.pallas import tpu as pltpu
from jax.sharding import PartitionSpec as P

BLOCK = 64
TILE = 128
CHUNKS = 2
F32 = jnp.float32
BF16 = jnp.bfloat16


def swap_cores(block):
    return lax.ppermute(block, "rep", [(0, 1), (1, 0)])


def swap_chips(block, mask):
    count = lax.axis_size("seq")
    return lax.ppermute(block, "seq", [(chip, chip ^ mask) for chip in range(count)])


def level_scale(level):
    return float(np.float32(1.0) / np.sqrt(np.float32(BLOCK * 2 ** max(level - 1, 0))))


def dot_tn(left, right):
    return lax.dot_general(left, right, (((0,), (0,)), ((), ())), preferred_element_type=F32)


def dot_nt(left, right):
    return lax.dot_general(left, right, (((1,), (1,)), ((), ())), preferred_element_type=F32)


def dot_nn(left, right):
    return lax.dot_general(left, right, (((1,), (0,)), ((), ())), preferred_element_type=F32)


def split(value):
    high = value.astype(BF16)
    return high, (value - high.astype(F32)).astype(BF16)


def state_kernel(heads, q_ref, k_ref, v_ref, g_ref, send_ref, keep_ref, per_head_ref, narrow, wide, arrived):
    rows = q_ref.shape[0] // heads
    half = heads // 2
    core = lax.axis_index("rep")
    sources = (q_ref, k_ref, v_ref, g_ref)
    length = rows * heads // CHUNKS

    def fetch(which, chunk):
        span = pl.ds(chunk * length, length)
        return pltpu.make_async_copy(sources[which].at[span], narrow.at[which, span], arrived.at[which, chunk])

    pairs = ((1, 2), (0, 3))
    for pair in pairs:
        for which in pair:
            for chunk in range(CHUNKS):
                fetch(which, chunk).start()
    for kind, pair in enumerate(pairs):
        for which in pair:
            for chunk in range(CHUNKS):
                fetch(which, chunk).wait()
            wide[which] = narrow[which].astype(F32)
            for head in range(heads):
                per_head_ref[which, head] = wide[which, pl.ds(head, rows, stride=heads), :].astype(BF16)
        for place in range(half):
            for owner, out_ref in ((1 - core, send_ref), (core, keep_ref)):
                head = owner * half + place
                out_ref[kind, place] = dot_tn(per_head_ref[pair[0], head], per_head_ref[pair[1], head])


def states(heads, flat):
    rows, width = flat[0].shape[0] // heads, flat[0].shape[1]
    half = (2, heads // 2, width, width)
    return pl.pallas_call(
        functools.partial(state_kernel, heads),
        out_shape=(
            jax.ShapeDtypeStruct(half, F32),
            jax.ShapeDtypeStruct(half, F32),
            jax.ShapeDtypeStruct((4, heads, rows, width), BF16),
        ),
        in_specs=[pl.BlockSpec(memory_space=pltpu.HBM)] * 4,
        out_specs=[pl.BlockSpec(memory_space=pltpu.VMEM)] * 3,
        scratch_shapes=[
            pltpu.VMEM((4, rows * heads, width), BF16),
            pltpu.VMEM((4, rows * heads, width), F32),
            pltpu.SemaphoreType.DMA((4, CHUNKS)),
        ],
        compiler_params=pltpu.CompilerParams(vmem_limit_bytes=24 * 2**20),
        name="states",
    )(*[pltpu.with_memory_space_constraint(array, pltpu.HBM) for array in flat])


def local_kernel(chosen, table_ref, per_head_ref, *refs):
    out_ref = refs[-1]
    rows = per_head_ref.shape[2]
    for head in chosen:
        local_head(head, rows, table_ref, per_head_ref.at[:, head], out_ref.at[:, head])


def local_head(head, rows, table_ref, per_head_ref, out_ref):
    tiles = rows // TILE
    inner = (TILE // BLOCK).bit_length()
    weight = [table_ref[head, level] * level_scale(level) for level in range(inner + tiles.bit_length() - 1)]
    row = lax.broadcasted_iota(jnp.int32, (TILE, TILE), 0)
    column = lax.broadcasted_iota(jnp.int32, (TILE, TILE), 1)
    apart = jnp.bitwise_xor(row // BLOCK, column // BLOCK)
    level_mask = jnp.where(apart == 0, weight[0], weight[1])
    for level in range(2, inner):
        level_mask = jnp.where(apart >= 1 << (level - 1), weight[level], level_mask)
    lower = jnp.where(row >= column, level_mask, 0.0)
    upper = jnp.where(row <= column, level_mask, 0.0)
    part = [[per_head_ref[which, pl.ds(tile * TILE, TILE), :] for tile in range(tiles)] for which in range(4)]
    queries, keys, values, out_grad = part

    def sums(states):
        table = {(0, tile): states[tile] for tile in range(tiles)}
        for bit in range(1, tiles.bit_length() - 1):
            for group in range(tiles >> bit):
                table[bit, group] = table[bit - 1, 2 * group] + table[bit - 1, 2 * group + 1]
        return table

    def gather(table, tile, side):
        total = None
        for bit in range(tiles.bit_length() - 1):
            if (tile >> bit) % 2 == side:
                term = weight[inner + bit] * table[bit, (tile >> bit) ^ 1]
                total = term if total is None else total + term
        return [] if total is None else split(total)

    turned = [[block.T for block in array] for array in part]
    q_t, k_t, v_t, g_t = turned
    key_sums = sums([dot_nn(k_t[tile], values[tile]) for tile in range(tiles)])
    key_sums_t = sums([dot_nn(v_t[tile], keys[tile]) for tile in range(tiles)])
    query_sums = sums([dot_nn(q_t[tile], out_grad[tile]) for tile in range(tiles)])
    query_sums_t = sums([dot_nn(g_t[tile], queries[tile]) for tile in range(tiles)])
    held = []
    for tile in range(tiles):
        q, k, v, g = (array[tile] for array in part)
        terms = (
            (dot_nn(q, k_t[tile]) * lower, v, q, gather(key_sums, tile, 1)),
            (dot_nn(g, v_t[tile]) * lower, k, g, gather(key_sums_t, tile, 1)),
            (dot_nn(v, g_t[tile]) * upper, q, v, gather(query_sums_t, tile, 0)),
            (dot_nn(k, q_t[tile]) * upper, g, k, gather(query_sums, tile, 0)),
        )
        held.append(terms)
    for tile in range(tiles):
        for which, (inside, other, mine, pieces) in enumerate(held[tile]):
            result = dot_nn(jnp.concatenate([*split(inside), *([mine, mine] if pieces else [])], 1), jnp.concatenate([other, other, *pieces], 0))
            out_ref[which, pl.ds(tile * TILE, TILE), :] = result


def local_part(chosen, flops, table, per_head, *earlier):
    vmem = pl.BlockSpec(memory_space=pltpu.VMEM)
    return pl.pallas_call(
        functools.partial(local_kernel, chosen),
        out_shape=jax.ShapeDtypeStruct(per_head.shape, F32),
        in_specs=[pl.BlockSpec(memory_space=pltpu.SMEM)] + [vmem] * (1 + len(earlier)),
        out_specs=vmem,
        input_output_aliases={2: 0} if earlier else {},
        compiler_params=pltpu.CompilerParams(vmem_limit_bytes=16 * 2**20),
        cost_estimate=pl.CostEstimate(flops=flops, bytes_accessed=flops // 1000, transcendentals=0),
        name="local",
    )(table, per_head, *earlier)


def far_states(table_ref, head, rows, near, pair, groups):
    core, chip = lax.axis_index("rep"), lax.axis_index("seq")
    terms = [(core == 1, near), (chip % 2 == 1, pair)]
    terms += [((chip >> bit) % 2 == 1, group) for bit, group in enumerate(groups, 1)]
    keys_far = queries_far = 0.0
    for level, (later, piece) in enumerate(terms, (rows // BLOCK).bit_length()):
        weight = table_ref[head, level] * level_scale(level)
        keys_far += jnp.where(later, weight, 0.0) * piece
        queries_far += jnp.where(later, 0.0, weight) * piece
    return [jnp.concatenate(split(state), 0) for state in (keys_far, keys_far.T, queries_far.T, queries_far)]


def far_heads(owner, table_ref, per_head_ref, local_ref, near, pair_ref, group_ref, wide_ref, finish=None):
    heads, rows = per_head_ref.shape[1:3]
    half = heads // 2
    chosen = [owner * half + place for place in range(half)]
    states = [
        far_states(table_ref, head, rows, near(place), pair_ref[place], [group_ref[place, bit] for bit in range(group_ref.shape[1])])
        for place, head in enumerate(chosen)
    ]
    for which, source in enumerate((0, 3, 2, 1)):
        for head, pieces in zip(chosen, states):
            mine = per_head_ref[source, head]
            result = local_ref[which, head] + dot_nn(jnp.concatenate([mine, mine], 1), pieces[which])
            wide_ref[which, pl.ds(head, rows, stride=heads), :] = result
        if finish is not None:
            finish(which)


def own_kernel(table_ref, per_head_ref, local_ref, received_ref, pair_ref, group_ref, wide_ref):
    core = lax.axis_index("rep")
    far_heads(core, table_ref, per_head_ref, local_ref, lambda place: received_ref[1 - core, place],
              pair_ref, group_ref, wide_ref)


def last_kernel(table_ref, per_head_ref, local_ref, near_ref, pair_ref, group_ref, _, *refs):
    out_refs, (wide_ref, narrow, left) = refs[:4], refs[4:]
    copies = []

    def finish(which):
        narrow[which] = wide_ref[which].astype(BF16)
        copy = pltpu.make_async_copy(narrow.at[which], out_refs[which], left.at[which])
        copy.start()
        copies.append(copy)

    far_heads(1 - lax.axis_index("rep"), table_ref, per_head_ref, local_ref, lambda place: near_ref[place],
              pair_ref, group_ref, wide_ref, finish)
    for copy in copies:
        copy.wait()


def own_part(table, per_head, *operands):
    _, heads, rows, width = per_head.shape
    vmem = pl.BlockSpec(memory_space=pltpu.VMEM)
    return pl.pallas_call(
        own_kernel,
        out_shape=jax.ShapeDtypeStruct((4, rows * heads, width), F32),
        in_specs=[pl.BlockSpec(memory_space=pltpu.SMEM)] + [vmem] * (1 + len(operands)),
        out_specs=vmem,
        compiler_params=pltpu.CompilerParams(vmem_limit_bytes=16 * 2**20),
        cost_estimate=pl.CostEstimate(flops=10**9, bytes_accessed=3 * 2**20, transcendentals=0),
        name="own",
    )(table, per_head, *operands)


def last_part(table, per_head, *operands):
    _, heads, rows, width = per_head.shape
    vmem = pl.BlockSpec(memory_space=pltpu.VMEM)
    wide = operands[-1]
    outs = pl.pallas_call(
        last_kernel,
        out_shape=[jax.ShapeDtypeStruct((rows * heads, width), BF16)] * 4 + [jax.ShapeDtypeStruct(wide.shape, F32)],
        in_specs=[pl.BlockSpec(memory_space=pltpu.SMEM)] + [vmem] * (1 + len(operands)),
        out_specs=[pl.BlockSpec(memory_space=pltpu.HBM)] * 4 + [vmem],
        scratch_shapes=[pltpu.VMEM((4, rows * heads, width), BF16), pltpu.SemaphoreType.DMA((4,))],
        input_output_aliases={1 + len(operands): 4},
        compiler_params=pltpu.CompilerParams(vmem_limit_bytes=16 * 2**20),
        name="last",
    )(table, per_head, *operands)
    return tuple(out.reshape(rows, heads, width) for out in outs[:4])


def load_kernel(keep_ref, received_ref, pair_ref, rest_ref, near_ref):
    core, chip = lax.axis_index("rep"), lax.axis_index("seq")
    kind = chip % 2
    pair_ref[...] = keep_ref[kind] + received_ref[kind]
    for bit in range(rest_ref.shape[0]):
        kind = (chip >> (bit + 1)) % 2
        rest_ref[bit] = keep_ref[kind, 1] + received_ref[kind, 1]
    near_ref[...] = keep_ref[core]


def loads_of(bits, keep, received):
    vmem = pl.BlockSpec(memory_space=pltpu.VMEM)
    half, width = keep.shape[1], keep.shape[2]
    shapes = ((half, width, width), (bits - 1, width, width), (half, width, width))
    return pl.pallas_call(
        load_kernel,
        out_shape=[jax.ShapeDtypeStruct(shape, F32) for shape in shapes],
        in_specs=[vmem] * 2,
        out_specs=[vmem] * 3,
        compiler_params=pltpu.CompilerParams(vmem_limit_bytes=4 * 2**20),
        cost_estimate=pl.CostEstimate(flops=10**9, bytes_accessed=3 * 2**20, transcendentals=0),
        name="loads",
    )(keep, received)


def per_device(queries, keys, values, out_grad, level_table):
    rows, heads, width = queries.shape
    half = heads // 2
    bits = lax.axis_size("seq").bit_length() - 1
    chip = lax.axis_index("seq")
    table = level_table.T
    flat = [array.reshape(rows * heads, width) for array in (queries, keys, values, out_grad)]
    send, keep, per_head = states(heads, flat)
    received = swap_cores(send)
    first = [
        jnp.where((chip >> bit) % 2 == 1, keep[1, 0] + received[1, 0], keep[0, 0] + received[0, 0])
        for bit in range(1, bits)
    ]
    first, keep, received = lax.optimization_barrier((first, keep, received))
    half_way = [
        sum(swap_chips(first[bit - 1], mask) for mask in range(1 << bit, 2 << bit, 2)) for bit in range(1, bits)
    ]
    pair_load, rest, near_load = loads_of(bits, keep, received)
    pair_load, rest, near_load, held = lax.optimization_barrier((pair_load, rest, near_load, per_head))
    group_b = [
        [swap_chips(rest[bit - 1], mask) for mask in range((2 << bit) - 1, (1 << bit) - 1, -1)] for bit in range(1, bits)
    ]
    pair = swap_chips(pair_load, 1)
    near = swap_cores(near_load)
    local_a = local_part((0,), 1000, table, held)
    half_way = jnp.stack(half_way)
    half_way, held, local_a = lax.optimization_barrier((half_way, held, local_a))
    hop = swap_chips(half_way, 1)
    local_b = local_part(tuple(range(1, heads)), 10**9, table, held, local_a)
    pair, hop, group_b, local_b = lax.optimization_barrier((pair, hop, group_b, local_b))
    pair_o = swap_cores(pair)
    group = jnp.stack([half_way + hop, jnp.stack([sum(pieces) for pieces in group_b])])
    group_o = swap_cores(group)
    wide = own_part(table, per_head, local_b, received, pair, group)
    return last_part(table, per_head, local_b, near, pair_o, group_o, wide)


def solution(mesh):
    part = P(("groups", "seq", "rep"), "head", None)
    return jax.shard_map(
        per_device,
        mesh=mesh,
        in_specs=(part, part, part, part, P(None, "head")),
        out_specs=(part, part, part, part),
        check_vma=False,
    )
```

time: 26.5 us -> 24.8 us (0.936)
  starting transfers between devices: 6.91 us -> 10.3 us
  waiting for transfers between devices: 5.14 us -> 2.14 us
  other arithmetic: 1.58 us -> 0.05 us
  local copies, waits for them, and re-layouts: 0.78 us -> 0.01 us
  Pallas kernels: 11.1 us -> 11.4 us
    ppermute x3 -> x5, starting transfers between devices: 5.76 us -> 9.23 us  [swap_chips(): lax.ppermute(block, 'seq', [(chip, chip ^ mask) for chip in range(count)])]
    ppermute x3 -> x5, waiting for transfers between devices: 4.28 us -> 0.97 us  [swap_chips(): lax.ppermute(block, 'seq', [(chip, chip ^ mask) for chip in range(count)])]
    mul x3 -> x0, other arithmetic: 1.12 us -> none  [the longest x1 0.69 us: per_device(): weights = level_table * scale[:, None]]
    unnamed x1 -> x2, local copies, waits for them, and re-layouts: 0.77 us -> 0.01 us
    ppermute x5 -> x4, waiting for transfers between devices: 0.86 us -> 1.17 us  [swap_cores(): return lax.ppermute(block, 'rep', [(0, 1), (1, 0)])]
    pallas_call x2 -> x5, Pallas kernels: 8.56 us -> 8.8 us  [the longest x2 4.81 us: local_part(): pl.pallas_call(functools.partial(local_kernel, chosen), out_shape=jax.Sha...]
    ppermute x5 -> x4, starting transfers between devices: 1.16 us -> 1.08 us  [swap_cores(): return lax.ppermute(block, 'rep', [(0, 1), (1, 0)])]
  transfers between devices with their start and end apart: 8 -> 9, of which waited for: 3 -> 2; matrix products, arithmetic and copies ran while one was open for 8% -> 0% of each run, Pallas kernels for 24% -> 25%
where the time goes in v3:
time: 24.8 us; the launch traced here: 24.6 us
  Pallas kernels  11.4 us (46%)
  starting transfers between devices  10.3 us (42%)
  waiting for transfers between devices  2.14 us (9%)
  between operations  0.75 us (3%)
    ppermute x5, starting transfers between devices, swap_chips(): lax.ppermute(block, 'seq', [(chip, chip ^ mask) for chip in range(count)])  9.23 us
    pallas_call x2, Pallas kernels, local_part(): pl.pallas_call(functools.partial(local_kernel, chosen), out_shape=jax.Sha...  4.81 us
    pallas_call x1, Pallas kernels, last_part(): pl.pallas_call(last_kernel, out_shape=[jax.ShapeDtypeStruct((rows * heads...  2.63 us
    pallas_call x1, Pallas kernels, states(): pl.pallas_call(functools.partial(state_kernel, heads), out_shape=(jax.Sha...  2.58 us
    pallas_call x1, Pallas kernels, own_part(): pl.pallas_call(own_kernel, out_shape=jax.ShapeDtypeStruct((4, rows * head...  1.32 us
    ppermute x4, waiting for transfers between devices, swap_cores(): return lax.ppermute(block, 'rep', [(0, 1), (1, 0)])  1.17 us
    ppermute x4, starting transfers between devices, swap_cores(): return lax.ppermute(block, 'rep', [(0, 1), (1, 0)])  1.08 us
    ppermute x5, waiting for transfers between devices, swap_chips(): lax.ppermute(block, 'seq', [(chip, chip ^ mask) for chip in range(count)])  0.97 us
  transfers between devices with their start and end apart: 9, of which 2 were waited for; matrix products, arithmetic and copies ran while one was open for 0% of the time, Pallas kernels for 25%

profile of v3, /device:TPU:0, one launch (start us, length us, event | category | flops | bytes accessed | tf_op | source)
XLA Modules:
  0.0 24.6 jit_solution(6208562231376507749)
XLA Ops:
  0.6 0.0 copy-start
  0.6 2.6 %states.1 = (f32[2,2,128,128]{3,2,1,0:T(8,128)S(1)}, f32[2,2,128,128]{3,2,1,0:T(8,128)S(1)}, bf16[4,4,512,128]{3,2,1,0:T(8,128)(2,1)S(1)}) custom-call(bf16[2048,128]{1,0:T(8,128)(2,1)} %bitcast.23, bf16[2048,128]{1,0:T(8,128)(2,1)} %bitcast.24, bf16[2048,128]{1,0:T(8,128)(2,1)} %bitcast.25, bf16[2048,128]{1,0:T(8,128)(2,1)} %bitcast.26), custom_call_target="tpu_custom_call" | custom-call | tf_op jit(solution)/shard_map/states/pallas_call | solution.py:81
  3.2 0.5 %collective-permute-start = (f32[2,2,128,128]{3,2,1,0:T(8,128)S(1)}, f32[2,2,128,128]{3,2,1,0:T(8,128)S(1)}, u32[]{:S(2)}, u32[]{:S(2)}) collective-permute-start(f32[2,2,128,128]{3,2,1,0:T(8,128)S(1)} %get-tuple-element.31), channel_id=1, source_target_pairs={{0,1},{1,0},{2,3},{3,2},{4,5},{5,4},{6,7},{7,6},{8,9},{9,8},{10,11... | collective-permute-start | bytes 786440 | tf_op jit(solution)/shard_map/ppermute | solution.py:20
  3.7 1.2 %collective-permute-done.received_ref = f32[2,2,128,128]{3,2,1,0:T(8,128)S(1)} collective-permute-done((f32[2,2,128,128]{3,2,1,0:T(8,128)S(1)}, f32[2,2,128,128]{3,2,1,0:T(8,128)S(1)}, u32[]{:S(2)}, u32[]{:S(2)}) %collective-permute-start) | collective-permute-done | bytes 262176 | tf_op jit(solution)/shard_map/ppermute | solution.py:20
  4.9 4.0 %collective-permute-start.2 = (f32[128,128]{1,0:T(8,128)S(1)}, f32[128,128]{1,0:T(8,128)S(1)}, u32[]{:S(2)}, u32[]{:S(2)}) collective-permute-start(f32[128,128]{1,0:T(8,128)S(1)} %fusion.1), channel_id=1, source_target_pairs={{0,8},{4,12},{8,0},{12,4},{1,9},{5,13},{9,1},{13,5},{2,10},{6,14},... | collective-permute-start | bytes 196616 | tf_op jit(solution)/shard_map/ppermute | solution.py:25
  9.0 1.6 %collective-permute-start.1 = (f32[2,128,128]{2,1,0:T(8,128)S(1)}, f32[2,128,128]{2,1,0:T(8,128)S(1)}, u32[]{:S(2)}, u32[]{:S(2)}) collective-permute-start(f32[2,128,128]{2,1,0:T(8,128)S(1)} %get-tuple-element.37), channel_id=1, source_target_pairs={{0,4},{4,0},{8,12},{12,8},{1,5},{5,1},{9,13},{13,9},{2,6},{6,2},{1... | collective-permute-start | bytes 393224 | tf_op jit(solution)/shard_map/ppermute | solution.py:25
  10.6 0.3 %collective-permute-start.5 = (f32[128,128]{1,0:T(8,128)S(1)}, f32[128,128]{1,0:T(8,128)S(1)}, u32[]{:S(2)}, u32[]{:S(2)}) collective-permute-start(f32[128,128]{1,0:T(8,128)S(1)} %bitcast.21), channel_id=1, source_target_pairs={{0,8},{4,12},{8,0},{12,4},{1,9},{5,13},{9,1},{13,5},{2,10},{6,14},... | collective-permute-start | bytes 196616 | tf_op jit(solution)/shard_map/ppermute | solution.py:25
  11.0 2.5 %collective-permute-start.4 = (f32[128,128]{1,0:T(8,128)S(1)}, f32[128,128]{1,0:T(8,128)S(1)}, u32[]{:S(2)}, u32[]{:S(2)}) collective-permute-start(f32[128,128]{1,0:T(8,128)S(1)} %bitcast.22), channel_id=1, source_target_pairs={{0,12},{4,8},{8,4},{12,0},{1,13},{5,9},{9,5},{13,1},{2,14},{6,10},... | collective-permute-start | bytes 196616 | tf_op jit(solution)/shard_map/ppermute | solution.py:25
  13.4 0.0 collective-permute-start.6
  13.4 0.0 copy-done
  13.4 1.6 %local.2.refs_0_ = f32[4,4,512,128]{3,2,1,0:T(8,128)S(1)} custom-call(f32[4,7]{1,0:T(4,128)S(1)} %bitcast.17, bf16[4,4,512,128]{3,2,1,0:T(8,128)(2,1)S(1)} %get-tuple-element.42.per_head_ref), custom_call_target="tpu_custom_call" | custom-call | flops 1000 | bytes 1 | tf_op jit(solution)/shard_map/local/pallas_call | solution.py:161
  15.0 0.0 collective-permute-done.2
  15.0 0.7 %collective-permute-start.3 = (f32[1,128,128]{2,1,0:T(8,128)S(1)}, f32[1,128,128]{2,1,0:T(8,128)S(1)}, u32[]{:S(2)}, u32[]{:S(2)}) collective-permute-start(f32[1,128,128]{2,1,0:T(8,128)S(1)} %bitcast.27), channel_id=1, source_target_pairs={{0,4},{4,0},{8,12},{12,8},{1,5},{5,1},{9,13},{13,9},{2,6},{6,2},{1... | collective-permute-start | bytes 196616 | tf_op jit(solution)/shard_map/ppermute | solution.py:25
  15.8 3.2 %local.3.local_ref = f32[4,4,512,128]{3,2,1,0:T(8,128)S(1)} custom-call(f32[4,7]{1,0:T(4,128)S(1)} %bitcast.18, bf16[4,4,512,128]{3,2,1,0:T(8,128)(2,1)S(1)} %get-tuple-element.42.per_head_ref, f32[4,4,512,128]{3,2,1,0:T(8,128)S(1)} %local.2.refs_0_), custom_call_target="tpu_custom_call", output_to_operand_aliasing={{}: (2, {})} | custom-call | flops 1000000000 | bytes 1000000 | tf_op jit(solution)/shard_map/local/pallas_call | solution.py:161
  19.0 0.0 collective-permute-done.5
  19.0 0.0 collective-permute-done.4
  19.0 0.0 collective-permute-done.1.pair_ref
  19.1 1.0 %collective-permute-done.3 = f32[1,128,128]{2,1,0:T(8,128)S(1)} collective-permute-done((f32[1,128,128]{2,1,0:T(8,128)S(1)}, f32[1,128,128]{2,1,0:T(8,128)S(1)}, u32[]{:S(2)}, u32[]{:S(2)}) %collective-permute-start.3) | collective-permute-done | bytes 65568 | tf_op jit(solution)/shard_map/ppermute | solution.py:25
  20.1 0.1 collective-permute-start.8
  20.2 0.5 %collective-permute-start.7 = (f32[2,128,128]{2,1,0:T(8,128)S(1)}, f32[2,128,128]{2,1,0:T(8,128)S(1)}, u32[]{:S(2)}, u32[]{:S(2)}) collective-permute-start(f32[2,128,128]{2,1,0:T(8,128)S(1)} %collective-permute-done.1.pair_ref), channel_id=1, source_target_pairs={{0,1},{1,0},{2,3},{3,2},{4,5},{5,4},{6,7},{7,6},{8,9},{9,8},{10,11... | collective-permute-start | bytes 393224 | tf_op jit(solution)/shard_map/ppermute | solution.py:20
  20.6 1.3 %own.1._ = f32[4,2048,128]{2,1,0:T(8,128)S(1)} custom-call(f32[4,7]{1,0:T(4,128)S(1)} %bitcast.19, bf16[4,4,512,128]{3,2,1,0:T(8,128)(2,1)S(1)} %get-tuple-element.42.per_head_ref, f32[4,4,512,128]{3,2,1,0:T(8,128)S(1)} %local.3.local_ref, f32[2,2,128,128]{3,2,1,0:T(8,128)S(1)} %collective-permute-done.received_ref, ...), custom_call_target="tpu_custom_call" | custom-call | flops 1000000000 | bytes 3145728 | tf_op jit(solution)/shard_map/own/pallas_call | solution.py:227
  22.0 0.0 collective-permute-done.6.near_ref
  22.0 0.0 collective-permute-done.8.group_ref
  22.0 0.0 collective-permute-done.7.pair_ref
  22.0 2.6 %last.1 = (bf16[2048,128]{1,0:T(8,128)(2,1)}, bf16[2048,128]{1,0:T(8,128)(2,1)}, bf16[2048,128]{1,0:T(8,128)(2,1)}, bf16[2048,128]{1,0:T(8,128)(2,1)}, f32[4,2048,128]{2,1,0:T(8,128)S(1)}) custom-call(f32[4,7]{1,0:T(4,128)S(1)} %bitcast.20, bf16[4,4,512,128]{3,2,1,0:T(8,128)(2,1)S(1)} %get-tuple-element.42.per_head_ref, ...), custom_call_target="tpu_custom_call", output_to_operand_aliasing={{4}: (6, {})} | custom-call | tf_op jit(solution)/shard_map/last/pallas_call | solution.py:242
  (5 shorter events, 0.1 us)
Async XLA Ops:
  0.6 12.8 %copy-start = (f32[7,4]{0,1:T(4,128)S(1)}, f32[7,4]{0,1:T(4,128)}, u32[]{:S(2)}) copy-start(f32[7,4]{0,1:T(4,128)} %param.9) | copy-start | bytes 340
  3.2 1.7 %collective-permute-start = (f32[2,2,128,128]{3,2,1,0:T(8,128)S(1)}, f32[2,2,128,128]{3,2,1,0:T(8,128)S(1)}, u32[]{:S(2)}, u32[]{:S(2)}) collective-permute-start(f32[2,2,128,128]{3,2,1,0:T(8,128)S(1)} %get-tuple-element.31), channel_id=1, source_target_pairs={{0,1},{1,0},{2,3},{3,2},{4,5},{5,4},{6,7},{7,6},{8,9},{9,8},{10,11... | collective-permute-start | bytes 786440 | tf_op jit(solution)/shard_map/ppermute | solution.py:20
  4.9 10.1 %collective-permute-start.2 = (f32[128,128]{1,0:T(8,128)S(1)}, f32[128,128]{1,0:T(8,128)S(1)}, u32[]{:S(2)}, u32[]{:S(2)}) collective-permute-start(f32[128,128]{1,0:T(8,128)S(1)} %fusion.1), channel_id=1, source_target_pairs={{0,8},{4,12},{8,0},{12,4},{1,9},{5,13},{9,1},{13,5},{2,10},{6,14},... | collective-permute-start | bytes 196616 | tf_op jit(solution)/shard_map/ppermute | solution.py:25
  9.0 10.1 %collective-permute-start.1 = (f32[2,128,128]{2,1,0:T(8,128)S(1)}, f32[2,128,128]{2,1,0:T(8,128)S(1)}, u32[]{:S(2)}, u32[]{:S(2)}) collective-permute-start(f32[2,128,128]{2,1,0:T(8,128)S(1)} %get-tuple-element.37), channel_id=1, source_target_pairs={{0,4},{4,0},{8,12},{12,8},{1,5},{5,1},{9,13},{13,9},{2,6},{6,2},{1... | collective-permute-start | bytes 393224 | tf_op jit(solution)/shard_map/ppermute | solution.py:25
  10.6 8.4 %collective-permute-start.5 = (f32[128,128]{1,0:T(8,128)S(1)}, f32[128,128]{1,0:T(8,128)S(1)}, u32[]{:S(2)}, u32[]{:S(2)}) collective-permute-start(f32[128,128]{1,0:T(8,128)S(1)} %bitcast.21), channel_id=1, source_target_pairs={{0,8},{4,12},{8,0},{12,4},{1,9},{5,13},{9,1},{13,5},{2,10},{6,14},... | collective-permute-start | bytes 196616 | tf_op jit(solution)/shard_map/ppermute | solution.py:25
  11.0 8.1 %collective-permute-start.4 = (f32[128,128]{1,0:T(8,128)S(1)}, f32[128,128]{1,0:T(8,128)S(1)}, u32[]{:S(2)}, u32[]{:S(2)}) collective-permute-start(f32[128,128]{1,0:T(8,128)S(1)} %bitcast.22), channel_id=1, source_target_pairs={{0,12},{4,8},{8,4},{12,0},{1,13},{5,9},{9,5},{13,1},{2,14},{6,10},... | collective-permute-start | bytes 196616 | tf_op jit(solution)/shard_map/ppermute | solution.py:25
  13.4 8.5 %collective-permute-start.6 = (f32[2,128,128]{2,1,0:T(8,128)S(1)}, f32[2,128,128]{2,1,0:T(8,128)S(1)}, u32[]{:S(2)}, u32[]{:S(2)}) collective-permute-start(f32[2,128,128]{2,1,0:T(8,128)S(1)} %get-tuple-element.45), channel_id=1, source_target_pairs={{0,1},{1,0},{2,3},{3,2},{4,5},{5,4},{6,7},{7,6},{8,9},{9,8},{10,11... | collective-permute-start | bytes 393224 | tf_op jit(solution)/shard_map/ppermute | solution.py:20
  15.0 5.0 %collective-permute-start.3 = (f32[1,128,128]{2,1,0:T(8,128)S(1)}, f32[1,128,128]{2,1,0:T(8,128)S(1)}, u32[]{:S(2)}, u32[]{:S(2)}) collective-permute-start(f32[1,128,128]{2,1,0:T(8,128)S(1)} %bitcast.27), channel_id=1, source_target_pairs={{0,4},{4,0},{8,12},{12,8},{1,5},{5,1},{9,13},{13,9},{2,6},{6,2},{1... | collective-permute-start | bytes 196616 | tf_op jit(solution)/shard_map/ppermute | solution.py:25
  20.1 1.9 %collective-permute-start.8 = (f32[2,1,128,128]{3,2,1,0:T(8,128)S(1)}, f32[2,1,128,128]{3,2,1,0:T(8,128)S(1)}, u32[]{:S(2)}, u32[]{:S(2)}) collective-permute-start(f32[2,1,128,128]{3,2,1,0:T(8,128)S(1)} %pad_maximum_fusion.group_ref), channel_id=1, source_target_pairs={{0,1},{1,0},{2,3},{3,2},{4,5},{5,4},{6,7},{7,6},{8,9},{9,8},{10,11... | collective-permute-start | bytes 393224 | tf_op jit(solution)/shard_map/ppermute | solution.py:20
  20.2 1.8 %collective-permute-start.7 = (f32[2,128,128]{2,1,0:T(8,128)S(1)}, f32[2,128,128]{2,1,0:T(8,128)S(1)}, u32[]{:S(2)}, u32[]{:S(2)}) collective-permute-start(f32[2,128,128]{2,1,0:T(8,128)S(1)} %collective-permute-done.1.pair_ref), channel_id=1, source_target_pairs={{0,1},{1,0},{2,3},{3,2},{4,5},{5,4},{6,7},{7,6},{8,9},{9,8},{10,11... | collective-permute-start | bytes 393224 | tf_op jit(solution)/shard_map/ppermute | solution.py:20

commit v4 on v3

--- a/solution.py
+++ b/solution.py
@@ -27,6 +27,10 @@
 
 def level_scale(level):
     return float(np.float32(1.0) / np.sqrt(np.float32(BLOCK * 2 ** max(level - 1, 0))))
+
+
+def weight_of(table_ref, head, level):
+    return table_ref[pl.ds(head, 1), level : level + 1] * level_scale(level)
 
 
 def dot_tn(left, right):
@@ -107,7 +111,7 @@
 def local_head(head, rows, table_ref, per_head_ref, out_ref):
     tiles = rows // TILE
     inner = (TILE // BLOCK).bit_length()
-    weight = [table_ref[head, level] * level_scale(level) for level in range(inner + tiles.bit_length() - 1)]
+    weight = [weight_of(table_ref, head, level) for level in range(inner + tiles.bit_length() - 1)]
     row = lax.broadcasted_iota(jnp.int32, (TILE, TILE), 0)
     column = lax.broadcasted_iota(jnp.int32, (TILE, TILE), 1)
     apart = jnp.bitwise_xor(row // BLOCK, column // BLOCK)
@@ -161,7 +165,7 @@
     return pl.pallas_call(
         functools.partial(local_kernel, chosen),
         out_shape=jax.ShapeDtypeStruct(per_head.shape, F32),
-        in_specs=[pl.BlockSpec(memory_space=pltpu.SMEM)] + [vmem] * (1 + len(earlier)),
+        in_specs=[pl.BlockSpec(memory_space=pltpu.VMEM)] + [vmem] * (1 + len(earlier)),
         out_specs=vmem,
         input_output_aliases={2: 0} if earlier else {},
         compiler_params=pltpu.CompilerParams(vmem_limit_bytes=16 * 2**20),
@@ -176,7 +180,7 @@
     terms += [((chip >> bit) % 2 == 1, group) for bit, group in enumerate(groups, 1)]
     keys_far = queries_far = 0.0
     for level, (later, piece) in enumerate(terms, (rows // BLOCK).bit_length()):
-        weight = table_ref[head, level] * level_scale(level)
+        weight = weight_of(table_ref, head, level)
         keys_far += jnp.where(later, weight, 0.0) * piece
         queries_far += jnp.where(later, 0.0, weight) * piece
     return [jnp.concatenate(split(state), 0) for state in (keys_far, keys_far.T, queries_far.T, queries_far)]
@@ -227,7 +231,7 @@
     return pl.pallas_call(
         own_kernel,
         out_shape=jax.ShapeDtypeStruct((4, rows * heads, width), F32),
-        in_specs=[pl.BlockSpec(memory_space=pltpu.SMEM)] + [vmem] * (1 + len(operands)),
+        in_specs=[pl.BlockSpec(memory_space=pltpu.VMEM)] + [vmem] * (1 + len(operands)),
         out_specs=vmem,
         compiler_params=pltpu.CompilerParams(vmem_limit_bytes=16 * 2**20),
         cost_estimate=pl.CostEstimate(flops=10**9, bytes_accessed=3 * 2**20, transcendentals=0),
@@ -242,7 +246,7 @@
     outs = pl.pallas_call(
         last_kernel,
         out_shape=[jax.ShapeDtypeStruct((rows * heads, width), BF16)] * 4 + [jax.ShapeDtypeStruct(wide.shape, F32)],
-        in_specs=[pl.BlockSpec(memory_space=pltpu.SMEM)] + [vmem] * (1 + len(operands)),
+        in_specs=[pl.BlockSpec(memory_space=pltpu.VMEM)] + [vmem] * (1 + len(operands)),
         out_specs=[pl.BlockSpec(memory_space=pltpu.HBM)] * 4 + [vmem],
         scratch_shapes=[pltpu.VMEM((4, rows * heads, width), BF16), pltpu.SemaphoreType.DMA((4,))],
         input_output_aliases={1 + len(operands): 4},

time: 24.8 us -> 24.1 us (0.972)
  Pallas kernels: 11.4 us -> 9.54 us
  waiting for transfers between devices: 2.14 us -> 3.34 us
    ppermute x5, waiting for transfers between devices: 0.97 us -> 2.04 us  [swap_chips(): lax.ppermute(block, 'seq', [(chip, chip ^ mask) for chip in range(count)])]
    pallas_call x2, Pallas kernels: 4.81 us -> 3.76 us  [local_part(): pl.pallas_call(functools.partial(local_kernel, chosen), out_shape=jax.Sha...]
    pallas_call x1, Pallas kernels: 1.32 us -> 0.86 us  [own_part(): pl.pallas_call(own_kernel, out_shape=jax.ShapeDtypeStruct((4, rows * head...]
    pallas_call x1, Pallas kernels: 2.63 us -> 2.31 us  [last_part(): pl.pallas_call(last_kernel, out_shape=[jax.ShapeDtypeStruct((rows * heads...]
  transfers between devices with their start and end apart: 9 -> 9, of which waited for: 2 -> 5; matrix products, arithmetic and copies ran while one was open for 0% -> 0% of each run, Pallas kernels for 25% -> 19%
where the time goes in v4:
time: 24.1 us; the launch traced here: 24 us
  starting transfers between devices  10.3 us (43%)
  Pallas kernels  9.54 us (40%)
  waiting for transfers between devices  3.34 us (14%)
  between operations  0.73 us (3%)
    ppermute x5, starting transfers between devices, swap_chips(): lax.ppermute(block, 'seq', [(chip, chip ^ mask) for chip in range(count)])  9.23 us
    pallas_call x2, Pallas kernels, local_part(): pl.pallas_call(functools.partial(local_kernel, chosen), out_shape=jax.Sha...  3.76 us
    pallas_call x1, Pallas kernels, states(): pl.pallas_call(functools.partial(state_kernel, heads), out_shape=(jax.Sha...  2.58 us
    pallas_call x1, Pallas kernels, last_part(): pl.pallas_call(last_kernel, out_shape=[jax.ShapeDtypeStruct((rows * heads...  2.31 us
    ppermute x5, waiting for transfers between devices, swap_chips(): lax.ppermute(block, 'seq', [(chip, chip ^ mask) for chip in range(count)])  2.04 us
    ppermute x4, waiting for transfers between devices, swap_cores(): return lax.ppermute(block, 'rep', [(0, 1), (1, 0)])  1.3 us
    ppermute x4, starting transfers between devices, swap_cores(): return lax.ppermute(block, 'rep', [(0, 1), (1, 0)])  1.08 us
    pallas_call x1, Pallas kernels, own_part(): pl.pallas_call(own_kernel, out_shape=jax.ShapeDtypeStruct((4, rows * head...  0.86 us
  transfers between devices with their start and end apart: 9, of which 5 were waited for; matrix products, arithmetic and copies ran while one was open for 0% of the time, Pallas kernels for 19%

profile of v4, /device:TPU:0, one launch (start us, length us, event | category | flops | bytes accessed | tf_op | source)
XLA Modules:
  0.0 24.0 jit_solution(6769213370413671383)
XLA Ops:
  0.6 0.0 copy-start
  0.6 2.6 %states.1 = (f32[2,2,128,128]{3,2,1,0:T(8,128)S(1)}, f32[2,2,128,128]{3,2,1,0:T(8,128)S(1)}, bf16[4,4,512,128]{3,2,1,0:T(8,128)(2,1)S(1)}) custom-call(bf16[2048,128]{1,0:T(8,128)(2,1)} %bitcast.23, bf16[2048,128]{1,0:T(8,128)(2,1)} %bitcast.24, bf16[2048,128]{1,0:T(8,128)(2,1)} %bitcast.25, bf16[2048,128]{1,0:T(8,128)(2,1)} %bitcast.26), custom_call_target="tpu_custom_call" | custom-call | tf_op jit(solution)/shard_map/states/pallas_call | solution.py:85
  3.2 0.5 %collective-permute-start = (f32[2,2,128,128]{3,2,1,0:T(8,128)S(1)}, f32[2,2,128,128]{3,2,1,0:T(8,128)S(1)}, u32[]{:S(2)}, u32[]{:S(2)}) collective-permute-start(f32[2,2,128,128]{3,2,1,0:T(8,128)S(1)} %get-tuple-element.31), channel_id=1, source_target_pairs={{0,1},{1,0},{2,3},{3,2},{4,5},{5,4},{6,7},{7,6},{8,9},{9,8},{10,11... | collective-permute-start | bytes 786440 | tf_op jit(solution)/shard_map/ppermute | solution.py:20
  3.7 1.2 %collective-permute-done.received_ref = f32[2,2,128,128]{3,2,1,0:T(8,128)S(1)} collective-permute-done((f32[2,2,128,128]{3,2,1,0:T(8,128)S(1)}, f32[2,2,128,128]{3,2,1,0:T(8,128)S(1)}, u32[]{:S(2)}, u32[]{:S(2)}) %collective-permute-start) | collective-permute-done | bytes 262176 | tf_op jit(solution)/shard_map/ppermute | solution.py:20
  4.9 4.0 %collective-permute-start.2 = (f32[128,128]{1,0:T(8,128)S(1)}, f32[128,128]{1,0:T(8,128)S(1)}, u32[]{:S(2)}, u32[]{:S(2)}) collective-permute-start(f32[128,128]{1,0:T(8,128)S(1)} %fusion.1), channel_id=1, source_target_pairs={{0,8},{4,12},{8,0},{12,4},{1,9},{5,13},{9,1},{13,5},{2,10},{6,14},... | collective-permute-start | bytes 196616 | tf_op jit(solution)/shard_map/ppermute | solution.py:25
  9.0 1.6 %collective-permute-start.1 = (f32[2,128,128]{2,1,0:T(8,128)S(1)}, f32[2,128,128]{2,1,0:T(8,128)S(1)}, u32[]{:S(2)}, u32[]{:S(2)}) collective-permute-start(f32[2,128,128]{2,1,0:T(8,128)S(1)} %get-tuple-element.37), channel_id=1, source_target_pairs={{0,4},{4,0},{8,12},{12,8},{1,5},{5,1},{9,13},{13,9},{2,6},{6,2},{1... | collective-permute-start | bytes 393224 | tf_op jit(solution)/shard_map/ppermute | solution.py:25
  10.6 0.3 %collective-permute-start.5 = (f32[128,128]{1,0:T(8,128)S(1)}, f32[128,128]{1,0:T(8,128)S(1)}, u32[]{:S(2)}, u32[]{:S(2)}) collective-permute-start(f32[128,128]{1,0:T(8,128)S(1)} %bitcast.21), channel_id=1, source_target_pairs={{0,8},{4,12},{8,0},{12,4},{1,9},{5,13},{9,1},{13,5},{2,10},{6,14},... | collective-permute-start | bytes 196616 | tf_op jit(solution)/shard_map/ppermute | solution.py:25
  11.0 2.5 %collective-permute-start.4 = (f32[128,128]{1,0:T(8,128)S(1)}, f32[128,128]{1,0:T(8,128)S(1)}, u32[]{:S(2)}, u32[]{:S(2)}) collective-permute-start(f32[128,128]{1,0:T(8,128)S(1)} %bitcast.22), channel_id=1, source_target_pairs={{0,12},{4,8},{8,4},{12,0},{1,13},{5,9},{9,5},{13,1},{2,14},{6,10},... | collective-permute-start | bytes 196616 | tf_op jit(solution)/shard_map/ppermute | solution.py:25
  13.4 0.0 collective-permute-start.6
  13.4 0.0 copy-done
  13.4 1.0 %local.2.refs_0_ = f32[4,4,512,128]{3,2,1,0:T(8,128)S(1)} custom-call(f32[4,7]{1,0:T(4,128)S(1)} %bitcast.17, bf16[4,4,512,128]{3,2,1,0:T(8,128)(2,1)S(1)} %get-tuple-element.42.per_head_ref), custom_call_target="tpu_custom_call" | custom-call | flops 1000 | bytes 1 | tf_op jit(solution)/shard_map/local/pallas_call | solution.py:165
  14.5 0.0 collective-permute-done.2
  14.5 0.7 %collective-permute-start.3 = (f32[1,128,128]{2,1,0:T(8,128)S(1)}, f32[1,128,128]{2,1,0:T(8,128)S(1)}, u32[]{:S(2)}, u32[]{:S(2)}) collective-permute-start(f32[1,128,128]{2,1,0:T(8,128)S(1)} %bitcast.27), channel_id=1, source_target_pairs={{0,4},{4,0},{8,12},{12,8},{1,5},{5,1},{9,13},{13,9},{2,6},{6,2},{1... | collective-permute-start | bytes 196616 | tf_op jit(solution)/shard_map/ppermute | solution.py:25
  15.2 2.7 %local.3.local_ref = f32[4,4,512,128]{3,2,1,0:T(8,128)S(1)} custom-call(f32[4,7]{1,0:T(4,128)S(1)} %bitcast.18, bf16[4,4,512,128]{3,2,1,0:T(8,128)(2,1)S(1)} %get-tuple-element.42.per_head_ref, f32[4,4,512,128]{3,2,1,0:T(8,128)S(1)} %local.2.refs_0_), custom_call_target="tpu_custom_call", output_to_operand_aliasing={{}: (2, {})} | custom-call | flops 1000000000 | bytes 1000000 | tf_op jit(solution)/shard_map/local/pallas_call | solution.py:165
  18.0 0.5 %collective-permute-done.5 = f32[128,128]{1,0:T(8,128)S(1)} collective-permute-done((f32[128,128]{1,0:T(8,128)S(1)}, f32[128,128]{1,0:T(8,128)S(1)}, u32[]{:S(2)}, u32[]{:S(2)}) %collective-permute-start.5) | collective-permute-done | bytes 65568 | tf_op jit(solution)/shard_map/ppermute | solution.py:25
  18.5 0.3 %collective-permute-done.4 = f32[128,128]{1,0:T(8,128)S(1)} collective-permute-done((f32[128,128]{1,0:T(8,128)S(1)}, f32[128,128]{1,0:T(8,128)S(1)}, u32[]{:S(2)}, u32[]{:S(2)}) %collective-permute-start.4) | collective-permute-done | bytes 65568 | tf_op jit(solution)/shard_map/ppermute | solution.py:25
  18.8 0.0 collective-permute-done.1.pair_ref
  18.8 1.2 %collective-permute-done.3 = f32[1,128,128]{2,1,0:T(8,128)S(1)} collective-permute-done((f32[1,128,128]{2,1,0:T(8,128)S(1)}, f32[1,128,128]{2,1,0:T(8,128)S(1)}, u32[]{:S(2)}, u32[]{:S(2)}) %collective-permute-start.3) | collective-permute-done | bytes 65568 | tf_op jit(solution)/shard_map/ppermute | solution.py:25
  20.1 0.1 collective-permute-start.8
  20.2 0.4 %collective-permute-start.7 = (f32[2,128,128]{2,1,0:T(8,128)S(1)}, f32[2,128,128]{2,1,0:T(8,128)S(1)}, u32[]{:S(2)}, u32[]{:S(2)}) collective-permute-start(f32[2,128,128]{2,1,0:T(8,128)S(1)} %collective-permute-done.1.pair_ref), channel_id=1, source_target_pairs={{0,1},{1,0},{2,3},{3,2},{4,5},{5,4},{6,7},{7,6},{8,9},{9,8},{10,11... | collective-permute-start | bytes 393224 | tf_op jit(solution)/shard_map/ppermute | solution.py:20
  20.6 0.9 %own.1._ = f32[4,2048,128]{2,1,0:T(8,128)S(1)} custom-call(f32[4,7]{1,0:T(4,128)S(1)} %bitcast.19, bf16[4,4,512,128]{3,2,1,0:T(8,128)(2,1)S(1)} %get-tuple-element.42.per_head_ref, f32[4,4,512,128]{3,2,1,0:T(8,128)S(1)} %local.3.local_ref, f32[2,2,128,128]{3,2,1,0:T(8,128)S(1)} %collective-permute-done.received_ref, ...), custom_call_target="tpu_custom_call" | custom-call | flops 1000000000 | bytes 3145728 | tf_op jit(solution)/shard_map/own/pallas_call | solution.py:231
  21.5 0.0 collective-permute-done.6.near_ref
  21.5 0.0 collective-permute-done.8.group_ref
  21.5 0.1 collective-permute-done.7.pair_ref
  21.7 2.3 %last.1 = (bf16[2048,128]{1,0:T(8,128)(2,1)}, bf16[2048,128]{1,0:T(8,128)(2,1)}, bf16[2048,128]{1,0:T(8,128)(2,1)}, bf16[2048,128]{1,0:T(8,128)(2,1)}, f32[4,2048,128]{2,1,0:T(8,128)S(1)}) custom-call(f32[4,7]{1,0:T(4,128)S(1)} %bitcast.20, bf16[4,4,512,128]{3,2,1,0:T(8,128)(2,1)S(1)} %get-tuple-element.42.per_head_ref, ...), custom_call_target="tpu_custom_call", output_to_operand_aliasing={{4}: (6, {})} | custom-call | tf_op jit(solution)/shard_map/last/pallas_call | solution.py:246
  (5 shorter events, 0.1 us)
Async XLA Ops:
  0.6 12.8 %copy-start = (f32[7,4]{0,1:T(4,128)S(1)}, f32[7,4]{0,1:T(4,128)}, u32[]{:S(2)}) copy-start(f32[7,4]{0,1:T(4,128)} %param.9) | copy-start | bytes 340
  3.2 1.7 %collective-permute-start = (f32[2,2,128,128]{3,2,1,0:T(8,128)S(1)}, f32[2,2,128,128]{3,2,1,0:T(8,128)S(1)}, u32[]{:S(2)}, u32[]{:S(2)}) collective-permute-start(f32[2,2,128,128]{3,2,1,0:T(8,128)S(1)} %get-tuple-element.31), channel_id=1, source_target_pairs={{0,1},{1,0},{2,3},{3,2},{4,5},{5,4},{6,7},{7,6},{8,9},{9,8},{10,11... | collective-permute-start | bytes 786440 | tf_op jit(solution)/shard_map/ppermute | solution.py:20
  4.9 9.6 %collective-permute-start.2 = (f32[128,128]{1,0:T(8,128)S(1)}, f32[128,128]{1,0:T(8,128)S(1)}, u32[]{:S(2)}, u32[]{:S(2)}) collective-permute-start(f32[128,128]{1,0:T(8,128)S(1)} %fusion.1), channel_id=1, source_target_pairs={{0,8},{4,12},{8,0},{12,4},{1,9},{5,13},{9,1},{13,5},{2,10},{6,14},... | collective-permute-start | bytes 196616 | tf_op jit(solution)/shard_map/ppermute | solution.py:25
  9.0 9.8 %collective-permute-start.1 = (f32[2,128,128]{2,1,0:T(8,128)S(1)}, f32[2,128,128]{2,1,0:T(8,128)S(1)}, u32[]{:S(2)}, u32[]{:S(2)}) collective-permute-start(f32[2,128,128]{2,1,0:T(8,128)S(1)} %get-tuple-element.37), channel_id=1, source_target_pairs={{0,4},{4,0},{8,12},{12,8},{1,5},{5,1},{9,13},{13,9},{2,6},{6,2},{1... | collective-permute-start | bytes 393224 | tf_op jit(solution)/shard_map/ppermute | solution.py:25
  10.6 7.9 %collective-permute-start.5 = (f32[128,128]{1,0:T(8,128)S(1)}, f32[128,128]{1,0:T(8,128)S(1)}, u32[]{:S(2)}, u32[]{:S(2)}) collective-permute-start(f32[128,128]{1,0:T(8,128)S(1)} %bitcast.21), channel_id=1, source_target_pairs={{0,8},{4,12},{8,0},{12,4},{1,9},{5,13},{9,1},{13,5},{2,10},{6,14},... | collective-permute-start | bytes 196616 | tf_op jit(solution)/shard_map/ppermute | solution.py:25
  11.0 7.8 %collective-permute-start.4 = (f32[128,128]{1,0:T(8,128)S(1)}, f32[128,128]{1,0:T(8,128)S(1)}, u32[]{:S(2)}, u32[]{:S(2)}) collective-permute-start(f32[128,128]{1,0:T(8,128)S(1)} %bitcast.22), channel_id=1, source_target_pairs={{0,12},{4,8},{8,4},{12,0},{1,13},{5,9},{9,5},{13,1},{2,14},{6,10},... | collective-permute-start | bytes 196616 | tf_op jit(solution)/shard_map/ppermute | solution.py:25
  13.4 8.1 %collective-permute-start.6 = (f32[2,128,128]{2,1,0:T(8,128)S(1)}, f32[2,128,128]{2,1,0:T(8,128)S(1)}, u32[]{:S(2)}, u32[]{:S(2)}) collective-permute-start(f32[2,128,128]{2,1,0:T(8,128)S(1)} %get-tuple-element.45), channel_id=1, source_target_pairs={{0,1},{1,0},{2,3},{3,2},{4,5},{5,4},{6,7},{7,6},{8,9},{9,8},{10,11... | collective-permute-start | bytes 393224 | tf_op jit(solution)/shard_map/ppermute | solution.py:20
  14.5 5.5 %collective-permute-start.3 = (f32[1,128,128]{2,1,0:T(8,128)S(1)}, f32[1,128,128]{2,1,0:T(8,128)S(1)}, u32[]{:S(2)}, u32[]{:S(2)}) collective-permute-start(f32[1,128,128]{2,1,0:T(8,128)S(1)} %bitcast.27), channel_id=1, source_target_pairs={{0,4},{4,0},{8,12},{12,8},{1,5},{5,1},{9,13},{13,9},{2,6},{6,2},{1... | collective-permute-start | bytes 196616 | tf_op jit(solution)/shard_map/ppermute | solution.py:25
  20.1 1.5 %collective-permute-start.8 = (f32[2,1,128,128]{3,2,1,0:T(8,128)S(1)}, f32[2,1,128,128]{3,2,1,0:T(8,128)S(1)}, u32[]{:S(2)}, u32[]{:S(2)}) collective-permute-start(f32[2,1,128,128]{3,2,1,0:T(8,128)S(1)} %pad_maximum_fusion.group_ref), channel_id=1, source_target_pairs={{0,1},{1,0},{2,3},{3,2},{4,5},{5,4},{6,7},{7,6},{8,9},{9,8},{10,11... | collective-permute-start | bytes 393224 | tf_op jit(solution)/shard_map/ppermute | solution.py:20
  20.2 1.5 %collective-permute-start.7 = (f32[2,128,128]{2,1,0:T(8,128)S(1)}, f32[2,128,128]{2,1,0:T(8,128)S(1)}, u32[]{:S(2)}, u32[]{:S(2)}) collective-permute-start(f32[2,128,128]{2,1,0:T(8,128)S(1)} %collective-permute-done.1.pair_ref), channel_id=1, source_target_pairs={{0,1},{1,0},{2,3},{3,2},{4,5},{5,4},{6,7},{7,6},{8,9},{9,8},{10,11... | collective-permute-start | bytes 393224 | tf_op jit(solution)/shard_map/ppermute | solution.py:20

commit v5 on v4

--- a/solution.py
+++ b/solution.py
@@ -50,7 +50,9 @@
     return high, (value - high.astype(F32)).astype(BF16)
 
 
-def state_kernel(heads, q_ref, k_ref, v_ref, g_ref, send_ref, keep_ref, per_head_ref, narrow, wide, arrived):
+def state_kernel(
+    heads, q_ref, k_ref, v_ref, g_ref, levels_ref, send_ref, keep_ref, per_head_ref, table_ref, narrow, wide, arrived, listed
+):
     rows = q_ref.shape[0] // heads
     half = heads // 2
     core = lax.axis_index("rep")
@@ -66,6 +68,8 @@
         for which in pair:
             for chunk in range(CHUNKS):
                 fetch(which, chunk).start()
+    table = pltpu.make_async_copy(levels_ref, table_ref, listed)
+    table.start()
     for kind, pair in enumerate(pairs):
         for which in pair:
             for chunk in range(CHUNKS):
@@ -77,9 +81,11 @@
             for owner, out_ref in ((1 - core, send_ref), (core, keep_ref)):
                 head = owner * half + place
                 out_ref[kind, place] = dot_tn(per_head_ref[pair[0], head], per_head_ref[pair[1], head])
-
-
-def states(heads, flat):
+    table.wait()
+
+
+def states(flat, table):
+    heads = table.shape[0]
     rows, width = flat[0].shape[0] // heads, flat[0].shape[1]
     half = (2, heads // 2, width, width)
     return pl.pallas_call(
@@ -88,17 +94,19 @@
             jax.ShapeDtypeStruct(half, F32),
             jax.ShapeDtypeStruct(half, F32),
             jax.ShapeDtypeStruct((4, heads, rows, width), BF16),
+            jax.ShapeDtypeStruct(table.shape, F32),
         ),
-        in_specs=[pl.BlockSpec(memory_space=pltpu.HBM)] * 4,
-        out_specs=[pl.BlockSpec(memory_space=pltpu.VMEM)] * 3,
+        in_specs=[pl.BlockSpec(memory_space=pltpu.HBM)] * 5,
+        out_specs=[pl.BlockSpec(memory_space=pltpu.VMEM)] * 4,
         scratch_shapes=[
             pltpu.VMEM((4, rows * heads, width), BF16),
             pltpu.VMEM((4, rows * heads, width), F32),
             pltpu.SemaphoreType.DMA((4, CHUNKS)),
+            pltpu.SemaphoreType.DMA,
         ],
         compiler_params=pltpu.CompilerParams(vmem_limit_bytes=24 * 2**20),
         name="states",
-    )(*[pltpu.with_memory_space_constraint(array, pltpu.HBM) for array in flat])
+    )(*[pltpu.with_memory_space_constraint(array, pltpu.HBM) for array in (*flat, table)])
 
 
 def local_kernel(chosen, table_ref, per_head_ref, *refs):
@@ -286,10 +294,11 @@
     half = heads // 2
     bits = lax.axis_size("seq").bit_length() - 1
     chip = lax.axis_index("seq")
-    table = level_table.T
     flat = [array.reshape(rows * heads, width) for array in (queries, keys, values, out_grad)]
-    send, keep, per_head = states(heads, flat)
+    send, keep, per_head, table = states(flat, level_table.T)
     received = swap_cores(send)
+    local_a = local_part((0,), 10**9, table, per_head)
+    received, per_head, local_a = lax.optimization_barrier((received, per_head, local_a))
     first = [
         jnp.where((chip >> bit) % 2 == 1, keep[1, 0] + received[1, 0], keep[0, 0] + received[0, 0])
         for bit in range(1, bits)
@@ -305,7 +314,6 @@
     ]
     pair = swap_chips(pair_load, 1)
     near = swap_cores(near_load)
-    local_a = local_part((0,), 1000, table, held)
     half_way = jnp.stack(half_way)
     half_way, held, local_a = lax.optimization_barrier((half_way, held, local_a))
     hop = swap_chips(half_way, 1)

time: 24.1 us -> 23.6 us (0.979)
  waiting for transfers between devices: 3.34 us -> 2.89 us
    ppermute x4, waiting for transfers between devices: 1.3 us -> 0.25 us  [swap_cores(): return lax.ppermute(block, 'rep', [(0, 1), (1, 0)])]
    ppermute x5, waiting for transfers between devices: 2.04 us -> 2.64 us  [swap_chips(): lax.ppermute(block, 'seq', [(chip, chip ^ mask) for chip in range(count)])]
  transfers between devices with their start and end apart: 9 -> 9, of which waited for: 5 -> 5; matrix products, arithmetic and copies ran while one was open for 0% -> 0% of each run, Pallas kernels for 19% -> 20%
where the time goes in v5:
time: 23.6 us; the launch traced here: 23.4 us
  starting transfers between devices  10.2 us (43%)
  Pallas kernels  9.55 us (40%)
  waiting for transfers between devices  2.89 us (12%)
  between operations  0.72 us (3%)
    ppermute x5, starting transfers between devices, swap_chips(): lax.ppermute(block, 'seq', [(chip, chip ^ mask) for chip in range(count)])  9.16 us
    pallas_call x2, Pallas kernels, local_part(): pl.pallas_call(functools.partial(local_kernel, chosen), out_shape=jax.Sha...  3.76 us
    ppermute x5, waiting for transfers between devices, swap_chips(): lax.ppermute(block, 'seq', [(chip, chip ^ mask) for chip in range(count)])  2.64 us
    pallas_call x1, Pallas kernels, states(): pl.pallas_call(functools.partial(state_kernel, heads), out_shape=(jax.Sha...  2.58 us
    pallas_call x1, Pallas kernels, last_part(): pl.pallas_call(last_kernel, out_shape=[jax.ShapeDtypeStruct((rows * heads...  2.3 us
    ppermute x4, starting transfers between devices, swap_cores(): return lax.ppermute(block, 'rep', [(0, 1), (1, 0)])  1.07 us
    pallas_call x1, Pallas kernels, own_part(): pl.pallas_call(own_kernel, out_shape=jax.ShapeDtypeStruct((4, rows * head...  0.87 us
  transfers between devices with their start and end apart: 9, of which 5 were waited for; matrix products, arithmetic and copies ran while one was open for 0% of the time, Pallas kernels for 20%

profile of v5, /device:TPU:0, one launch (start us, length us, event | category | flops | bytes accessed | tf_op | source)
XLA Modules:
  0.0 23.4 jit_solution(3401025432248215668)
XLA Ops:
  0.6 2.6 %states.1 = (f32[2,2,128,128]{3,2,1,0:T(8,128)S(1)}, f32[2,2,128,128]{3,2,1,0:T(8,128)S(1)}, bf16[4,4,512,128]{3,2,1,0:T(8,128)(2,1)S(1)}, f32[4,7]{1,0:T(4,128)S(1)}) custom-call(bf16[2048,128]{1,0:T(8,128)(2,1)} %bitcast.19, bf16[2048,128]{1,0:T(8,128)(2,1)} %bitcast.20, bf16[2048,128]{1,0:T(8,128)(2,1)} %bitcast.21, bf16[2048,128]{1,0:T(8,128)(2,1)} %bitcast.22, ...), custom_call_target="tpu_custom_call" | custom-call | tf_op jit(solution)/shard_map/states/pallas_call | solution.py:91
  3.2 0.5 %collective-permute-start = (f32[2,2,128,128]{3,2,1,0:T(8,128)S(1)}, f32[2,2,128,128]{3,2,1,0:T(8,128)S(1)}, u32[]{:S(2)}, u32[]{:S(2)}) collective-permute-start(f32[2,2,128,128]{3,2,1,0:T(8,128)S(1)} %get-tuple-element.34), channel_id=1, source_target_pairs={{0,1},{1,0},{2,3},{3,2},{4,5},{5,4},{6,7},{7,6},{8,9},{9,8},{10,11... | collective-permute-start | bytes 786440 | tf_op jit(solution)/shard_map/ppermute | solution.py:20
  3.7 1.0 %local.2.refs_0_ = f32[4,4,512,128]{3,2,1,0:T(8,128)S(1)} custom-call(f32[4,7]{1,0:T(4,128)S(1)} %get-tuple-element.33.table_ref, bf16[4,4,512,128]{3,2,1,0:T(8,128)(2,1)S(1)} %get-tuple-element.50.per_head_ref), custom_call_target="tpu_custom_call" | custom-call | flops 1000000000 | bytes 1000000 | tf_op jit(solution)/shard_map/local/pallas_call | solution.py:173
  4.8 0.1 collective-permute-done.received_ref
  4.9 4.0 %collective-permute-start.2 = (f32[128,128]{1,0:T(8,128)S(1)}, f32[128,128]{1,0:T(8,128)S(1)}, u32[]{:S(2)}, u32[]{:S(2)}) collective-permute-start(f32[128,128]{1,0:T(8,128)S(1)} %select_bitcast_fusion), channel_id=1, source_target_pairs={{0,8},{4,12},{8,0},{12,4},{1,9},{5,13},{9,1},{13,5},{2,10},{6,14},... | collective-permute-start | bytes 196616 | tf_op jit(solution)/shard_map/ppermute | solution.py:25
  9.0 1.6 %collective-permute-start.1 = (f32[2,128,128]{2,1,0:T(8,128)S(1)}, f32[2,128,128]{2,1,0:T(8,128)S(1)}, u32[]{:S(2)}, u32[]{:S(2)}) collective-permute-start(f32[2,128,128]{2,1,0:T(8,128)S(1)} %get-tuple-element.44), channel_id=1, source_target_pairs={{0,4},{4,0},{8,12},{12,8},{1,5},{5,1},{9,13},{13,9},{2,6},{6,2},{1... | collective-permute-start | bytes 393224 | tf_op jit(solution)/shard_map/ppermute | solution.py:25
  10.6 0.3 %collective-permute-start.5 = (f32[128,128]{1,0:T(8,128)S(1)}, f32[128,128]{1,0:T(8,128)S(1)}, u32[]{:S(2)}, u32[]{:S(2)}) collective-permute-start(f32[128,128]{1,0:T(8,128)S(1)} %bitcast.17), channel_id=1, source_target_pairs={{0,8},{4,12},{8,0},{12,4},{1,9},{5,13},{9,1},{13,5},{2,10},{6,14},... | collective-permute-start | bytes 196616 | tf_op jit(solution)/shard_map/ppermute | solution.py:25
  11.0 2.5 %collective-permute-start.4 = (f32[128,128]{1,0:T(8,128)S(1)}, f32[128,128]{1,0:T(8,128)S(1)}, u32[]{:S(2)}, u32[]{:S(2)}) collective-permute-start(f32[128,128]{1,0:T(8,128)S(1)} %bitcast.18), channel_id=1, source_target_pairs={{0,12},{4,8},{8,4},{12,0},{1,13},{5,9},{9,5},{13,1},{2,14},{6,10},... | collective-permute-start | bytes 196616 | tf_op jit(solution)/shard_map/ppermute | solution.py:25
  13.4 0.0 collective-permute-start.6
  13.4 0.0 collective-permute-done.2
  13.4 0.7 %collective-permute-start.3 = (f32[1,128,128]{2,1,0:T(8,128)S(1)}, f32[1,128,128]{2,1,0:T(8,128)S(1)}, u32[]{:S(2)}, u32[]{:S(2)}) collective-permute-start(f32[1,128,128]{2,1,0:T(8,128)S(1)} %bitcast.23), channel_id=1, source_target_pairs={{0,4},{4,0},{8,12},{12,8},{1,5},{5,1},{9,13},{13,9},{2,6},{6,2},{1... | collective-permute-start | bytes 196616 | tf_op jit(solution)/shard_map/ppermute | solution.py:25
  14.1 2.7 %local.3.local_ref = f32[4,4,512,128]{3,2,1,0:T(8,128)S(1)} custom-call(f32[4,7]{1,0:T(4,128)S(1)} %get-tuple-element.33.table_ref, bf16[4,4,512,128]{3,2,1,0:T(8,128)(2,1)S(1)} %get-tuple-element.50.per_head_ref, f32[4,4,512,128]{3,2,1,0:T(8,128)S(1)} %local.2.refs_0_), custom_call_target="tpu_custom_call", output_to_operand_aliasing={{}: (2, {})} | custom-call | flops 1000000000 | bytes 1000000 | tf_op jit(solution)/shard_map/local/pallas_call | solution.py:173
  16.8 1.6 %collective-permute-done.5 = f32[128,128]{1,0:T(8,128)S(1)} collective-permute-done((f32[128,128]{1,0:T(8,128)S(1)}, f32[128,128]{1,0:T(8,128)S(1)}, u32[]{:S(2)}, u32[]{:S(2)}) %collective-permute-start.5) | collective-permute-done | bytes 65568 | tf_op jit(solution)/shard_map/ppermute | solution.py:25
  18.4 0.4 %collective-permute-done.4 = f32[128,128]{1,0:T(8,128)S(1)} collective-permute-done((f32[128,128]{1,0:T(8,128)S(1)}, f32[128,128]{1,0:T(8,128)S(1)}, u32[]{:S(2)}, u32[]{:S(2)}) %collective-permute-start.4) | collective-permute-done | bytes 65568 | tf_op jit(solution)/shard_map/ppermute | solution.py:25
  18.8 0.0 collective-permute-done.1.pair_ref
  18.8 0.7 %collective-permute-done.3 = f32[1,128,128]{2,1,0:T(8,128)S(1)} collective-permute-done((f32[1,128,128]{2,1,0:T(8,128)S(1)}, f32[1,128,128]{2,1,0:T(8,128)S(1)}, u32[]{:S(2)}, u32[]{:S(2)}) %collective-permute-start.3) | collective-permute-done | bytes 65568 | tf_op jit(solution)/shard_map/ppermute | solution.py:25
  19.5 0.1 collective-permute-start.8
  19.6 0.5 %collective-permute-start.7 = (f32[2,128,128]{2,1,0:T(8,128)S(1)}, f32[2,128,128]{2,1,0:T(8,128)S(1)}, u32[]{:S(2)}, u32[]{:S(2)}) collective-permute-start(f32[2,128,128]{2,1,0:T(8,128)S(1)} %collective-permute-done.1.pair_ref), channel_id=1, source_target_pairs={{0,1},{1,0},{2,3},{3,2},{4,5},{5,4},{6,7},{7,6},{8,9},{9,8},{10,11... | collective-permute-start | bytes 393224 | tf_op jit(solution)/shard_map/ppermute | solution.py:20
  20.1 0.9 %own.1._ = f32[4,2048,128]{2,1,0:T(8,128)S(1)} custom-call(f32[4,7]{1,0:T(4,128)S(1)} %get-tuple-element.33.table_ref, bf16[4,4,512,128]{3,2,1,0:T(8,128)(2,1)S(1)} %get-tuple-element.50.per_head_ref, f32[4,4,512,128]{3,2,1,0:T(8,128)S(1)} %local.3.local_ref, f32[2,2,128,128]{3,2,1,0:T(8,128)S(1)} %collective-permute-done.received_ref, ...), custom_call_target="tpu_custom_call" | custom-call | flops 1000000000 | bytes 3145728 | tf_op jit(solution)/shard_map/own/pallas_call | solution.py:239
  21.0 0.0 collective-permute-done.6.near_ref
  21.0 0.0 collective-permute-done.8.group_ref
  21.0 0.1 collective-permute-done.7.pair_ref
  21.1 2.3 %last.1 = (bf16[2048,128]{1,0:T(8,128)(2,1)}, bf16[2048,128]{1,0:T(8,128)(2,1)}, bf16[2048,128]{1,0:T(8,128)(2,1)}, bf16[2048,128]{1,0:T(8,128)(2,1)}, f32[4,2048,128]{2,1,0:T(8,128)S(1)}) custom-call(f32[4,7]{1,0:T(4,128)S(1)} %get-tuple-element.33.table_ref, ...), custom_call_target="tpu_custom_call", output_to_operand_aliasing={{4}: (6, {})} | custom-call | tf_op jit(solution)/shard_map/last/pallas_call | solution.py:254
  (5 shorter events, 0.1 us)
Async XLA Ops:
  3.2 1.7 %collective-permute-start = (f32[2,2,128,128]{3,2,1,0:T(8,128)S(1)}, f32[2,2,128,128]{3,2,1,0:T(8,128)S(1)}, u32[]{:S(2)}, u32[]{:S(2)}) collective-permute-start(f32[2,2,128,128]{3,2,1,0:T(8,128)S(1)} %get-tuple-element.34), channel_id=1, source_target_pairs={{0,1},{1,0},{2,3},{3,2},{4,5},{5,4},{6,7},{7,6},{8,9},{9,8},{10,11... | collective-permute-start | bytes 786440 | tf_op jit(solution)/shard_map/ppermute | solution.py:20
  4.9 8.5 %collective-permute-start.2 = (f32[128,128]{1,0:T(8,128)S(1)}, f32[128,128]{1,0:T(8,128)S(1)}, u32[]{:S(2)}, u32[]{:S(2)}) collective-permute-start(f32[128,128]{1,0:T(8,128)S(1)} %select_bitcast_fusion), channel_id=1, source_target_pairs={{0,8},{4,12},{8,0},{12,4},{1,9},{5,13},{9,1},{13,5},{2,10},{6,14},... | collective-permute-start | bytes 196616 | tf_op jit(solution)/shard_map/ppermute | solution.py:25
  9.0 9.8 %collective-permute-start.1 = (f32[2,128,128]{2,1,0:T(8,128)S(1)}, f32[2,128,128]{2,1,0:T(8,128)S(1)}, u32[]{:S(2)}, u32[]{:S(2)}) collective-permute-start(f32[2,128,128]{2,1,0:T(8,128)S(1)} %get-tuple-element.44), channel_id=1, source_target_pairs={{0,4},{4,0},{8,12},{12,8},{1,5},{5,1},{9,13},{13,9},{2,6},{6,2},{1... | collective-permute-start | bytes 393224 | tf_op jit(solution)/shard_map/ppermute | solution.py:25
  10.6 7.8 %collective-permute-start.5 = (f32[128,128]{1,0:T(8,128)S(1)}, f32[128,128]{1,0:T(8,128)S(1)}, u32[]{:S(2)}, u32[]{:S(2)}) collective-permute-start(f32[128,128]{1,0:T(8,128)S(1)} %bitcast.17), channel_id=1, source_target_pairs={{0,8},{4,12},{8,0},{12,4},{1,9},{5,13},{9,1},{13,5},{2,10},{6,14},... | collective-permute-start | bytes 196616 | tf_op jit(solution)/shard_map/ppermute | solution.py:25
  11.0 7.8 %collective-permute-start.4 = (f32[128,128]{1,0:T(8,128)S(1)}, f32[128,128]{1,0:T(8,128)S(1)}, u32[]{:S(2)}, u32[]{:S(2)}) collective-permute-start(f32[128,128]{1,0:T(8,128)S(1)} %bitcast.18), channel_id=1, source_target_pairs={{0,12},{4,8},{8,4},{12,0},{1,13},{5,9},{9,5},{13,1},{2,14},{6,10},... | collective-permute-start | bytes 196616 | tf_op jit(solution)/shard_map/ppermute | solution.py:25
  13.4 7.6 %collective-permute-start.6 = (f32[2,128,128]{2,1,0:T(8,128)S(1)}, f32[2,128,128]{2,1,0:T(8,128)S(1)}, u32[]{:S(2)}, u32[]{:S(2)}) collective-permute-start(f32[2,128,128]{2,1,0:T(8,128)S(1)} %get-tuple-element.53), channel_id=1, source_target_pairs={{0,1},{1,0},{2,3},{3,2},{4,5},{5,4},{6,7},{7,6},{8,9},{9,8},{10,11... | collective-permute-start | bytes 393224 | tf_op jit(solution)/shard_map/ppermute | solution.py:20
  13.4 6.0 %collective-permute-start.3 = (f32[1,128,128]{2,1,0:T(8,128)S(1)}, f32[1,128,128]{2,1,0:T(8,128)S(1)}, u32[]{:S(2)}, u32[]{:S(2)}) collective-permute-start(f32[1,128,128]{2,1,0:T(8,128)S(1)} %bitcast.23), channel_id=1, source_target_pairs={{0,4},{4,0},{8,12},{12,8},{1,5},{5,1},{9,13},{13,9},{2,6},{6,2},{1... | collective-permute-start | bytes 196616 | tf_op jit(solution)/shard_map/ppermute | solution.py:25
  19.5 1.5 %collective-permute-start.8 = (f32[2,1,128,128]{3,2,1,0:T(8,128)S(1)}, f32[2,1,128,128]{3,2,1,0:T(8,128)S(1)}, u32[]{:S(2)}, u32[]{:S(2)}) collective-permute-start(f32[2,1,128,128]{3,2,1,0:T(8,128)S(1)} %pad_maximum_fusion.group_ref), channel_id=1, source_target_pairs={{0,1},{1,0},{2,3},{3,2},{4,5},{5,4},{6,7},{7,6},{8,9},{9,8},{10,11... | collective-permute-start | bytes 393224 | tf_op jit(solution)/shard_map/ppermute | solution.py:20
  19.6 1.5 %collective-permute-start.7 = (f32[2,128,128]{2,1,0:T(8,128)S(1)}, f32[2,128,128]{2,1,0:T(8,128)S(1)}, u32[]{:S(2)}, u32[]{:S(2)}) collective-permute-start(f32[2,128,128]{2,1,0:T(8,128)S(1)} %collective-permute-done.1.pair_ref), channel_id=1, source_target_pairs={{0,1},{1,0},{2,3},{3,2},{4,5},{5,4},{6,7},{7,6},{8,9},{9,8},{10,11... | collective-permute-start | bytes 393224 | tf_op jit(solution)/shard_map/ppermute | solution.py:20

commit v6 on v5

--- a/solution.py
+++ b/solution.py
@@ -12,6 +12,7 @@
 BLOCK = 64
 TILE = 128
 CHUNKS = 2
+PARTS = 2
 F32 = jnp.float32
 BF16 = jnp.bfloat16
 
@@ -65,18 +66,22 @@
 
     pairs = ((1, 2), (0, 3))
     for pair in pairs:
-        for which in pair:
-            for chunk in range(CHUNKS):
+        for chunk in range(CHUNKS):
+            for which in pair:
                 fetch(which, chunk).start()
     table = pltpu.make_async_copy(levels_ref, table_ref, listed)
     table.start()
+    tokens = rows // CHUNKS
     for kind, pair in enumerate(pairs):
-        for which in pair:
-            for chunk in range(CHUNKS):
+        for chunk in range(CHUNKS):
+            span, part = pl.ds(chunk * length, length), pl.ds(chunk * tokens, tokens)
+            for which in pair:
                 fetch(which, chunk).wait()
-            wide[which] = narrow[which].astype(F32)
-            for head in range(heads):
-                per_head_ref[which, head] = wide[which, pl.ds(head, rows, stride=heads), :].astype(BF16)
+                wide[which, span] = narrow[which, span].astype(F32)
+                for head in range(heads):
+                    per_head_ref[which, head, part] = wide[
+                        which, pl.ds(chunk * length + head, tokens, stride=heads), :
+                    ].astype(BF16)
         for place in range(half):
             for owner, out_ref in ((1 - core, send_ref), (core, keep_ref)):
                 head = owner * half + place
@@ -194,7 +199,7 @@
     return [jnp.concatenate(split(state), 0) for state in (keys_far, keys_far.T, queries_far.T, queries_far)]
 
 
-def far_heads(owner, table_ref, per_head_ref, local_ref, near, pair_ref, group_ref, wide_ref, finish=None):
+def far_heads(owner, table_ref, per_head_ref, local_ref, near, pair_ref, group_ref, wide_ref, finish=None, parts=1):
     heads, rows = per_head_ref.shape[1:3]
     half = heads // 2
     chosen = [owner * half + place for place in range(half)]
@@ -202,13 +207,16 @@
         far_states(table_ref, head, rows, near(place), pair_ref[place], [group_ref[place, bit] for bit in range(group_ref.shape[1])])
         for place, head in enumerate(chosen)
     ]
+    part = rows // parts
     for which, source in enumerate((0, 3, 2, 1)):
-        for head, pieces in zip(chosen, states):
-            mine = per_head_ref[source, head]
-            result = local_ref[which, head] + dot_nn(jnp.concatenate([mine, mine], 1), pieces[which])
-            wide_ref[which, pl.ds(head, rows, stride=heads), :] = result
-        if finish is not None:
-            finish(which)
+        for piece in range(parts):
+            span = pl.ds(piece * part, part)
+            for head, pieces in zip(chosen, states):
+                mine = per_head_ref[source, head, span]
+                result = local_ref[which, head, span] + dot_nn(jnp.concatenate([mine, mine], 1), pieces[which])
+                wide_ref[which, pl.ds(piece * part * heads + head, part, stride=heads), :] = result
+            if finish is not None:
+                finish(which, pl.ds(piece * part * heads, part * heads))
 
 
 def own_kernel(table_ref, per_head_ref, local_ref, received_ref, pair_ref, group_ref, wide_ref):
@@ -221,14 +229,14 @@
     out_refs, (wide_ref, narrow, left) = refs[:4], refs[4:]
     copies = []
 
-    def finish(which):
-        narrow[which] = wide_ref[which].astype(BF16)
-        copy = pltpu.make_async_copy(narrow.at[which], out_refs[which], left.at[which])
+    def finish(which, span):
+        narrow[which, span] = wide_ref[which, span].astype(BF16)
+        copy = pltpu.make_async_copy(narrow.at[which, span], out_refs[which].at[span], left.at[len(copies)])
         copy.start()
         copies.append(copy)
 
     far_heads(1 - lax.axis_index("rep"), table_ref, per_head_ref, local_ref, lambda place: near_ref[place],
-              pair_ref, group_ref, wide_ref, finish)
+              pair_ref, group_ref, wide_ref, finish, PARTS)
     for copy in copies:
         copy.wait()
 
@@ -256,7 +264,7 @@
         out_shape=[jax.ShapeDtypeStruct((rows * heads, width), BF16)] * 4 + [jax.ShapeDtypeStruct(wide.shape, F32)],
         in_specs=[pl.BlockSpec(memory_space=pltpu.VMEM)] + [vmem] * (1 + len(operands)),
         out_specs=[pl.BlockSpec(memory_space=pltpu.HBM)] * 4 + [vmem],
-        scratch_shapes=[pltpu.VMEM((4, rows * heads, width), BF16), pltpu.SemaphoreType.DMA((4,))],
+        scratch_shapes=[pltpu.VMEM((4, rows * heads, width), BF16), pltpu.SemaphoreType.DMA((4 * PARTS,))],
         input_output_aliases={1 + len(operands): 4},
         compiler_params=pltpu.CompilerParams(vmem_limit_bytes=16 * 2**20),
         name="last",

time: 23.6 us -> 23.2 us (0.983)
  Pallas kernels: 9.55 us -> 9.18 us
where the time goes in v6:
time: 23.2 us; the launch traced here: 23.1 us
  starting transfers between devices  10.2 us (44%)
  Pallas kernels  9.18 us (40%)
  waiting for transfers between devices  2.88 us (12%)
  between operations  0.72 us (3%)
    ppermute x5, starting transfers between devices, swap_chips(): lax.ppermute(block, 'seq', [(chip, chip ^ mask) for chip in range(count)])  9.16 us
    pallas_call x2, Pallas kernels, local_part(): pl.pallas_call(functools.partial(local_kernel, chosen), out_shape=jax.Sha...  3.76 us
    ppermute x5, waiting for transfers between devices, swap_chips(): lax.ppermute(block, 'seq', [(chip, chip ^ mask) for chip in range(count)])  2.63 us
    pallas_call x1, Pallas kernels, states(): pl.pallas_call(functools.partial(state_kernel, heads), out_shape=(jax.Sha...  2.43 us
    pallas_call x1, Pallas kernels, last_part(): pl.pallas_call(last_kernel, out_shape=[jax.ShapeDtypeStruct((rows * heads...  2.09 us
    ppermute x4, starting transfers between devices, swap_cores(): return lax.ppermute(block, 'rep', [(0, 1), (1, 0)])  1.08 us
    pallas_call x1, Pallas kernels, own_part(): pl.pallas_call(own_kernel, out_shape=jax.ShapeDtypeStruct((4, rows * head...  0.87 us
  transfers between devices with their start and end apart: 9, of which 5 were waited for; matrix products, arithmetic and copies ran while one was open for 0% of the time, Pallas kernels for 20%

profile of v6, /device:TPU:0, one launch (start us, length us, event | category | flops | bytes accessed | tf_op | source)
XLA Modules:
  0.0 23.1 jit_solution(16428345205608496937)
XLA Ops:
  0.6 2.4 %states.1 = (f32[2,2,128,128]{3,2,1,0:T(8,128)S(1)}, f32[2,2,128,128]{3,2,1,0:T(8,128)S(1)}, bf16[4,4,512,128]{3,2,1,0:T(8,128)(2,1)S(1)}, f32[4,7]{1,0:T(4,128)S(1)}) custom-call(bf16[2048,128]{1,0:T(8,128)(2,1)} %bitcast.19, bf16[2048,128]{1,0:T(8,128)(2,1)} %bitcast.20, bf16[2048,128]{1,0:T(8,128)(2,1)} %bitcast.21, bf16[2048,128]{1,0:T(8,128)(2,1)} %bitcast.22, ...), custom_call_target="tpu_custom_call" | custom-call | tf_op jit(solution)/shard_map/states/pallas_call | solution.py:96
  3.1 0.5 %collective-permute-start = (f32[2,2,128,128]{3,2,1,0:T(8,128)S(1)}, f32[2,2,128,128]{3,2,1,0:T(8,128)S(1)}, u32[]{:S(2)}, u32[]{:S(2)}) collective-permute-start(f32[2,2,128,128]{3,2,1,0:T(8,128)S(1)} %get-tuple-element.34), channel_id=1, source_target_pairs={{0,1},{1,0},{2,3},{3,2},{4,5},{5,4},{6,7},{7,6},{8,9},{9,8},{10,11... | collective-permute-start | bytes 786440 | tf_op jit(solution)/shard_map/ppermute | solution.py:21
  3.6 1.0 %local.2.refs_0_ = f32[4,4,512,128]{3,2,1,0:T(8,128)S(1)} custom-call(f32[4,7]{1,0:T(4,128)S(1)} %get-tuple-element.33.table_ref, bf16[4,4,512,128]{3,2,1,0:T(8,128)(2,1)S(1)} %get-tuple-element.50.per_head_ref), custom_call_target="tpu_custom_call" | custom-call | flops 1000000000 | bytes 1000000 | tf_op jit(solution)/shard_map/local/pallas_call | solution.py:178
  4.6 0.1 collective-permute-done.received_ref
  4.8 4.0 %collective-permute-start.2 = (f32[128,128]{1,0:T(8,128)S(1)}, f32[128,128]{1,0:T(8,128)S(1)}, u32[]{:S(2)}, u32[]{:S(2)}) collective-permute-start(f32[128,128]{1,0:T(8,128)S(1)} %select_bitcast_fusion), channel_id=1, source_target_pairs={{0,8},{4,12},{8,0},{12,4},{1,9},{5,13},{9,1},{13,5},{2,10},{6,14},... | collective-permute-start | bytes 196616 | tf_op jit(solution)/shard_map/ppermute | solution.py:26
  8.8 1.6 %collective-permute-start.1 = (f32[2,128,128]{2,1,0:T(8,128)S(1)}, f32[2,128,128]{2,1,0:T(8,128)S(1)}, u32[]{:S(2)}, u32[]{:S(2)}) collective-permute-start(f32[2,128,128]{2,1,0:T(8,128)S(1)} %get-tuple-element.44), channel_id=1, source_target_pairs={{0,4},{4,0},{8,12},{12,8},{1,5},{5,1},{9,13},{13,9},{2,6},{6,2},{1... | collective-permute-start | bytes 393224 | tf_op jit(solution)/shard_map/ppermute | solution.py:26
  10.5 0.3 %collective-permute-start.5 = (f32[128,128]{1,0:T(8,128)S(1)}, f32[128,128]{1,0:T(8,128)S(1)}, u32[]{:S(2)}, u32[]{:S(2)}) collective-permute-start(f32[128,128]{1,0:T(8,128)S(1)} %bitcast.17), channel_id=1, source_target_pairs={{0,8},{4,12},{8,0},{12,4},{1,9},{5,13},{9,1},{13,5},{2,10},{6,14},... | collective-permute-start | bytes 196616 | tf_op jit(solution)/shard_map/ppermute | solution.py:26
  10.8 2.5 %collective-permute-start.4 = (f32[128,128]{1,0:T(8,128)S(1)}, f32[128,128]{1,0:T(8,128)S(1)}, u32[]{:S(2)}, u32[]{:S(2)}) collective-permute-start(f32[128,128]{1,0:T(8,128)S(1)} %bitcast.18), channel_id=1, source_target_pairs={{0,12},{4,8},{8,4},{12,0},{1,13},{5,9},{9,5},{13,1},{2,14},{6,10},... | collective-permute-start | bytes 196616 | tf_op jit(solution)/shard_map/ppermute | solution.py:26
  13.3 0.0 collective-permute-start.6
  13.3 0.0 collective-permute-done.2
  13.3 0.7 %collective-permute-start.3 = (f32[1,128,128]{2,1,0:T(8,128)S(1)}, f32[1,128,128]{2,1,0:T(8,128)S(1)}, u32[]{:S(2)}, u32[]{:S(2)}) collective-permute-start(f32[1,128,128]{2,1,0:T(8,128)S(1)} %bitcast.23), channel_id=1, source_target_pairs={{0,4},{4,0},{8,12},{12,8},{1,5},{5,1},{9,13},{13,9},{2,6},{6,2},{1... | collective-permute-start | bytes 196616 | tf_op jit(solution)/shard_map/ppermute | solution.py:26
  14.0 2.7 %local.3.local_ref = f32[4,4,512,128]{3,2,1,0:T(8,128)S(1)} custom-call(f32[4,7]{1,0:T(4,128)S(1)} %get-tuple-element.33.table_ref, bf16[4,4,512,128]{3,2,1,0:T(8,128)(2,1)S(1)} %get-tuple-element.50.per_head_ref, f32[4,4,512,128]{3,2,1,0:T(8,128)S(1)} %local.2.refs_0_), custom_call_target="tpu_custom_call", output_to_operand_aliasing={{}: (2, {})} | custom-call | flops 1000000000 | bytes 1000000 | tf_op jit(solution)/shard_map/local/pallas_call | solution.py:178
  16.7 1.6 %collective-permute-done.5 = f32[128,128]{1,0:T(8,128)S(1)} collective-permute-done((f32[128,128]{1,0:T(8,128)S(1)}, f32[128,128]{1,0:T(8,128)S(1)}, u32[]{:S(2)}, u32[]{:S(2)}) %collective-permute-start.5) | collective-permute-done | bytes 65568 | tf_op jit(solution)/shard_map/ppermute | solution.py:26
  18.3 0.4 %collective-permute-done.4 = f32[128,128]{1,0:T(8,128)S(1)} collective-permute-done((f32[128,128]{1,0:T(8,128)S(1)}, f32[128,128]{1,0:T(8,128)S(1)}, u32[]{:S(2)}, u32[]{:S(2)}) %collective-permute-start.4) | collective-permute-done | bytes 65568 | tf_op jit(solution)/shard_map/ppermute | solution.py:26
  18.6 0.0 collective-permute-done.1.pair_ref
  18.6 0.7 %collective-permute-done.3 = f32[1,128,128]{2,1,0:T(8,128)S(1)} collective-permute-done((f32[1,128,128]{2,1,0:T(8,128)S(1)}, f32[1,128,128]{2,1,0:T(8,128)S(1)}, u32[]{:S(2)}, u32[]{:S(2)}) %collective-permute-start.3) | collective-permute-done | bytes 65568 | tf_op jit(solution)/shard_map/ppermute | solution.py:26
  19.4 0.1 collective-permute-start.8
  19.5 0.5 %collective-permute-start.7 = (f32[2,128,128]{2,1,0:T(8,128)S(1)}, f32[2,128,128]{2,1,0:T(8,128)S(1)}, u32[]{:S(2)}, u32[]{:S(2)}) collective-permute-start(f32[2,128,128]{2,1,0:T(8,128)S(1)} %collective-permute-done.1.pair_ref), channel_id=1, source_target_pairs={{0,1},{1,0},{2,3},{3,2},{4,5},{5,4},{6,7},{7,6},{8,9},{9,8},{10,11... | collective-permute-start | bytes 393224 | tf_op jit(solution)/shard_map/ppermute | solution.py:21
  20.0 0.9 %own.1._ = f32[4,2048,128]{2,1,0:T(8,128)S(1)} custom-call(f32[4,7]{1,0:T(4,128)S(1)} %get-tuple-element.33.table_ref, bf16[4,4,512,128]{3,2,1,0:T(8,128)(2,1)S(1)} %get-tuple-element.50.per_head_ref, f32[4,4,512,128]{3,2,1,0:T(8,128)S(1)} %local.3.local_ref, f32[2,2,128,128]{3,2,1,0:T(8,128)S(1)} %collective-permute-done.received_ref, ...), custom_call_target="tpu_custom_call" | custom-call | flops 1000000000 | bytes 3145728 | tf_op jit(solution)/shard_map/own/pallas_call | solution.py:247
  20.8 0.0 collective-permute-done.6.near_ref
  20.8 0.0 collective-permute-done.8.group_ref
  20.8 0.1 collective-permute-done.7.pair_ref
  21.0 2.1 %last.1 = (bf16[2048,128]{1,0:T(8,128)(2,1)}, bf16[2048,128]{1,0:T(8,128)(2,1)}, bf16[2048,128]{1,0:T(8,128)(2,1)}, bf16[2048,128]{1,0:T(8,128)(2,1)}, f32[4,2048,128]{2,1,0:T(8,128)S(1)}) custom-call(f32[4,7]{1,0:T(4,128)S(1)} %get-tuple-element.33.table_ref, ...), custom_call_target="tpu_custom_call", output_to_operand_aliasing={{4}: (6, {})} | custom-call | tf_op jit(solution)/shard_map/last/pallas_call | solution.py:262
  (5 shorter events, 0.1 us)
Async XLA Ops:
  3.1 1.7 %collective-permute-start = (f32[2,2,128,128]{3,2,1,0:T(8,128)S(1)}, f32[2,2,128,128]{3,2,1,0:T(8,128)S(1)}, u32[]{:S(2)}, u32[]{:S(2)}) collective-permute-start(f32[2,2,128,128]{3,2,1,0:T(8,128)S(1)} %get-tuple-element.34), channel_id=1, source_target_pairs={{0,1},{1,0},{2,3},{3,2},{4,5},{5,4},{6,7},{7,6},{8,9},{9,8},{10,11... | collective-permute-start | bytes 786440 | tf_op jit(solution)/shard_map/ppermute | solution.py:21
  4.8 8.5 %collective-permute-start.2 = (f32[128,128]{1,0:T(8,128)S(1)}, f32[128,128]{1,0:T(8,128)S(1)}, u32[]{:S(2)}, u32[]{:S(2)}) collective-permute-start(f32[128,128]{1,0:T(8,128)S(1)} %select_bitcast_fusion), channel_id=1, source_target_pairs={{0,8},{4,12},{8,0},{12,4},{1,9},{5,13},{9,1},{13,5},{2,10},{6,14},... | collective-permute-start | bytes 196616 | tf_op jit(solution)/shard_map/ppermute | solution.py:26
  8.8 9.8 %collective-permute-start.1 = (f32[2,128,128]{2,1,0:T(8,128)S(1)}, f32[2,128,128]{2,1,0:T(8,128)S(1)}, u32[]{:S(2)}, u32[]{:S(2)}) collective-permute-start(f32[2,128,128]{2,1,0:T(8,128)S(1)} %get-tuple-element.44), channel_id=1, source_target_pairs={{0,4},{4,0},{8,12},{12,8},{1,5},{5,1},{9,13},{13,9},{2,6},{6,2},{1... | collective-permute-start | bytes 393224 | tf_op jit(solution)/shard_map/ppermute | solution.py:26
  10.5 7.8 %collective-permute-start.5 = (f32[128,128]{1,0:T(8,128)S(1)}, f32[128,128]{1,0:T(8,128)S(1)}, u32[]{:S(2)}, u32[]{:S(2)}) collective-permute-start(f32[128,128]{1,0:T(8,128)S(1)} %bitcast.17), channel_id=1, source_target_pairs={{0,8},{4,12},{8,0},{12,4},{1,9},{5,13},{9,1},{13,5},{2,10},{6,14},... | collective-permute-start | bytes 196616 | tf_op jit(solution)/shard_map/ppermute | solution.py:26
  10.8 7.8 %collective-permute-start.4 = (f32[128,128]{1,0:T(8,128)S(1)}, f32[128,128]{1,0:T(8,128)S(1)}, u32[]{:S(2)}, u32[]{:S(2)}) collective-permute-start(f32[128,128]{1,0:T(8,128)S(1)} %bitcast.18), channel_id=1, source_target_pairs={{0,12},{4,8},{8,4},{12,0},{1,13},{5,9},{9,5},{13,1},{2,14},{6,10},... | collective-permute-start | bytes 196616 | tf_op jit(solution)/shard_map/ppermute | solution.py:26
  13.3 7.6 %collective-permute-start.6 = (f32[2,128,128]{2,1,0:T(8,128)S(1)}, f32[2,128,128]{2,1,0:T(8,128)S(1)}, u32[]{:S(2)}, u32[]{:S(2)}) collective-permute-start(f32[2,128,128]{2,1,0:T(8,128)S(1)} %get-tuple-element.53), channel_id=1, source_target_pairs={{0,1},{1,0},{2,3},{3,2},{4,5},{5,4},{6,7},{7,6},{8,9},{9,8},{10,11... | collective-permute-start | bytes 393224 | tf_op jit(solution)/shard_map/ppermute | solution.py:21
  13.3 6.0 %collective-permute-start.3 = (f32[1,128,128]{2,1,0:T(8,128)S(1)}, f32[1,128,128]{2,1,0:T(8,128)S(1)}, u32[]{:S(2)}, u32[]{:S(2)}) collective-permute-start(f32[1,128,128]{2,1,0:T(8,128)S(1)} %bitcast.23), channel_id=1, source_target_pairs={{0,4},{4,0},{8,12},{12,8},{1,5},{5,1},{9,13},{13,9},{2,6},{6,2},{1... | collective-permute-start | bytes 196616 | tf_op jit(solution)/shard_map/ppermute | solution.py:26
  19.4 1.5 %collective-permute-start.8 = (f32[2,1,128,128]{3,2,1,0:T(8,128)S(1)}, f32[2,1,128,128]{3,2,1,0:T(8,128)S(1)}, u32[]{:S(2)}, u32[]{:S(2)}) collective-permute-start(f32[2,1,128,128]{3,2,1,0:T(8,128)S(1)} %pad_maximum_fusion.group_ref), channel_id=1, source_target_pairs={{0,1},{1,0},{2,3},{3,2},{4,5},{5,4},{6,7},{7,6},{8,9},{9,8},{10,11... | collective-permute-start | bytes 393224 | tf_op jit(solution)/shard_map/ppermute | solution.py:21
  19.5 1.5 %collective-permute-start.7 = (f32[2,128,128]{2,1,0:T(8,128)S(1)}, f32[2,128,128]{2,1,0:T(8,128)S(1)}, u32[]{:S(2)}, u32[]{:S(2)}) collective-permute-start(f32[2,128,128]{2,1,0:T(8,128)S(1)} %collective-permute-done.1.pair_ref), channel_id=1, source_target_pairs={{0,1},{1,0},{2,3},{3,2},{4,5},{5,4},{6,7},{7,6},{8,9},{9,8},{10,11... | collective-permute-start | bytes 393224 | tf_op jit(solution)/shard_map/ppermute | solution.py:21

commit v7 on v6

--- a/solution.py
+++ b/solution.py
@@ -52,7 +52,7 @@
 
 
 def state_kernel(
-    heads, q_ref, k_ref, v_ref, g_ref, levels_ref, send_ref, keep_ref, per_head_ref, table_ref, narrow, wide, arrived, listed
+    heads, q_ref, k_ref, v_ref, g_ref, levels_ref, send_a_ref, send_b_ref, keep_ref, per_head_ref, table_ref, narrow, wide, arrived, listed
 ):
     rows = q_ref.shape[0] // heads
     half = heads // 2
@@ -83,9 +83,15 @@
                         which, pl.ds(chunk * length + head, tokens, stride=heads), :
                     ].astype(BF16)
         for place in range(half):
-            for owner, out_ref in ((1 - core, send_ref), (core, keep_ref)):
-                head = owner * half + place
-                out_ref[kind, place] = dot_tn(per_head_ref[pair[0], head], per_head_ref[pair[1], head])
+            for sent in (True, False):
+                head = (1 - core if sent else core) * half + place
+                state = dot_tn(per_head_ref[pair[0], head], per_head_ref[pair[1], head])
+                if not sent:
+                    keep_ref[kind, place] = state
+                elif place == 0:
+                    send_a_ref[kind] = state
+                else:
+                    send_b_ref[kind, place - 1] = state
     table.wait()
 
 
@@ -96,13 +102,14 @@
     return pl.pallas_call(
         functools.partial(state_kernel, heads),
         out_shape=(
-            jax.ShapeDtypeStruct(half, F32),
+            jax.ShapeDtypeStruct((2, width, width), F32),
+            jax.ShapeDtypeStruct((2, heads // 2 - 1, width, width), F32),
             jax.ShapeDtypeStruct(half, F32),
             jax.ShapeDtypeStruct((4, heads, rows, width), BF16),
             jax.ShapeDtypeStruct(table.shape, F32),
         ),
         in_specs=[pl.BlockSpec(memory_space=pltpu.HBM)] * 5,
-        out_specs=[pl.BlockSpec(memory_space=pltpu.VMEM)] * 4,
+        out_specs=[pl.BlockSpec(memory_space=pltpu.VMEM)] * 5,
         scratch_shapes=[
             pltpu.VMEM((4, rows * heads, width), BF16),
             pltpu.VMEM((4, rows * heads, width), F32),
@@ -117,11 +124,11 @@
 def local_kernel(chosen, table_ref, per_head_ref, *refs):
     out_ref = refs[-1]
     rows = per_head_ref.shape[2]
-    for head in chosen:
-        local_head(head, rows, table_ref, per_head_ref.at[:, head], out_ref.at[:, head])
-
-
-def local_head(head, rows, table_ref, per_head_ref, out_ref):
+    for head, sides in chosen:
+        local_head(head, sides, rows, table_ref, per_head_ref.at[:, head], out_ref.at[:, head])
+
+
+def local_head(head, sides, rows, table_ref, per_head_ref, out_ref):
     tiles = rows // TILE
     inner = (TILE // BLOCK).bit_length()
     weight = [weight_of(table_ref, head, level) for level in range(inner + tiles.bit_length() - 1)]
@@ -153,22 +160,29 @@
 
     turned = [[block.T for block in array] for array in part]
     q_t, k_t, v_t, g_t = turned
-    key_sums = sums([dot_nn(k_t[tile], values[tile]) for tile in range(tiles)])
-    key_sums_t = sums([dot_nn(v_t[tile], keys[tile]) for tile in range(tiles)])
-    query_sums = sums([dot_nn(q_t[tile], out_grad[tile]) for tile in range(tiles)])
-    query_sums_t = sums([dot_nn(g_t[tile], queries[tile]) for tile in range(tiles)])
+    if 0 in sides:
+        key_sums = sums([dot_nn(k_t[tile], values[tile]) for tile in range(tiles)])
+        key_sums_t = sums([dot_nn(v_t[tile], keys[tile]) for tile in range(tiles)])
+    if 1 in sides:
+        query_sums = sums([dot_nn(q_t[tile], out_grad[tile]) for tile in range(tiles)])
+        query_sums_t = sums([dot_nn(g_t[tile], queries[tile]) for tile in range(tiles)])
     held = []
     for tile in range(tiles):
         q, k, v, g = (array[tile] for array in part)
-        terms = (
-            (dot_nn(q, k_t[tile]) * lower, v, q, gather(key_sums, tile, 1)),
-            (dot_nn(g, v_t[tile]) * lower, k, g, gather(key_sums_t, tile, 1)),
-            (dot_nn(v, g_t[tile]) * upper, q, v, gather(query_sums_t, tile, 0)),
-            (dot_nn(k, q_t[tile]) * upper, g, k, gather(query_sums, tile, 0)),
-        )
+        terms = []
+        if 0 in sides:
+            terms += [
+                (0, dot_nn(q, k_t[tile]) * lower, v, q, gather(key_sums, tile, 1)),
+                (1, dot_nn(g, v_t[tile]) * lower, k, g, gather(key_sums_t, tile, 1)),
+            ]
+        if 1 in sides:
+            terms += [
+                (2, dot_nn(v, g_t[tile]) * upper, q, v, gather(query_sums_t, tile, 0)),
+                (3, dot_nn(k, q_t[tile]) * upper, g, k, gather(query_sums, tile, 0)),
+            ]
         held.append(terms)
     for tile in range(tiles):
-        for which, (inside, other, mine, pieces) in enumerate(held[tile]):
+        for which, inside, other, mine, pieces in held[tile]:
             result = dot_nn(jnp.concatenate([*split(inside), *([mine, mine] if pieces else [])], 1), jnp.concatenate([other, other, *pieces], 0))
             out_ref[which, pl.ds(tile * TILE, TILE), :] = result
 
@@ -219,9 +233,9 @@
                 finish(which, pl.ds(piece * part * heads, part * heads))
 
 
-def own_kernel(table_ref, per_head_ref, local_ref, received_ref, pair_ref, group_ref, wide_ref):
+def own_kernel(table_ref, per_head_ref, local_ref, received_a_ref, received_b_ref, pair_ref, group_ref, wide_ref):
     core = lax.axis_index("rep")
-    far_heads(core, table_ref, per_head_ref, local_ref, lambda place: received_ref[1 - core, place],
+    far_heads(core, table_ref, per_head_ref, local_ref, lambda place: received_b_ref[1 - core, place - 1] if place else received_a_ref[1 - core],
               pair_ref, group_ref, wide_ref)
 
 
@@ -272,29 +286,30 @@
     return tuple(out.reshape(rows, heads, width) for out in outs[:4])
 
 
-def load_kernel(keep_ref, received_ref, pair_ref, rest_ref, near_ref):
+def load_kernel(keep_ref, received_a_ref, received_b_ref, pair_ref, rest_ref, near_ref):
     core, chip = lax.axis_index("rep"), lax.axis_index("seq")
     kind = chip % 2
-    pair_ref[...] = keep_ref[kind] + received_ref[kind]
+    pair_ref[0] = keep_ref[kind, 0] + received_a_ref[kind]
+    pair_ref[1:] = keep_ref[kind, 1:] + received_b_ref[kind]
     for bit in range(rest_ref.shape[0]):
         kind = (chip >> (bit + 1)) % 2
-        rest_ref[bit] = keep_ref[kind, 1] + received_ref[kind, 1]
+        rest_ref[bit] = keep_ref[kind, 1] + received_b_ref[kind, 0]
     near_ref[...] = keep_ref[core]
 
 
-def loads_of(bits, keep, received):
+def loads_of(bits, keep, *received):
     vmem = pl.BlockSpec(memory_space=pltpu.VMEM)
     half, width = keep.shape[1], keep.shape[2]
     shapes = ((half, width, width), (bits - 1, width, width), (half, width, width))
     return pl.pallas_call(
         load_kernel,
         out_shape=[jax.ShapeDtypeStruct(shape, F32) for shape in shapes],
-        in_specs=[vmem] * 2,
+        in_specs=[vmem] * 3,
         out_specs=[vmem] * 3,
         compiler_params=pltpu.CompilerParams(vmem_limit_bytes=4 * 2**20),
         cost_estimate=pl.CostEstimate(flops=10**9, bytes_accessed=3 * 2**20, transcendentals=0),
         name="loads",
-    )(keep, received)
+    )(keep, *received)
 
 
 def per_device(queries, keys, values, out_grad, level_table):
@@ -303,19 +318,19 @@
     bits = lax.axis_size("seq").bit_length() - 1
     chip = lax.axis_index("seq")
     flat = [array.reshape(rows * heads, width) for array in (queries, keys, values, out_grad)]
-    send, keep, per_head, table = states(flat, level_table.T)
-    received = swap_cores(send)
-    local_a = local_part((0,), 10**9, table, per_head)
-    received, per_head, local_a = lax.optimization_barrier((received, per_head, local_a))
+    send_a, send_b, keep, per_head, table = states(flat, level_table.T)
+    received_a, received_b = swap_cores(send_a), swap_cores(send_b)
+    local_a = local_part([(0, (0,))], 10**9, table, per_head)
+    received_a, per_head, local_a = lax.optimization_barrier((received_a, per_head, local_a))
     first = [
-        jnp.where((chip >> bit) % 2 == 1, keep[1, 0] + received[1, 0], keep[0, 0] + received[0, 0])
+        jnp.where((chip >> bit) % 2 == 1, keep[1, 0] + received_a[1], keep[0, 0] + received_a[0])
         for bit in range(1, bits)
     ]
-    first, keep, received = lax.optimization_barrier((first, keep, received))
+    first, keep, received_a = lax.optimization_barrier((first, keep, received_a))
     half_way = [
         sum(swap_chips(first[bit - 1], mask) for mask in range(1 << bit, 2 << bit, 2)) for bit in range(1, bits)
     ]
-    pair_load, rest, near_load = loads_of(bits, keep, received)
+    pair_load, rest, near_load = loads_of(bits, keep, received_a, received_b)
     pair_load, rest, near_load, held = lax.optimization_barrier((pair_load, rest, near_load, per_head))
     group_b = [
         [swap_chips(rest[bit - 1], mask) for mask in range((2 << bit) - 1, (1 << bit) - 1, -1)] for bit in range(1, bits)
@@ -325,12 +340,12 @@
     half_way = jnp.stack(half_way)
     half_way, held, local_a = lax.optimization_barrier((half_way, held, local_a))
     hop = swap_chips(half_way, 1)
-    local_b = local_part(tuple(range(1, heads)), 10**9, table, held, local_a)
+    local_b = local_part([(0, (1,))] + [(head, (0, 1)) for head in range(1, heads)], 10**9, table, held, local_a)
     pair, hop, group_b, local_b = lax.optimization_barrier((pair, hop, group_b, local_b))
     pair_o = swap_cores(pair)
     group = jnp.stack([half_way + hop, jnp.stack([sum(pieces) for pieces in group_b])])
     group_o = swap_cores(group)
-    wide = own_part(table, per_head, local_b, received, pair, group)
+    wide = own_part(table, per_head, local_b, received_a, received_b, pair, group)
     return last_part(table, per_head, local_b, near, pair_o, group_o, wide)
 
 

time: 23.2 us -> 23 us (level)
  waiting for transfers between devices: 2.88 us -> 2.59 us
    ppermute x5, waiting for transfers between devices: 2.63 us -> 2.2 us  [swap_chips(): lax.ppermute(block, 'seq', [(chip, chip ^ mask) for chip in range(count)])]
    ppermute x4 -> x5, starting transfers between devices: 1.08 us -> 1.16 us  [swap_cores(): return lax.ppermute(block, 'rep', [(0, 1), (1, 0)])]
  transfers between devices with their start and end apart: 9 -> 10, of which waited for: 5 -> 5; matrix products, arithmetic and copies ran while one was open for 0% -> 0% of each run, Pallas kernels for 20% -> 21%
where the time goes in v7:
time: 23 us; the launch traced here: 22.9 us
  starting transfers between devices  10.3 us (45%)
  Pallas kernels  9.23 us (40%)
  waiting for transfers between devices  2.59 us (11%)
  between operations  0.72 us (3%)
    ppermute x5, starting transfers between devices, swap_chips(): lax.ppermute(block, 'seq', [(chip, chip ^ mask) for chip in range(count)])  9.15 us
    pallas_call x2, Pallas kernels, local_part(): pl.pallas_call(functools.partial(local_kernel, chosen), out_shape=jax.Sha...  3.82 us
    pallas_call x1, Pallas kernels, states(): pl.pallas_call(functools.partial(state_kernel, heads), out_shape=(jax.Sha...  2.43 us
    ppermute x5, waiting for transfers between devices, swap_chips(): lax.ppermute(block, 'seq', [(chip, chip ^ mask) for chip in range(count)])  2.2 us
    pallas_call x1, Pallas kernels, last_part(): pl.pallas_call(last_kernel, out_shape=[jax.ShapeDtypeStruct((rows * heads...  2.09 us
    ppermute x5, starting transfers between devices, swap_cores(): return lax.ppermute(block, 'rep', [(0, 1), (1, 0)])  1.16 us
    pallas_call x1, Pallas kernels, own_part(): pl.pallas_call(own_kernel, out_shape=jax.ShapeDtypeStruct((4, rows * head...  0.86 us
  transfers between devices with their start and end apart: 10, of which 5 were waited for; matrix products, arithmetic and copies ran while one was open for 0% of the time, Pallas kernels for 21%

profile of v7, /device:TPU:0, one launch (start us, length us, event | category | flops | bytes accessed | tf_op | source)
XLA Modules:
  0.0 22.9 jit_solution(14727560514773221242)
XLA Ops:
  0.6 2.4 %states.1 = (f32[2,128,128]{2,1,0:T(8,128)S(1)}, f32[2,1,128,128]{3,2,1,0:T(8,128)S(1)}, f32[2,2,128,128]{3,2,1,0:T(8,128)S(1)}, bf16[4,4,512,128]{3,2,1,0:T(8,128)(2,1)S(1)}, f32[4,7]{1,0:T(4,128)S(1)}) custom-call(bf16[2048,128]{1,0:T(8,128)(2,1)} %bitcast.29, bf16[2048,128]{1,0:T(8,128)(2,1)} %bitcast.30, bf16[2048,128]{1,0:T(8,128)(2,1)} %bitcast.31, ...), custom_call_target="tpu_custom_call" | custom-call | tf_op jit(solution)/shard_map/states/pallas_call | solution.py:102
  3.1 0.5 %collective-permute-start = (f32[2,128,128]{2,1,0:T(8,128)S(1)}, f32[2,128,128]{2,1,0:T(8,128)S(1)}, u32[]{:S(2)}, u32[]{:S(2)}) collective-permute-start(f32[2,128,128]{2,1,0:T(8,128)S(1)} %get-tuple-element.35), channel_id=1, source_target_pairs={{0,1},{1,0},{2,3},{3,2},{4,5},{5,4},{6,7},{7,6},{8,9},{9,8},{10,11... | collective-permute-start | bytes 393224 | tf_op jit(solution)/shard_map/ppermute | solution.py:21
  3.6 0.1 collective-permute-start.1
  3.7 0.6 %local.2.refs_0_ = f32[4,4,512,128]{3,2,1,0:T(8,128)S(1)} custom-call(f32[4,7]{1,0:T(4,128)S(1)} %get-tuple-element.34.table_ref, bf16[4,4,512,128]{3,2,1,0:T(8,128)(2,1)S(1)} %get-tuple-element.52.per_head_ref), custom_call_target="tpu_custom_call" | custom-call | flops 1000000000 | bytes 1000000 | tf_op jit(solution)/shard_map/local/pallas_call | solution.py:192
  4.3 0.3 %collective-permute-done.received_a_ref = f32[2,128,128]{2,1,0:T(8,128)S(1)} collective-permute-done((f32[2,128,128]{2,1,0:T(8,128)S(1)}, f32[2,128,128]{2,1,0:T(8,128)S(1)}, u32[]{:S(2)}, u32[]{:S(2)}) %collective-permute-start) | collective-permute-done | bytes 131104 | tf_op jit(solution)/shard_map/ppermute | solution.py:21
  4.6 4.0 %collective-permute-start.3 = (f32[128,128]{1,0:T(8,128)S(1)}, f32[128,128]{1,0:T(8,128)S(1)}, u32[]{:S(2)}, u32[]{:S(2)}) collective-permute-start(f32[128,128]{1,0:T(8,128)S(1)} %fusion), channel_id=1, source_target_pairs={{0,8},{4,12},{8,0},{12,4},{1,9},{5,13},{9,1},{13,5},{2,10},{6,14},... | collective-permute-start | bytes 196616 | tf_op jit(solution)/shard_map/ppermute | solution.py:26
  8.6 0.0 collective-permute-done.1.received_b_ref
  8.6 1.6 %collective-permute-start.2 = (f32[2,128,128]{2,1,0:T(8,128)S(1)}, f32[2,128,128]{2,1,0:T(8,128)S(1)}, u32[]{:S(2)}, u32[]{:S(2)}) collective-permute-start(f32[2,128,128]{2,1,0:T(8,128)S(1)} %get-tuple-element.46), channel_id=1, source_target_pairs={{0,4},{4,0},{8,12},{12,8},{1,5},{5,1},{9,13},{13,9},{2,6},{6,2},{1... | collective-permute-start | bytes 393224 | tf_op jit(solution)/shard_map/ppermute | solution.py:26
  10.3 0.3 %collective-permute-start.6 = (f32[128,128]{1,0:T(8,128)S(1)}, f32[128,128]{1,0:T(8,128)S(1)}, u32[]{:S(2)}, u32[]{:S(2)}) collective-permute-start(f32[128,128]{1,0:T(8,128)S(1)} %bitcast.27), channel_id=1, source_target_pairs={{0,8},{4,12},{8,0},{12,4},{1,9},{5,13},{9,1},{13,5},{2,10},{6,14},... | collective-permute-start | bytes 196616 | tf_op jit(solution)/shard_map/ppermute | solution.py:26
  10.6 2.5 %collective-permute-start.5 = (f32[128,128]{1,0:T(8,128)S(1)}, f32[128,128]{1,0:T(8,128)S(1)}, u32[]{:S(2)}, u32[]{:S(2)}) collective-permute-start(f32[128,128]{1,0:T(8,128)S(1)} %bitcast.28), channel_id=1, source_target_pairs={{0,12},{4,8},{8,4},{12,0},{1,13},{5,9},{9,5},{13,1},{2,14},{6,10},... | collective-permute-start | bytes 196616 | tf_op jit(solution)/shard_map/ppermute | solution.py:26
  13.1 0.0 collective-permute-start.7
  13.1 0.0 collective-permute-done.3
  13.1 0.7 %collective-permute-start.4 = (f32[1,128,128]{2,1,0:T(8,128)S(1)}, f32[1,128,128]{2,1,0:T(8,128)S(1)}, u32[]{:S(2)}, u32[]{:S(2)}) collective-permute-start(f32[1,128,128]{2,1,0:T(8,128)S(1)} %bitcast.33), channel_id=1, source_target_pairs={{0,4},{4,0},{8,12},{12,8},{1,5},{5,1},{9,13},{13,9},{2,6},{6,2},{1... | collective-permute-start | bytes 196616 | tf_op jit(solution)/shard_map/ppermute | solution.py:26
  13.8 3.2 %local.3.local_ref = f32[4,4,512,128]{3,2,1,0:T(8,128)S(1)} custom-call(f32[4,7]{1,0:T(4,128)S(1)} %get-tuple-element.34.table_ref, bf16[4,4,512,128]{3,2,1,0:T(8,128)(2,1)S(1)} %get-tuple-element.52.per_head_ref, f32[4,4,512,128]{3,2,1,0:T(8,128)S(1)} %local.2.refs_0_), custom_call_target="tpu_custom_call", output_to_operand_aliasing={{}: (2, {})} | custom-call | flops 1000000000 | bytes 1000000 | tf_op jit(solution)/shard_map/local/pallas_call | solution.py:192
  17.0 1.1 %collective-permute-done.6 = f32[128,128]{1,0:T(8,128)S(1)} collective-permute-done((f32[128,128]{1,0:T(8,128)S(1)}, f32[128,128]{1,0:T(8,128)S(1)}, u32[]{:S(2)}, u32[]{:S(2)}) %collective-permute-start.6) | collective-permute-done | bytes 65568 | tf_op jit(solution)/shard_map/ppermute | solution.py:26
  18.1 0.3 %collective-permute-done.5 = f32[128,128]{1,0:T(8,128)S(1)} collective-permute-done((f32[128,128]{1,0:T(8,128)S(1)}, f32[128,128]{1,0:T(8,128)S(1)}, u32[]{:S(2)}, u32[]{:S(2)}) %collective-permute-start.5) | collective-permute-done | bytes 65568 | tf_op jit(solution)/shard_map/ppermute | solution.py:26
  18.4 0.7 %collective-permute-done.4 = f32[1,128,128]{2,1,0:T(8,128)S(1)} collective-permute-done((f32[1,128,128]{2,1,0:T(8,128)S(1)}, f32[1,128,128]{2,1,0:T(8,128)S(1)}, u32[]{:S(2)}, u32[]{:S(2)}) %collective-permute-start.4) | collective-permute-done | bytes 65568 | tf_op jit(solution)/shard_map/ppermute | solution.py:26
  19.2 0.0 collective-permute-done.2.pair_ref
  19.2 0.1 collective-permute-start.9
  19.3 0.5 %collective-permute-start.8 = (f32[2,128,128]{2,1,0:T(8,128)S(1)}, f32[2,128,128]{2,1,0:T(8,128)S(1)}, u32[]{:S(2)}, u32[]{:S(2)}) collective-permute-start(f32[2,128,128]{2,1,0:T(8,128)S(1)} %collective-permute-done.2.pair_ref), channel_id=1, source_target_pairs={{0,1},{1,0},{2,3},{3,2},{4,5},{5,4},{6,7},{7,6},{8,9},{9,8},{10,11... | collective-permute-start | bytes 393224 | tf_op jit(solution)/shard_map/ppermute | solution.py:21
  19.8 0.9 %own.1._ = f32[4,2048,128]{2,1,0:T(8,128)S(1)} custom-call(f32[4,7]{1,0:T(4,128)S(1)} %get-tuple-element.34.table_ref, bf16[4,4,512,128]{3,2,1,0:T(8,128)(2,1)S(1)} %get-tuple-element.52.per_head_ref, f32[4,4,512,128]{3,2,1,0:T(8,128)S(1)} %local.3.local_ref, f32[2,128,128]{2,1,0:T(8,128)S(1)} %collective-permute-done.received_a_ref, ...), custom_call_target="tpu_custom_call" | custom-call | flops 1000000000 | bytes 3145728 | tf_op jit(solution)/shard_map/own/pallas_call | solution.py:261
  20.6 0.0 collective-permute-done.7.near_ref
  20.7 0.0 collective-permute-done.9.group_ref
  20.7 0.1 collective-permute-done.8.pair_ref
  20.8 2.1 %last.1 = (bf16[2048,128]{1,0:T(8,128)(2,1)}, bf16[2048,128]{1,0:T(8,128)(2,1)}, bf16[2048,128]{1,0:T(8,128)(2,1)}, bf16[2048,128]{1,0:T(8,128)(2,1)}, f32[4,2048,128]{2,1,0:T(8,128)S(1)}) custom-call(f32[4,7]{1,0:T(4,128)S(1)} %get-tuple-element.34.table_ref, ...), custom_call_target="tpu_custom_call", output_to_operand_aliasing={{4}: (6, {})} | custom-call | tf_op jit(solution)/shard_map/last/pallas_call | solution.py:276
  (5 shorter events, 0.1 us)
Async XLA Ops:
  3.1 1.5 %collective-permute-start = (f32[2,128,128]{2,1,0:T(8,128)S(1)}, f32[2,128,128]{2,1,0:T(8,128)S(1)}, u32[]{:S(2)}, u32[]{:S(2)}) collective-permute-start(f32[2,128,128]{2,1,0:T(8,128)S(1)} %get-tuple-element.35), channel_id=1, source_target_pairs={{0,1},{1,0},{2,3},{3,2},{4,5},{5,4},{6,7},{7,6},{8,9},{9,8},{10,11... | collective-permute-start | bytes 393224 | tf_op jit(solution)/shard_map/ppermute | solution.py:21
  3.6 5.0 %collective-permute-start.1 = (f32[2,1,128,128]{3,2,1,0:T(8,128)S(1)}, f32[2,1,128,128]{3,2,1,0:T(8,128)S(1)}, u32[]{:S(2)}, u32[]{:S(2)}) collective-permute-start(f32[2,1,128,128]{3,2,1,0:T(8,128)S(1)} %get-tuple-element.42), channel_id=1, source_target_pairs={{0,1},{1,0},{2,3},{3,2},{4,5},{5,4},{6,7},{7,6},{8,9},{9,8},{10,11... | collective-permute-start | bytes 393224 | tf_op jit(solution)/shard_map/ppermute | solution.py:21
  4.6 8.5 %collective-permute-start.3 = (f32[128,128]{1,0:T(8,128)S(1)}, f32[128,128]{1,0:T(8,128)S(1)}, u32[]{:S(2)}, u32[]{:S(2)}) collective-permute-start(f32[128,128]{1,0:T(8,128)S(1)} %fusion), channel_id=1, source_target_pairs={{0,8},{4,12},{8,0},{12,4},{1,9},{5,13},{9,1},{13,5},{2,10},{6,14},... | collective-permute-start | bytes 196616 | tf_op jit(solution)/shard_map/ppermute | solution.py:26
  8.6 10.5 %collective-permute-start.2 = (f32[2,128,128]{2,1,0:T(8,128)S(1)}, f32[2,128,128]{2,1,0:T(8,128)S(1)}, u32[]{:S(2)}, u32[]{:S(2)}) collective-permute-start(f32[2,128,128]{2,1,0:T(8,128)S(1)} %get-tuple-element.46), channel_id=1, source_target_pairs={{0,4},{4,0},{8,12},{12,8},{1,5},{5,1},{9,13},{13,9},{2,6},{6,2},{1... | collective-permute-start | bytes 393224 | tf_op jit(solution)/shard_map/ppermute | solution.py:26
  10.3 7.8 %collective-permute-start.6 = (f32[128,128]{1,0:T(8,128)S(1)}, f32[128,128]{1,0:T(8,128)S(1)}, u32[]{:S(2)}, u32[]{:S(2)}) collective-permute-start(f32[128,128]{1,0:T(8,128)S(1)} %bitcast.27), channel_id=1, source_target_pairs={{0,8},{4,12},{8,0},{12,4},{1,9},{5,13},{9,1},{13,5},{2,10},{6,14},... | collective-permute-start | bytes 196616 | tf_op jit(solution)/shard_map/ppermute | solution.py:26
  10.6 7.8 %collective-permute-start.5 = (f32[128,128]{1,0:T(8,128)S(1)}, f32[128,128]{1,0:T(8,128)S(1)}, u32[]{:S(2)}, u32[]{:S(2)}) collective-permute-start(f32[128,128]{1,0:T(8,128)S(1)} %bitcast.28), channel_id=1, source_target_pairs={{0,12},{4,8},{8,4},{12,0},{1,13},{5,9},{9,5},{13,1},{2,14},{6,10},... | collective-permute-start | bytes 196616 | tf_op jit(solution)/shard_map/ppermute | solution.py:26
  13.1 7.6 %collective-permute-start.7 = (f32[2,128,128]{2,1,0:T(8,128)S(1)}, f32[2,128,128]{2,1,0:T(8,128)S(1)}, u32[]{:S(2)}, u32[]{:S(2)}) collective-permute-start(f32[2,128,128]{2,1,0:T(8,128)S(1)} %get-tuple-element.55), channel_id=1, source_target_pairs={{0,1},{1,0},{2,3},{3,2},{4,5},{5,4},{6,7},{7,6},{8,9},{9,8},{10,11... | collective-permute-start | bytes 393224 | tf_op jit(solution)/shard_map/ppermute | solution.py:21
  13.1 6.0 %collective-permute-start.4 = (f32[1,128,128]{2,1,0:T(8,128)S(1)}, f32[1,128,128]{2,1,0:T(8,128)S(1)}, u32[]{:S(2)}, u32[]{:S(2)}) collective-permute-start(f32[1,128,128]{2,1,0:T(8,128)S(1)} %bitcast.33), channel_id=1, source_target_pairs={{0,4},{4,0},{8,12},{12,8},{1,5},{5,1},{9,13},{13,9},{2,6},{6,2},{1... | collective-permute-start | bytes 196616 | tf_op jit(solution)/shard_map/ppermute | solution.py:26
  19.2 1.5 %collective-permute-start.9 = (f32[2,1,128,128]{3,2,1,0:T(8,128)S(1)}, f32[2,1,128,128]{3,2,1,0:T(8,128)S(1)}, u32[]{:S(2)}, u32[]{:S(2)}) collective-permute-start(f32[2,1,128,128]{3,2,1,0:T(8,128)S(1)} %pad_maximum_fusion.group_ref), channel_id=1, source_target_pairs={{0,1},{1,0},{2,3},{3,2},{4,5},{5,4},{6,7},{7,6},{8,9},{9,8},{10,11... | collective-permute-start | bytes 393224 | tf_op jit(solution)/shard_map/ppermute | solution.py:21
  19.3 1.5 %collective-permute-start.8 = (f32[2,128,128]{2,1,0:T(8,128)S(1)}, f32[2,128,128]{2,1,0:T(8,128)S(1)}, u32[]{:S(2)}, u32[]{:S(2)}) collective-permute-start(f32[2,128,128]{2,1,0:T(8,128)S(1)} %collective-permute-done.2.pair_ref), channel_id=1, source_target_pairs={{0,1},{1,0},{2,3},{3,2},{4,5},{5,4},{6,7},{7,6},{8,9},{9,8},{10,11... | collective-permute-start | bytes 393224 | tf_op jit(solution)/shard_map/ppermute | solution.py:21

commit v8 on v7

--- a/solution.py
+++ b/solution.py
@@ -13,6 +13,7 @@
 TILE = 128
 CHUNKS = 2
 PARTS = 2
+FIRST = 160
 F32 = jnp.float32
 BF16 = jnp.bfloat16
 
@@ -86,25 +87,30 @@
             for sent in (True, False):
                 head = (1 - core if sent else core) * half + place
                 state = dot_tn(per_head_ref[pair[0], head], per_head_ref[pair[1], head])
+                low, high = place * state.shape[0], (place + 1) * state.shape[0]
                 if not sent:
-                    keep_ref[kind, place] = state
-                elif place == 0:
-                    send_a_ref[kind] = state
-                else:
-                    send_b_ref[kind, place - 1] = state
+                    keep_ref[kind, low:high] = state
+                    continue
+                cut = min(max(send_a_ref.shape[1], low), high)
+                if cut > low:
+                    send_a_ref[kind, low:cut] = state[: cut - low]
+                if cut < high:
+                    start = cut - send_a_ref.shape[1]
+                    send_b_ref[kind, start : start + high - cut] = state[cut - low :]
     table.wait()
 
 
 def states(flat, table):
     heads = table.shape[0]
     rows, width = flat[0].shape[0] // heads, flat[0].shape[1]
-    half = (2, heads // 2, width, width)
+    tall = heads // 2 * width
+    first = FIRST * width // 128
     return pl.pallas_call(
         functools.partial(state_kernel, heads),
         out_shape=(
-            jax.ShapeDtypeStruct((2, width, width), F32),
-            jax.ShapeDtypeStruct((2, heads // 2 - 1, width, width), F32),
-            jax.ShapeDtypeStruct(half, F32),
+            jax.ShapeDtypeStruct((2, first, width), F32),
+            jax.ShapeDtypeStruct((2, tall - first, width), F32),
+            jax.ShapeDtypeStruct((2, tall, width), F32),
             jax.ShapeDtypeStruct((4, heads, rows, width), BF16),
             jax.ShapeDtypeStruct(table.shape, F32),
         ),
@@ -217,9 +223,11 @@
     heads, rows = per_head_ref.shape[1:3]
     half = heads // 2
     chosen = [owner * half + place for place in range(half)]
+    width = pair_ref.shape[1]
+    spans = [slice(place * width, (place + 1) * width) for place in range(half)]
     states = [
-        far_states(table_ref, head, rows, near(place), pair_ref[place], [group_ref[place, bit] for bit in range(group_ref.shape[1])])
-        for place, head in enumerate(chosen)
+        far_states(table_ref, head, rows, near(span), pair_ref[span], [group_ref[bit, span] for bit in range(group_ref.shape[0])])
+        for head, span in zip(chosen, spans)
     ]
     part = rows // parts
     for which, source in enumerate((0, 3, 2, 1)):
@@ -235,7 +243,7 @@
 
 def own_kernel(table_ref, per_head_ref, local_ref, received_a_ref, received_b_ref, pair_ref, group_ref, wide_ref):
     core = lax.axis_index("rep")
-    far_heads(core, table_ref, per_head_ref, local_ref, lambda place: received_b_ref[1 - core, place - 1] if place else received_a_ref[1 - core],
+    far_heads(core, table_ref, per_head_ref, local_ref, lambda span: jnp.concatenate([received_a_ref[1 - core], received_b_ref[1 - core]], 0)[span],
               pair_ref, group_ref, wide_ref)
 
 
@@ -249,7 +257,7 @@
         copy.start()
         copies.append(copy)
 
-    far_heads(1 - lax.axis_index("rep"), table_ref, per_head_ref, local_ref, lambda place: near_ref[place],
+    far_heads(1 - lax.axis_index("rep"), table_ref, per_head_ref, local_ref, lambda span: near_ref[span],
               pair_ref, group_ref, wide_ref, finish, PARTS)
     for copy in copies:
         copy.wait()
@@ -288,19 +296,20 @@
 
 def load_kernel(keep_ref, received_a_ref, received_b_ref, pair_ref, rest_ref, near_ref):
     core, chip = lax.axis_index("rep"), lax.axis_index("seq")
+    first = received_a_ref.shape[1]
     kind = chip % 2
-    pair_ref[0] = keep_ref[kind, 0] + received_a_ref[kind]
-    pair_ref[1:] = keep_ref[kind, 1:] + received_b_ref[kind]
+    pair_ref[:first] = keep_ref[kind, :first] + received_a_ref[kind]
+    pair_ref[first:] = keep_ref[kind, first:] + received_b_ref[kind]
     for bit in range(rest_ref.shape[0]):
         kind = (chip >> (bit + 1)) % 2
-        rest_ref[bit] = keep_ref[kind, 1] + received_b_ref[kind, 0]
+        rest_ref[bit] = keep_ref[kind, first:] + received_b_ref[kind]
     near_ref[...] = keep_ref[core]
 
 
 def loads_of(bits, keep, *received):
     vmem = pl.BlockSpec(memory_space=pltpu.VMEM)
-    half, width = keep.shape[1], keep.shape[2]
-    shapes = ((half, width, width), (bits - 1, width, width), (half, width, width))
+    tall, width = keep.shape[1:]
+    shapes = ((tall, width), (bits - 1, received[1].shape[1], width), (tall, width))
     return pl.pallas_call(
         load_kernel,
         out_shape=[jax.ShapeDtypeStruct(shape, F32) for shape in shapes],
@@ -322,8 +331,9 @@
     received_a, received_b = swap_cores(send_a), swap_cores(send_b)
     local_a = local_part([(0, (0,))], 10**9, table, per_head)
     received_a, per_head, local_a = lax.optimization_barrier((received_a, per_head, local_a))
+    first_rows = received_a.shape[1]
     first = [
-        jnp.where((chip >> bit) % 2 == 1, keep[1, 0] + received_a[1], keep[0, 0] + received_a[0])
+        jnp.where((chip >> bit) % 2 == 1, keep[1, :first_rows] + received_a[1], keep[0, :first_rows] + received_a[0])
         for bit in range(1, bits)
     ]
     first, keep, received_a = lax.optimization_barrier((first, keep, received_a))
@@ -343,7 +353,7 @@
     local_b = local_part([(0, (1,))] + [(head, (0, 1)) for head in range(1, heads)], 10**9, table, held, local_a)
     pair, hop, group_b, local_b = lax.optimization_barrier((pair, hop, group_b, local_b))
     pair_o = swap_cores(pair)
-    group = jnp.stack([half_way + hop, jnp.stack([sum(pieces) for pieces in group_b])])
+    group = jnp.concatenate([half_way + hop, jnp.stack([sum(pieces) for pieces in group_b])], 1)
     group_o = swap_cores(group)
     wide = own_part(table, per_head, local_b, received_a, received_b, pair, group)
     return last_part(table, per_head, local_b, near, pair_o, group_o, wide)

time: 23 us -> 22.7 us (0.987)
  waiting for transfers between devices: 2.59 us -> 2.01 us
    ppermute x5, waiting for transfers between devices: 2.2 us -> 1.57 us  [swap_chips(): lax.ppermute(block, 'seq', [(chip, chip ^ mask) for chip in range(count)])]
  transfers between devices with their start and end apart: 10 -> 10, of which waited for: 5 -> 4; matrix products, arithmetic and copies ran while one was open for 0% -> 0% of each run, Pallas kernels for 21% -> 21%
where the time goes in v8:
time: 22.7 us; the launch traced here: 22.5 us
  starting transfers between devices  10.5 us (46%)
  Pallas kernels  9.23 us (41%)
  waiting for transfers between devices  2.01 us (9%)
  between operations  0.73 us (3%)
    ppermute x5, starting transfers between devices, swap_chips(): lax.ppermute(block, 'seq', [(chip, chip ^ mask) for chip in range(count)])  9.33 us
    pallas_call x2, Pallas kernels, local_part(): pl.pallas_call(functools.partial(local_kernel, chosen), out_shape=jax.Sha...  3.83 us
    pallas_call x1, Pallas kernels, states(): pl.pallas_call(functools.partial(state_kernel, heads), out_shape=(jax.Sha...  2.43 us
    pallas_call x1, Pallas kernels, last_part(): pl.pallas_call(last_kernel, out_shape=[jax.ShapeDtypeStruct((rows * heads...  2.09 us
    ppermute x5, waiting for transfers between devices, swap_chips(): lax.ppermute(block, 'seq', [(chip, chip ^ mask) for chip in range(count)])  1.57 us
    ppermute x5, starting transfers between devices, swap_cores(): return lax.ppermute(block, 'rep', [(0, 1), (1, 0)])  1.16 us
    pallas_call x1, Pallas kernels, own_part(): pl.pallas_call(own_kernel, out_shape=jax.ShapeDtypeStruct((4, rows * head...  0.86 us
  transfers between devices with their start and end apart: 10, of which 4 were waited for; matrix products, arithmetic and copies ran while one was open for 0% of the time, Pallas kernels for 21%

profile of v8, /device:TPU:0, one launch (start us, length us, event | category | flops | bytes accessed | tf_op | source)
XLA Modules:
  0.0 22.5 jit_solution(15395278677975014461)
XLA Ops:
  0.6 2.4 %states.1 = (f32[2,160,128]{2,1,0:T(8,128)S(1)}, f32[2,96,128]{2,1,0:T(8,128)S(1)}, f32[2,256,128]{2,1,0:T(8,128)S(1)}, bf16[4,4,512,128]{3,2,1,0:T(8,128)(2,1)S(1)}, f32[4,7]{1,0:T(4,128)S(1)}) custom-call(bf16[2048,128]{1,0:T(8,128)(2,1)} %bitcast.17, bf16[2048,128]{1,0:T(8,128)(2,1)} %bitcast.18, bf16[2048,128]{1,0:T(8,128)(2,1)} %bitcast.19, ...), custom_call_target="tpu_custom_call" | custom-call | tf_op jit(solution)/shard_map/states/pallas_call | solution.py:108
  3.1 0.5 %collective-permute-start = (f32[2,160,128]{2,1,0:T(8,128)S(1)}, f32[2,160,128]{2,1,0:T(8,128)S(1)}, u32[]{:S(2)}, u32[]{:S(2)}) collective-permute-start(f32[2,160,128]{2,1,0:T(8,128)S(1)} %get-tuple-element.35), channel_id=1, source_target_pairs={{0,1},{1,0},{2,3},{3,2},{4,5},{5,4},{6,7},{7,6},{8,9},{9,8},{10,11... | collective-permute-start | bytes 491528 | tf_op jit(solution)/shard_map/ppermute | solution.py:22
  3.6 0.1 collective-permute-start.1
  3.7 0.6 %local.2.refs_0_ = f32[4,4,512,128]{3,2,1,0:T(8,128)S(1)} custom-call(f32[4,7]{1,0:T(4,128)S(1)} %get-tuple-element.34.table_ref, bf16[4,4,512,128]{3,2,1,0:T(8,128)(2,1)S(1)} %get-tuple-element.52.per_head_ref), custom_call_target="tpu_custom_call" | custom-call | flops 1000000000 | bytes 1000000 | tf_op jit(solution)/shard_map/local/pallas_call | solution.py:198
  4.3 0.3 %collective-permute-done.received_a_ref = f32[2,160,128]{2,1,0:T(8,128)S(1)} collective-permute-done((f32[2,160,128]{2,1,0:T(8,128)S(1)}, f32[2,160,128]{2,1,0:T(8,128)S(1)}, u32[]{:S(2)}, u32[]{:S(2)}) %collective-permute-start) | collective-permute-done | bytes 163872 | tf_op jit(solution)/shard_map/ppermute | solution.py:22
  4.6 4.0 %collective-permute-start.3 = (f32[160,128]{1,0:T(8,128)S(1)}, f32[160,128]{1,0:T(8,128)S(1)}, u32[]{:S(2)}, u32[]{:S(2)}) collective-permute-start(f32[160,128]{1,0:T(8,128)S(1)} %select_bitcast_fusion), channel_id=1, source_target_pairs={{0,8},{4,12},{8,0},{12,4},{1,9},{5,13},{9,1},{13,5},{2,10},{6,14},... | collective-permute-start | bytes 245768 | tf_op jit(solution)/shard_map/ppermute | solution.py:27
  8.7 0.0 collective-permute-done.1.received_b_ref
  8.7 1.6 %collective-permute-start.2 = (f32[256,128]{1,0:T(8,128)S(1)}, f32[256,128]{1,0:T(8,128)S(1)}, u32[]{:S(2)}, u32[]{:S(2)}) collective-permute-start(f32[256,128]{1,0:T(8,128)S(1)} %get-tuple-element.46), channel_id=1, source_target_pairs={{0,4},{4,0},{8,12},{12,8},{1,5},{5,1},{9,13},{13,9},{2,6},{6,2},{1... | collective-permute-start | bytes 393224 | tf_op jit(solution)/shard_map/ppermute | solution.py:27
  10.3 0.3 %collective-permute-start.6 = (f32[96,128]{1,0:T(8,128)S(1)}, f32[96,128]{1,0:T(8,128)S(1)}, u32[]{:S(2)}, u32[]{:S(2)}) collective-permute-start(f32[96,128]{1,0:T(8,128)S(1)} %bitcast.15), channel_id=1, source_target_pairs={{0,8},{4,12},{8,0},{12,4},{1,9},{5,13},{9,1},{13,5},{2,10},{6,14},... | collective-permute-start | bytes 147464 | tf_op jit(solution)/shard_map/ppermute | solution.py:27
  10.7 2.5 %collective-permute-start.5 = (f32[96,128]{1,0:T(8,128)S(1)}, f32[96,128]{1,0:T(8,128)S(1)}, u32[]{:S(2)}, u32[]{:S(2)}) collective-permute-start(f32[96,128]{1,0:T(8,128)S(1)} %bitcast.16), channel_id=1, source_target_pairs={{0,12},{4,8},{8,4},{12,0},{1,13},{5,9},{9,5},{13,1},{2,14},{6,10},... | collective-permute-start | bytes 147464 | tf_op jit(solution)/shard_map/ppermute | solution.py:27
  13.1 0.0 collective-permute-start.7
  13.1 0.0 collective-permute-done.3
  13.2 0.8 %collective-permute-start.4 = (f32[1,160,128]{2,1,0:T(8,128)S(1)}, f32[1,160,128]{2,1,0:T(8,128)S(1)}, u32[]{:S(2)}, u32[]{:S(2)}) collective-permute-start(f32[1,160,128]{2,1,0:T(8,128)S(1)} %bitcast.21), channel_id=1, source_target_pairs={{0,4},{4,0},{8,12},{12,8},{1,5},{5,1},{9,13},{13,9},{2,6},{6,2},{1... | collective-permute-start | bytes 245768 | tf_op jit(solution)/shard_map/ppermute | solution.py:27
  14.0 3.2 %local.3.local_ref = f32[4,4,512,128]{3,2,1,0:T(8,128)S(1)} custom-call(f32[4,7]{1,0:T(4,128)S(1)} %get-tuple-element.34.table_ref, bf16[4,4,512,128]{3,2,1,0:T(8,128)(2,1)S(1)} %get-tuple-element.52.per_head_ref, f32[4,4,512,128]{3,2,1,0:T(8,128)S(1)} %local.2.refs_0_), custom_call_target="tpu_custom_call", output_to_operand_aliasing={{}: (2, {})} | custom-call | flops 1000000000 | bytes 1000000 | tf_op jit(solution)/shard_map/local/pallas_call | solution.py:198
  17.2 0.0 collective-permute-done.6
  17.2 0.4 %collective-permute-done.5 = f32[96,128]{1,0:T(8,128)S(1)} collective-permute-done((f32[96,128]{1,0:T(8,128)S(1)}, f32[96,128]{1,0:T(8,128)S(1)}, u32[]{:S(2)}, u32[]{:S(2)}) %collective-permute-start.5) | collective-permute-done | bytes 49184 | tf_op jit(solution)/shard_map/ppermute | solution.py:27
  17.6 0.0 collective-permute-done.2.pair_ref
  17.6 1.1 %collective-permute-done.4 = f32[1,160,128]{2,1,0:T(8,128)S(1)} collective-permute-done((f32[1,160,128]{2,1,0:T(8,128)S(1)}, f32[1,160,128]{2,1,0:T(8,128)S(1)}, u32[]{:S(2)}, u32[]{:S(2)}) %collective-permute-start.4) | collective-permute-done | bytes 81952 | tf_op jit(solution)/shard_map/ppermute | solution.py:27
  18.8 0.1 collective-permute-start.9
  18.9 0.5 %collective-permute-start.8 = (f32[256,128]{1,0:T(8,128)S(1)}, f32[256,128]{1,0:T(8,128)S(1)}, u32[]{:S(2)}, u32[]{:S(2)}) collective-permute-start(f32[256,128]{1,0:T(8,128)S(1)} %collective-permute-done.2.pair_ref), channel_id=1, source_target_pairs={{0,1},{1,0},{2,3},{3,2},{4,5},{5,4},{6,7},{7,6},{8,9},{9,8},{10,11... | collective-permute-start | bytes 393224 | tf_op jit(solution)/shard_map/ppermute | solution.py:22
  19.4 0.9 %own.1._ = f32[4,2048,128]{2,1,0:T(8,128)S(1)} custom-call(f32[4,7]{1,0:T(4,128)S(1)} %get-tuple-element.34.table_ref, bf16[4,4,512,128]{3,2,1,0:T(8,128)(2,1)S(1)} %get-tuple-element.52.per_head_ref, f32[4,4,512,128]{3,2,1,0:T(8,128)S(1)} %local.3.local_ref, f32[2,160,128]{2,1,0:T(8,128)S(1)} %collective-permute-done.received_a_ref, ...), custom_call_target="tpu_custom_call" | custom-call | flops 1000000000 | bytes 3145728 | tf_op jit(solution)/shard_map/own/pallas_call | solution.py:269
  20.3 0.0 collective-permute-done.7.near_ref
  20.3 0.0 collective-permute-done.9.group_ref
  20.3 0.1 collective-permute-done.8.pair_ref
  20.4 2.1 %last.1 = (bf16[2048,128]{1,0:T(8,128)(2,1)}, bf16[2048,128]{1,0:T(8,128)(2,1)}, bf16[2048,128]{1,0:T(8,128)(2,1)}, bf16[2048,128]{1,0:T(8,128)(2,1)}, f32[4,2048,128]{2,1,0:T(8,128)S(1)}) custom-call(f32[4,7]{1,0:T(4,128)S(1)} %get-tuple-element.34.table_ref, ...), custom_call_target="tpu_custom_call", output_to_operand_aliasing={{4}: (6, {})} | custom-call | tf_op jit(solution)/shard_map/last/pallas_call | solution.py:284
  (5 shorter events, 0.1 us)
Async XLA Ops:
  3.1 1.5 %collective-permute-start = (f32[2,160,128]{2,1,0:T(8,128)S(1)}, f32[2,160,128]{2,1,0:T(8,128)S(1)}, u32[]{:S(2)}, u32[]{:S(2)}) collective-permute-start(f32[2,160,128]{2,1,0:T(8,128)S(1)} %get-tuple-element.35), channel_id=1, source_target_pairs={{0,1},{1,0},{2,3},{3,2},{4,5},{5,4},{6,7},{7,6},{8,9},{9,8},{10,11... | collective-permute-start | bytes 491528 | tf_op jit(solution)/shard_map/ppermute | solution.py:22
  3.6 5.1 %collective-permute-start.1 = (f32[2,96,128]{2,1,0:T(8,128)S(1)}, f32[2,96,128]{2,1,0:T(8,128)S(1)}, u32[]{:S(2)}, u32[]{:S(2)}) collective-permute-start(f32[2,96,128]{2,1,0:T(8,128)S(1)} %get-tuple-element.42), channel_id=1, source_target_pairs={{0,1},{1,0},{2,3},{3,2},{4,5},{5,4},{6,7},{7,6},{8,9},{9,8},{10,11... | collective-permute-start | bytes 294920 | tf_op jit(solution)/shard_map/ppermute | solution.py:22
  4.6 8.5 %collective-permute-start.3 = (f32[160,128]{1,0:T(8,128)S(1)}, f32[160,128]{1,0:T(8,128)S(1)}, u32[]{:S(2)}, u32[]{:S(2)}) collective-permute-start(f32[160,128]{1,0:T(8,128)S(1)} %select_bitcast_fusion), channel_id=1, source_target_pairs={{0,8},{4,12},{8,0},{12,4},{1,9},{5,13},{9,1},{13,5},{2,10},{6,14},... | collective-permute-start | bytes 245768 | tf_op jit(solution)/shard_map/ppermute | solution.py:27
  8.7 8.9 %collective-permute-start.2 = (f32[256,128]{1,0:T(8,128)S(1)}, f32[256,128]{1,0:T(8,128)S(1)}, u32[]{:S(2)}, u32[]{:S(2)}) collective-permute-start(f32[256,128]{1,0:T(8,128)S(1)} %get-tuple-element.46), channel_id=1, source_target_pairs={{0,4},{4,0},{8,12},{12,8},{1,5},{5,1},{9,13},{13,9},{2,6},{6,2},{1... | collective-permute-start | bytes 393224 | tf_op jit(solution)/shard_map/ppermute | solution.py:27
  10.3 6.9 %collective-permute-start.6 = (f32[96,128]{1,0:T(8,128)S(1)}, f32[96,128]{1,0:T(8,128)S(1)}, u32[]{:S(2)}, u32[]{:S(2)}) collective-permute-start(f32[96,128]{1,0:T(8,128)S(1)} %bitcast.15), channel_id=1, source_target_pairs={{0,8},{4,12},{8,0},{12,4},{1,9},{5,13},{9,1},{13,5},{2,10},{6,14},... | collective-permute-start | bytes 147464 | tf_op jit(solution)/shard_map/ppermute | solution.py:27
  10.7 7.0 %collective-permute-start.5 = (f32[96,128]{1,0:T(8,128)S(1)}, f32[96,128]{1,0:T(8,128)S(1)}, u32[]{:S(2)}, u32[]{:S(2)}) collective-permute-start(f32[96,128]{1,0:T(8,128)S(1)} %bitcast.16), channel_id=1, source_target_pairs={{0,12},{4,8},{8,4},{12,0},{1,13},{5,9},{9,5},{13,1},{2,14},{6,10},... | collective-permute-start | bytes 147464 | tf_op jit(solution)/shard_map/ppermute | solution.py:27
  13.1 7.1 %collective-permute-start.7 = (f32[256,128]{1,0:T(8,128)S(1)}, f32[256,128]{1,0:T(8,128)S(1)}, u32[]{:S(2)}, u32[]{:S(2)}) collective-permute-start(f32[256,128]{1,0:T(8,128)S(1)} %get-tuple-element.55), channel_id=1, source_target_pairs={{0,1},{1,0},{2,3},{3,2},{4,5},{5,4},{6,7},{7,6},{8,9},{9,8},{10,11... | collective-permute-start | bytes 393224 | tf_op jit(solution)/shard_map/ppermute | solution.py:22
  13.2 5.6 %collective-permute-start.4 = (f32[1,160,128]{2,1,0:T(8,128)S(1)}, f32[1,160,128]{2,1,0:T(8,128)S(1)}, u32[]{:S(2)}, u32[]{:S(2)}) collective-permute-start(f32[1,160,128]{2,1,0:T(8,128)S(1)} %bitcast.21), channel_id=1, source_target_pairs={{0,4},{4,0},{8,12},{12,8},{1,5},{5,1},{9,13},{13,9},{2,6},{6,2},{1... | collective-permute-start | bytes 245768 | tf_op jit(solution)/shard_map/ppermute | solution.py:27
  18.8 1.5 %collective-permute-start.9 = (f32[1,256,128]{2,1,0:T(8,128)S(1)}, f32[1,256,128]{2,1,0:T(8,128)S(1)}, u32[]{:S(2)}, u32[]{:S(2)}) collective-permute-start(f32[1,256,128]{2,1,0:T(8,128)S(1)} %pad_maximum_fusion.group_ref), channel_id=1, source_target_pairs={{0,1},{1,0},{2,3},{3,2},{4,5},{5,4},{6,7},{7,6},{8,9},{9,8},{10,11... | collective-permute-start | bytes 393224 | tf_op jit(solution)/shard_map/ppermute | solution.py:22
  18.9 1.5 %collective-permute-start.8 = (f32[256,128]{1,0:T(8,128)S(1)}, f32[256,128]{1,0:T(8,128)S(1)}, u32[]{:S(2)}, u32[]{:S(2)}) collective-permute-start(f32[256,128]{1,0:T(8,128)S(1)} %collective-permute-done.2.pair_ref), channel_id=1, source_target_pairs={{0,1},{1,0},{2,3},{3,2},{4,5},{5,4},{6,7},{7,6},{8,9},{9,8},{10,11... | collective-permute-start | bytes 393224 | tf_op jit(solution)/shard_map/ppermute | solution.py:22

commit v9 on v8

--- a/solution.py
+++ b/solution.py
@@ -207,7 +207,7 @@
     )(table, per_head, *earlier)
 
 
-def far_states(table_ref, head, rows, near, pair, groups):
+def far_states(table_ref, head, rows, near, pair, *groups):
     core, chip = lax.axis_index("rep"), lax.axis_index("seq")
     terms = [(core == 1, near), (chip % 2 == 1, pair)]
     terms += [((chip >> bit) % 2 == 1, group) for bit, group in enumerate(groups, 1)]
@@ -219,14 +219,14 @@
     return [jnp.concatenate(split(state), 0) for state in (keys_far, keys_far.T, queries_far.T, queries_far)]
 
 
-def far_heads(owner, table_ref, per_head_ref, local_ref, near, pair_ref, group_ref, wide_ref, finish=None, parts=1):
+def far_heads(owner, table_ref, per_head_ref, local_ref, near, far_ref, wide_ref, finish=None, parts=1):
     heads, rows = per_head_ref.shape[1:3]
     half = heads // 2
     chosen = [owner * half + place for place in range(half)]
-    width = pair_ref.shape[1]
+    width = far_ref.shape[2]
     spans = [slice(place * width, (place + 1) * width) for place in range(half)]
     states = [
-        far_states(table_ref, head, rows, near(span), pair_ref[span], [group_ref[bit, span] for bit in range(group_ref.shape[0])])
+        far_states(table_ref, head, rows, near(span), *[far_ref[bit, span] for bit in range(far_ref.shape[0])])
         for head, span in zip(chosen, spans)
     ]
     part = rows // parts
@@ -241,13 +241,13 @@
                 finish(which, pl.ds(piece * part * heads, part * heads))
 
 
-def own_kernel(table_ref, per_head_ref, local_ref, received_a_ref, received_b_ref, pair_ref, group_ref, wide_ref):
+def own_kernel(table_ref, per_head_ref, local_ref, received_a_ref, received_b_ref, far_ref, wide_ref):
     core = lax.axis_index("rep")
     far_heads(core, table_ref, per_head_ref, local_ref, lambda span: jnp.concatenate([received_a_ref[1 - core], received_b_ref[1 - core]], 0)[span],
-              pair_ref, group_ref, wide_ref)
-
-
-def last_kernel(table_ref, per_head_ref, local_ref, near_ref, pair_ref, group_ref, _, *refs):
+              far_ref, wide_ref)
+
+
+def last_kernel(table_ref, per_head_ref, local_ref, near_ref, far_ref, _, *refs):
     out_refs, (wide_ref, narrow, left) = refs[:4], refs[4:]
     copies = []
 
@@ -258,7 +258,7 @@
         copies.append(copy)
 
     far_heads(1 - lax.axis_index("rep"), table_ref, per_head_ref, local_ref, lambda span: near_ref[span],
-              pair_ref, group_ref, wide_ref, finish, PARTS)
+              far_ref, wide_ref, finish, PARTS)
     for copy in copies:
         copy.wait()
 
@@ -352,11 +352,11 @@
     hop = swap_chips(half_way, 1)
     local_b = local_part([(0, (1,))] + [(head, (0, 1)) for head in range(1, heads)], 10**9, table, held, local_a)
     pair, hop, group_b, local_b = lax.optimization_barrier((pair, hop, group_b, local_b))
-    pair_o = swap_cores(pair)
     group = jnp.concatenate([half_way + hop, jnp.stack([sum(pieces) for pieces in group_b])], 1)
-    group_o = swap_cores(group)
-    wide = own_part(table, per_head, local_b, received_a, received_b, pair, group)
-    return last_part(table, per_head, local_b, near, pair_o, group_o, wide)
+    far = jnp.concatenate([pair[None], group])
+    far_o = swap_cores(far)
+    wide = own_part(table, per_head, local_b, received_a, received_b, far)
+    return last_part(table, per_head, local_b, near, far_o, wide)
 
 
 def solution(mesh):

time: 22.7 us -> 22.6 us (level)
    ppermute x5, waiting for transfers between devices: 1.57 us -> 1.28 us  [swap_chips(): lax.ppermute(block, 'seq', [(chip, chip ^ mask) for chip in range(count)])]
    ppermute x5 -> x4, waiting for transfers between devices: 0.44 us -> 0.64 us  [swap_cores(): return lax.ppermute(block, 'rep', [(0, 1), (1, 0)])]
    ppermute x5 -> x4, starting transfers between devices: 1.16 us -> 1.15 us  [swap_cores(): return lax.ppermute(block, 'rep', [(0, 1), (1, 0)])]
  transfers between devices with their start and end apart: 10 -> 9, of which waited for: 4 -> 4; matrix products, arithmetic and copies ran while one was open for 0% -> 0% of each run, Pallas kernels for 21% -> 21%
where the time goes in v9:
time: 22.6 us; the launch traced here: 22.4 us
  starting transfers between devices  10.5 us (46%)
  Pallas kernels  9.24 us (41%)
  waiting for transfers between devices  1.93 us (9%)
  between operations  0.71 us (3%)
    ppermute x5, starting transfers between devices, swap_chips(): lax.ppermute(block, 'seq', [(chip, chip ^ mask) for chip in range(count)])  9.33 us
    pallas_call x2, Pallas kernels, local_part(): pl.pallas_call(functools.partial(local_kernel, chosen), out_shape=jax.Sha...  3.83 us
    pallas_call x1, Pallas kernels, states(): pl.pallas_call(functools.partial(state_kernel, heads), out_shape=(jax.Sha...  2.43 us
    pallas_call x1, Pallas kernels, last_part(): pl.pallas_call(last_kernel, out_shape=[jax.ShapeDtypeStruct((rows * heads...  2.09 us
    ppermute x5, waiting for transfers between devices, swap_chips(): lax.ppermute(block, 'seq', [(chip, chip ^ mask) for chip in range(count)])  1.28 us
    ppermute x4, starting transfers between devices, swap_cores(): return lax.ppermute(block, 'rep', [(0, 1), (1, 0)])  1.15 us
    pallas_call x1, Pallas kernels, own_part(): pl.pallas_call(own_kernel, out_shape=jax.ShapeDtypeStruct((4, rows * head...  0.86 us
    ppermute x4, waiting for transfers between devices, swap_cores(): return lax.ppermute(block, 'rep', [(0, 1), (1, 0)])  0.64 us
  transfers between devices with their start and end apart: 9, of which 4 were waited for; matrix products, arithmetic and copies ran while one was open for 0% of the time, Pallas kernels for 21%

profile of v9, /device:TPU:0, one launch (start us, length us, event | category | flops | bytes accessed | tf_op | source)
XLA Modules:
  0.0 22.4 jit_solution(17949412248998090886)
XLA Ops:
  0.6 2.4 %states.1 = (f32[2,160,128]{2,1,0:T(8,128)S(1)}, f32[2,96,128]{2,1,0:T(8,128)S(1)}, f32[2,256,128]{2,1,0:T(8,128)S(1)}, bf16[4,4,512,128]{3,2,1,0:T(8,128)(2,1)S(1)}, f32[4,7]{1,0:T(4,128)S(1)}) custom-call(bf16[2048,128]{1,0:T(8,128)(2,1)} %bitcast.18, bf16[2048,128]{1,0:T(8,128)(2,1)} %bitcast.19, bf16[2048,128]{1,0:T(8,128)(2,1)} %bitcast.20, ...), custom_call_target="tpu_custom_call" | custom-call | tf_op jit(solution)/shard_map/states/pallas_call | solution.py:108
  3.1 0.5 %collective-permute-start = (f32[2,160,128]{2,1,0:T(8,128)S(1)}, f32[2,160,128]{2,1,0:T(8,128)S(1)}, u32[]{:S(2)}, u32[]{:S(2)}) collective-permute-start(f32[2,160,128]{2,1,0:T(8,128)S(1)} %get-tuple-element.35), channel_id=1, source_target_pairs={{0,1},{1,0},{2,3},{3,2},{4,5},{5,4},{6,7},{7,6},{8,9},{9,8},{10,11... | collective-permute-start | bytes 491528 | tf_op jit(solution)/shard_map/ppermute | solution.py:22
  3.6 0.1 collective-permute-start.1
  3.7 0.6 %local.2.refs_0_ = f32[4,4,512,128]{3,2,1,0:T(8,128)S(1)} custom-call(f32[4,7]{1,0:T(4,128)S(1)} %get-tuple-element.34.table_ref, bf16[4,4,512,128]{3,2,1,0:T(8,128)(2,1)S(1)} %get-tuple-element.52.per_head_ref), custom_call_target="tpu_custom_call" | custom-call | flops 1000000000 | bytes 1000000 | tf_op jit(solution)/shard_map/local/pallas_call | solution.py:198
  4.3 0.3 %collective-permute-done.received_a_ref = f32[2,160,128]{2,1,0:T(8,128)S(1)} collective-permute-done((f32[2,160,128]{2,1,0:T(8,128)S(1)}, f32[2,160,128]{2,1,0:T(8,128)S(1)}, u32[]{:S(2)}, u32[]{:S(2)}) %collective-permute-start) | collective-permute-done | bytes 163872 | tf_op jit(solution)/shard_map/ppermute | solution.py:22
  4.6 4.0 %collective-permute-start.3 = (f32[160,128]{1,0:T(8,128)S(1)}, f32[160,128]{1,0:T(8,128)S(1)}, u32[]{:S(2)}, u32[]{:S(2)}) collective-permute-start(f32[160,128]{1,0:T(8,128)S(1)} %select_bitcast_fusion), channel_id=1, source_target_pairs={{0,8},{4,12},{8,0},{12,4},{1,9},{5,13},{9,1},{13,5},{2,10},{6,14},... | collective-permute-start | bytes 245768 | tf_op jit(solution)/shard_map/ppermute | solution.py:27
  8.7 0.0 collective-permute-done.1.received_b_ref
  8.7 1.6 %collective-permute-start.2 = (f32[256,128]{1,0:T(8,128)S(1)}, f32[256,128]{1,0:T(8,128)S(1)}, u32[]{:S(2)}, u32[]{:S(2)}) collective-permute-start(f32[256,128]{1,0:T(8,128)S(1)} %get-tuple-element.46), channel_id=1, source_target_pairs={{0,4},{4,0},{8,12},{12,8},{1,5},{5,1},{9,13},{13,9},{2,6},{6,2},{1... | collective-permute-start | bytes 393224 | tf_op jit(solution)/shard_map/ppermute | solution.py:27
  10.3 0.3 %collective-permute-start.6 = (f32[96,128]{1,0:T(8,128)S(1)}, f32[96,128]{1,0:T(8,128)S(1)}, u32[]{:S(2)}, u32[]{:S(2)}) collective-permute-start(f32[96,128]{1,0:T(8,128)S(1)} %bitcast.16), channel_id=1, source_target_pairs={{0,8},{4,12},{8,0},{12,4},{1,9},{5,13},{9,1},{13,5},{2,10},{6,14},... | collective-permute-start | bytes 147464 | tf_op jit(solution)/shard_map/ppermute | solution.py:27
  10.7 2.5 %collective-permute-start.5 = (f32[96,128]{1,0:T(8,128)S(1)}, f32[96,128]{1,0:T(8,128)S(1)}, u32[]{:S(2)}, u32[]{:S(2)}) collective-permute-start(f32[96,128]{1,0:T(8,128)S(1)} %bitcast.17), channel_id=1, source_target_pairs={{0,12},{4,8},{8,4},{12,0},{1,13},{5,9},{9,5},{13,1},{2,14},{6,10},... | collective-permute-start | bytes 147464 | tf_op jit(solution)/shard_map/ppermute | solution.py:27
  13.1 0.0 collective-permute-done.3
  13.1 0.9 %collective-permute-start.4 = (f32[1,160,128]{2,1,0:T(8,128)S(1)}, f32[1,160,128]{2,1,0:T(8,128)S(1)}, u32[]{:S(2)}, u32[]{:S(2)}) collective-permute-start(f32[1,160,128]{2,1,0:T(8,128)S(1)} %bitcast.23), channel_id=1, source_target_pairs={{0,4},{4,0},{8,12},{12,8},{1,5},{5,1},{9,13},{13,9},{2,6},{6,2},{1... | collective-permute-start | bytes 245768 | tf_op jit(solution)/shard_map/ppermute | solution.py:27
  14.0 3.2 %local.3.local_ref = f32[4,4,512,128]{3,2,1,0:T(8,128)S(1)} custom-call(f32[4,7]{1,0:T(4,128)S(1)} %get-tuple-element.34.table_ref, bf16[4,4,512,128]{3,2,1,0:T(8,128)(2,1)S(1)} %get-tuple-element.52.per_head_ref, f32[4,4,512,128]{3,2,1,0:T(8,128)S(1)} %local.2.refs_0_), custom_call_target="tpu_custom_call", output_to_operand_aliasing={{}: (2, {})} | custom-call | flops 1000000000 | bytes 1000000 | tf_op jit(solution)/shard_map/local/pallas_call | solution.py:198
  17.2 0.0 collective-permute-done.6
  17.2 0.4 %collective-permute-done.5 = f32[96,128]{1,0:T(8,128)S(1)} collective-permute-done((f32[96,128]{1,0:T(8,128)S(1)}, f32[96,128]{1,0:T(8,128)S(1)}, u32[]{:S(2)}, u32[]{:S(2)}) %collective-permute-start.5) | collective-permute-done | bytes 49184 | tf_op jit(solution)/shard_map/ppermute | solution.py:27
  17.6 0.0 collective-permute-done.2
  17.6 0.9 %collective-permute-done.4 = f32[1,160,128]{2,1,0:T(8,128)S(1)} collective-permute-done((f32[1,160,128]{2,1,0:T(8,128)S(1)}, f32[1,160,128]{2,1,0:T(8,128)S(1)}, u32[]{:S(2)}, u32[]{:S(2)}) %collective-permute-start.4) | collective-permute-done | bytes 81952 | tf_op jit(solution)/shard_map/ppermute | solution.py:27
  18.5 0.1 collective-permute-start.8
  18.6 0.5 %collective-permute-start.7 = (f32[256,128]{1,0:T(8,128)S(1)}, f32[256,128]{1,0:T(8,128)S(1)}, u32[]{:S(2)}, u32[]{:S(2)}) collective-permute-start(f32[256,128]{1,0:T(8,128)S(1)} %get-tuple-element.55), channel_id=1, source_target_pairs={{0,1},{1,0},{2,3},{3,2},{4,5},{5,4},{6,7},{7,6},{8,9},{9,8},{10,11... | collective-permute-start | bytes 393224 | tf_op jit(solution)/shard_map/ppermute | solution.py:22
  19.1 0.9 %own.1._ = f32[4,2048,128]{2,1,0:T(8,128)S(1)} custom-call(f32[4,7]{1,0:T(4,128)S(1)} %get-tuple-element.34.table_ref, bf16[4,4,512,128]{3,2,1,0:T(8,128)(2,1)S(1)} %get-tuple-element.52.per_head_ref, f32[4,4,512,128]{3,2,1,0:T(8,128)S(1)} %local.3.local_ref, f32[2,160,128]{2,1,0:T(8,128)S(1)} %collective-permute-done.received_a_ref, ...), custom_call_target="tpu_custom_call" | custom-call | flops 1000000000 | bytes 3145728 | tf_op jit(solution)/shard_map/own/pallas_call | solution.py:269
  20.0 0.3 %collective-permute-done.7.near_ref = f32[256,128]{1,0:T(8,128)S(1)} collective-permute-done((f32[256,128]{1,0:T(8,128)S(1)}, f32[256,128]{1,0:T(8,128)S(1)}, u32[]{:S(2)}, u32[]{:S(2)}) %collective-permute-start.7) | collective-permute-done | bytes 131104 | tf_op jit(solution)/shard_map/ppermute | solution.py:22
  20.3 0.0 collective-permute-done.8.far_ref
  20.3 2.1 %last.1 = (bf16[2048,128]{1,0:T(8,128)(2,1)}, bf16[2048,128]{1,0:T(8,128)(2,1)}, bf16[2048,128]{1,0:T(8,128)(2,1)}, bf16[2048,128]{1,0:T(8,128)(2,1)}, f32[4,2048,128]{2,1,0:T(8,128)S(1)}) custom-call(f32[4,7]{1,0:T(4,128)S(1)} %get-tuple-element.34.table_ref, ...), custom_call_target="tpu_custom_call", output_to_operand_aliasing={{4}: (5, {})} | custom-call | tf_op jit(solution)/shard_map/last/pallas_call | solution.py:284
  (5 shorter events, 0.1 us)
Async XLA Ops:
  3.1 1.5 %collective-permute-start = (f32[2,160,128]{2,1,0:T(8,128)S(1)}, f32[2,160,128]{2,1,0:T(8,128)S(1)}, u32[]{:S(2)}, u32[]{:S(2)}) collective-permute-start(f32[2,160,128]{2,1,0:T(8,128)S(1)} %get-tuple-element.35), channel_id=1, source_target_pairs={{0,1},{1,0},{2,3},{3,2},{4,5},{5,4},{6,7},{7,6},{8,9},{9,8},{10,11... | collective-permute-start | bytes 491528 | tf_op jit(solution)/shard_map/ppermute | solution.py:22
  3.6 5.1 %collective-permute-start.1 = (f32[2,96,128]{2,1,0:T(8,128)S(1)}, f32[2,96,128]{2,1,0:T(8,128)S(1)}, u32[]{:S(2)}, u32[]{:S(2)}) collective-permute-start(f32[2,96,128]{2,1,0:T(8,128)S(1)} %get-tuple-element.42), channel_id=1, source_target_pairs={{0,1},{1,0},{2,3},{3,2},{4,5},{5,4},{6,7},{7,6},{8,9},{9,8},{10,11... | collective-permute-start | bytes 294920 | tf_op jit(solution)/shard_map/ppermute | solution.py:22
  4.6 8.5 %collective-permute-start.3 = (f32[160,128]{1,0:T(8,128)S(1)}, f32[160,128]{1,0:T(8,128)S(1)}, u32[]{:S(2)}, u32[]{:S(2)}) collective-permute-start(f32[160,128]{1,0:T(8,128)S(1)} %select_bitcast_fusion), channel_id=1, source_target_pairs={{0,8},{4,12},{8,0},{12,4},{1,9},{5,13},{9,1},{13,5},{2,10},{6,14},... | collective-permute-start | bytes 245768 | tf_op jit(solution)/shard_map/ppermute | solution.py:27
  8.7 8.9 %collective-permute-start.2 = (f32[256,128]{1,0:T(8,128)S(1)}, f32[256,128]{1,0:T(8,128)S(1)}, u32[]{:S(2)}, u32[]{:S(2)}) collective-permute-start(f32[256,128]{1,0:T(8,128)S(1)} %get-tuple-element.46), channel_id=1, source_target_pairs={{0,4},{4,0},{8,12},{12,8},{1,5},{5,1},{9,13},{13,9},{2,6},{6,2},{1... | collective-permute-start | bytes 393224 | tf_op jit(solution)/shard_map/ppermute | solution.py:27
  10.3 6.9 %collective-permute-start.6 = (f32[96,128]{1,0:T(8,128)S(1)}, f32[96,128]{1,0:T(8,128)S(1)}, u32[]{:S(2)}, u32[]{:S(2)}) collective-permute-start(f32[96,128]{1,0:T(8,128)S(1)} %bitcast.16), channel_id=1, source_target_pairs={{0,8},{4,12},{8,0},{12,4},{1,9},{5,13},{9,1},{13,5},{2,10},{6,14},... | collective-permute-start | bytes 147464 | tf_op jit(solution)/shard_map/ppermute | solution.py:27
  10.7 6.9 %collective-permute-start.5 = (f32[96,128]{1,0:T(8,128)S(1)}, f32[96,128]{1,0:T(8,128)S(1)}, u32[]{:S(2)}, u32[]{:S(2)}) collective-permute-start(f32[96,128]{1,0:T(8,128)S(1)} %bitcast.17), channel_id=1, source_target_pairs={{0,12},{4,8},{8,4},{12,0},{1,13},{5,9},{9,5},{13,1},{2,14},{6,10},... | collective-permute-start | bytes 147464 | tf_op jit(solution)/shard_map/ppermute | solution.py:27
  13.1 5.3 %collective-permute-start.4 = (f32[1,160,128]{2,1,0:T(8,128)S(1)}, f32[1,160,128]{2,1,0:T(8,128)S(1)}, u32[]{:S(2)}, u32[]{:S(2)}) collective-permute-start(f32[1,160,128]{2,1,0:T(8,128)S(1)} %bitcast.23), channel_id=1, source_target_pairs={{0,4},{4,0},{8,12},{12,8},{1,5},{5,1},{9,13},{13,9},{2,6},{6,2},{1... | collective-permute-start | bytes 245768 | tf_op jit(solution)/shard_map/ppermute | solution.py:27
  18.5 1.8 %collective-permute-start.8 = (f32[2,256,128]{2,1,0:T(8,128)S(1)}, f32[2,256,128]{2,1,0:T(8,128)S(1)}, u32[]{:S(2)}, u32[]{:S(2)}) collective-permute-start(f32[2,256,128]{2,1,0:T(8,128)S(1)} %maximum_maximum_fusion.far_ref), channel_id=1, source_target_pairs={{0,1},{1,0},{2,3},{3,2},{4,5},{5,4},{6,7},{7,6},{8,9},{9,8},{10,11... | collective-permute-start | bytes 786440 | tf_op jit(solution)/shard_map/ppermute | solution.py:22
  18.6 1.7 %collective-permute-start.7 = (f32[256,128]{1,0:T(8,128)S(1)}, f32[256,128]{1,0:T(8,128)S(1)}, u32[]{:S(2)}, u32[]{:S(2)}) collective-permute-start(f32[256,128]{1,0:T(8,128)S(1)} %get-tuple-element.55), channel_id=1, source_target_pairs={{0,1},{1,0},{2,3},{3,2},{4,5},{5,4},{6,7},{7,6},{8,9},{9,8},{10,11... | collective-permute-start | bytes 393224 | tf_op jit(solution)/shard_map/ppermute | solution.py:22
